TPU v7x, 32 devices: a whole 2x2x4 slice. The times are simulated.
32 devices in a mesh: groups: 2 (over x), tensor: 8 (over z, y), replica: 2 (over core).
Axes of the slice: x: 2, y: 2, z: 4, core: 2. Of those that a mesh axis runs over, the one named last changes fastest.
Arguments:
- tokens: bfloat16 [2048, 8192], P(('groups', 'replica'), 'tensor'), parts along dimension 0, may hold values from -6 to 6
- context: bfloat16 [2048, 8192], P(('groups', 'replica'), 'tensor'), parts along dimension 0, may hold values from -6 to 6
- query_weight: bfloat16 [8192, 8192], P(None, 'tensor'), may hold values from -0.0625 to 0.0625
- output_weight: bfloat16 [8192, 8192], P('tensor'), may hold values from -0.09375 to 0.09375
- store_aq: bfloat16 [64, 64, 8192], P(('groups', 'replica'), None, 'tensor'), parts along dimension 0, may hold values from -0.0625 to 0.0625
- store_bq: bfloat16 [64, 64, 8192], P(('groups', 'replica'), None, 'tensor'), parts along dimension 0, may hold values from -0.75 to 0.75
- store_ao: bfloat16 [64, 64, 8192], P(('groups', 'replica'), None, 'tensor'), parts along dimension 0, may hold values from -0.0625 to 0.0625
- store_bo: bfloat16 [64, 64, 8192], P(('groups', 'replica'), None, 'tensor'), parts along dimension 0, may hold values from -0.75 to 0.75
- adapter_of: int32 [8], P('groups'), parts along dimension 0, may hold values from 0 to 31
- location: int32 [64], P('groups'), parts along dimension 0, may hold values from 0 to 31, each once
- token_count: int32 [8], P('groups'), parts along dimension 0, may hold values from 1 to 256, 768 in all
Outputs:
- queries: bfloat16 [2048, 8192], P(('groups', 'replica'), 'tensor'), parts along dimension 0
- attended: bfloat16 [2048, 8192], P(('groups', 'replica'), 'tensor'), parts along dimension 0
There are 2 independent parts, one for each index of `groups`. A program takes and returns all parts, laid end to end along the dimension named above; an argument that names none is the same for every part. Nothing has to cross between parts.
Inputs may be any that keep to these rules, and one draw needn't show every extreme that they name: `location`: a permutation; store slots i * 16 to (i + 1) * 16 - 1 lie on index i of replica. `token_count`: one request reaches 256 in every draw; they sum to 768.
All inputs are finite; a program needn't handle non-finite values.
Results may differ from a plain program's by a relative error of at most 0.0029.
Values may be sent and summed in bfloat16 or wider, within the bound.
No kernel may reach another device: no remote copies, remote signals or barrier semaphores. Data moves between devices by JAX's collectives and lax.ppermute only.
A program may use at most 192 MiB of HBM per device.

v0:
```python
import jax
import jax.numpy as jnp
from jax import lax
from jax.sharding import PartitionSpec as P

REQUEST_LENGTH = 256


adapter_scale = 0.5


def local(
    tokens,
    context,
    query_weight,
    output_weight,
    store_aq,
    store_bq,
    store_ao,
    store_bo,
    adapter_of,
    location,
    token_count,
):
    rows, width = tokens.shape
    request_device_rows = rows // REQUEST_LENGTH
    replica = lax.axis_index("replica")
    mine_ids = lax.dynamic_slice_in_dim(
        adapter_of, replica * request_device_rows, request_device_rows
    )
    mine_counts = lax.dynamic_slice_in_dim(
        token_count, replica * request_device_rows, request_device_rows
    )
    everything = (
        lax.all_gather(store_aq, "replica", axis=0, tiled=True),
        lax.all_gather(store_bq, "replica", axis=0, tiled=True),
        lax.all_gather(store_ao, "replica", axis=0, tiled=True),
        lax.all_gather(store_bo, "replica", axis=0, tiled=True),
    )
    my_slots = jnp.take(location, mine_ids, axis=0)
    fetched = [jnp.take(table, my_slots, axis=0) for table in everything]
    down_aq, up_bq, down_ao, up_bo = fetched
    query_columns = query_weight.shape[1]
    output_token_rows = output_weight.shape[0]
    grouped_ctx = context.reshape(request_device_rows, REQUEST_LENGTH, width)
    part_o = jnp.einsum("rln,rkn->rlk", grouped_ctx, down_ao, preferred_element_type=jnp.float32)
    query_base_rows = jnp.dot(
        lax.all_gather(tokens, "tensor", axis=1, tiled=True),
        query_weight,
        preferred_element_type=jnp.float32,
    )
    grouped = tokens.reshape(request_device_rows, REQUEST_LENGTH, width)
    part_q = jnp.einsum("rln,rkn->rlk", grouped, down_aq, preferred_element_type=jnp.float32)
    low_q, low_o = lax.psum((part_q, part_o), "tensor")
    output_base_rows = lax.psum_scatter(
        lax.dot_general(
            output_weight, context, (((0,), (1,)), ((), ())), preferred_element_type=jnp.float32
        ),
        "tensor",
        scatter_dimension=0,
        tiled=True,
    ).T
    query_adapter_delta = jnp.einsum(
        "rlk,rke->rle", low_q.astype(jnp.bfloat16), up_bq, preferred_element_type=jnp.float32
    )
    output_adapter_delta = jnp.einsum(
        "rlk,rke->rle", low_o.astype(jnp.bfloat16), up_bo, preferred_element_type=jnp.float32
    )
    active_rows = (
        jnp.arange(REQUEST_LENGTH, dtype=jnp.int32)[None, :, None] < mine_counts[:, None, None]
    )
    queries = jnp.where(
        active_rows,
        query_base_rows.reshape(request_device_rows, REQUEST_LENGTH, query_columns)
        + adapter_scale * query_adapter_delta,
        jnp.float32(0.0),
    )
    attended = jnp.where(
        active_rows,
        output_base_rows.reshape(request_device_rows, REQUEST_LENGTH, output_token_rows)
        + adapter_scale * output_adapter_delta,
        jnp.float32(0.0),
    )
    return (
        queries.astype(jnp.bfloat16).reshape(rows, query_columns),
        attended.astype(jnp.bfloat16).reshape(rows, output_token_rows),
    )


def solution(mesh):
    return jax.shard_map(
        local,
        mesh=mesh,
        in_specs=(
            P(("groups", "replica"), "tensor"),
            P(("groups", "replica"), "tensor"),
            P(None, "tensor"),
            P("tensor", None),
            P(("groups", "replica"), None, "tensor"),
            P(("groups", "replica"), None, "tensor"),
            P(("groups", "replica"), None, "tensor"),
            P(("groups", "replica"), None, "tensor"),
            P("groups"),
            P("groups"),
            P("groups"),
        ),
        out_specs=(P(("groups", "replica"), "tensor"), P(("groups", "replica"), "tensor")),
        check_vma=False,
    )
```

profile of v0, /device:TPU:0, one launch (start us, length us, event | category | flops | bytes accessed | tf_op | source)
XLA Modules:
  0.0 501.9 jit_solution(11778315575338047501)
XLA Ops:
  7.2 0.7 all-gather.12.cloned.1.call-update
  8.0 0.7 all-gather.8.cloned.1.call-update
  8.7 0.7 all-gather.14.cloned.1.call-update
  9.4 0.5 all-gather.10.cloned.1.call-update
  10.0 0.5 all-gather.6.cloned.1.call-update
  10.6 15.8 %fusion.19 = f32[8192,512]{1,0:T(8,128)} fusion(bf16[1024,8192]{1,0:T(8,128)(2,1)} %param.16, bf16[512,1024]{1,0:T(8,128)(2,1)S(1)} %copy-done), kind=kOutput, calls=%fused_computation.35 | convolution fusion | flops 8589934592 | bytes 34603008 | tf_op jit(solution)/shard_map/dot_general | solution.py:56
  26.5 0.6 copy-done.5
  27.3 0.6 gather_fusion
  28.1 2.8 gather_fusion.3
  30.8 0.4 convolution_bitcast_fusion
  31.3 11.1 %all-gather.8.cloned.1.call-done = bf16[32,64,1024]{2,1,0:T(8,128)(2,1)} async-done(((bf16[16,64,1024]{2,1,0:T(8,128)(2,1)}), bf16[32,64,1024]{2,1,0:T(8,128)(2,1)}) %all-gather.8.cloned.1.call-update) | async-done | bytes 4194320 | tf_op jit(solution)/shard_map/all_gather | solution.py:35
  42.4 2.7 gather_fusion.1
  45.1 0.4 convolution_bitcast_fusion.1
  45.6 13.2 %all-gather.14.cloned.1.call-done = bf16[32,64,1024]{2,1,0:T(8,128)(2,1)} async-done(((bf16[16,64,1024]{2,1,0:T(8,128)(2,1)}), bf16[32,64,1024]{2,1,0:T(8,128)(2,1)}) %all-gather.14.cloned.1.call-update) | async-done | bytes 4194320 | tf_op jit(solution)/shard_map/all_gather | solution.py:38
  58.8 2.7 gather_fusion.4
  61.6 13.5 %all-gather.10.cloned.1.call-done = bf16[32,64,1024]{2,1,0:T(8,128)(2,1)} async-done(((bf16[16,64,1024]{2,1,0:T(8,128)(2,1)}), bf16[32,64,1024]{2,1,0:T(8,128)(2,1)}) %all-gather.10.cloned.1.call-update) | async-done | bytes 4194320 | tf_op jit(solution)/shard_map/all_gather | solution.py:36
  75.1 2.7 gather_fusion.2
  77.8 44.7 %all-reduce.2 = (bf16[2,256,64]{1,2,0:T(8,128)(2,1)S(1)}, bf16[2,256,64]{1,2,0:T(8,128)(2,1)S(1)}) all-reduce(f32[2,256,64]{1,2,0:T(8,128)S(1)} %convolution_bitcast_fusion.1, f32[2,256,64]{1,2,0:T(8,128)S(1)} %convolution_bitcast_fusion), channel_id=1, replica_groups=mesh['groups'=2,'tensor'=8,'replica'=2] {'tensor'}, use_global_device_ids=true, to_apply=%region_0.0 | all-reduce | flops 65536 | bytes 393216 | tf_op jit(solution)/shard_map/psum | solution.py:54
  122.5 84.5 %all-gather.6.cloned.1.call-done = bf16[512,8192]{1,0:T(8,128)(2,1)} async-done(((bf16[512,1024]{1,0:T(8,128)(2,1)}), bf16[512,8192]{1,0:T(8,128)(2,1)}) %all-gather.6.cloned.1.call-update) | async-done | bytes 8388624 | tf_op jit(solution)/shard_map/all_gather | solution.py:48
  207.0 14.4 %fusion.18 = f32[512,1024]{1,0:T(8,128)S(1)} fusion(bf16[512,8192]{1,0:T(8,128)(2,1)} %all-gather.6.cloned.1.call-done, bf16[8192,1024]{1,0:T(8,128)(2,1)} %param.15), kind=kOutput, calls=%fused_computation.34 | convolution fusion | flops 8589934592 | bytes 27262976 | tf_op jit(solution)/shard_map/dot_general | solution.py:47
  221.4 1.5 select_convert_fusion.1
  222.9 268.7 %reduce-scatter.2.cloned.1.call-done = f32[1024,512]{1,0:T(8,128)} async-done(((f32[8192,512]{1,0:T(8,128)}), f32[1024,512]{1,0:T(8,128)}) %reduce-scatter.2.cloned.1.call-update) | async-done | bytes 2097168 | tf_op jit(solution)/shard_map/reduce_scatter | solution.py:55
  491.6 1.9 copy.15
  493.6 1.5 select_convert_fusion
  (25 shorter events, 0.6 us)
Async XLA Ops:
  7.2 3.4 copy-start
  7.2 20.9 %all-gather.12.cloned.1.call-start = ((), (), s32[]{:S(2)}) async-start(), calls=%async_computation.5 | async-start | bytes 6291456 | tf_op jit(solution)/shard_map/all_gather | solution.py:37
  7.9 34.5 %all-gather.8.cloned.1.call-start = ((), (), s32[]{:S(2)}) async-start(), calls=%async_computation.2 | async-start | bytes 6291456 | tf_op jit(solution)/shard_map/all_gather | solution.py:35
  8.7 50.1 %all-gather.14.cloned.1.call-start = ((), (), s32[]{:S(2)}) async-start(), calls=%async_computation.6 | async-start | bytes 6291456 | tf_op jit(solution)/shard_map/all_gather | solution.py:38
  9.4 65.7 %all-gather.10.cloned.1.call-start = ((), (), s32[]{:S(2)}) async-start(), calls=%async_computation.3 | async-start | bytes 6291456 | tf_op jit(solution)/shard_map/all_gather | solution.py:36
  10.0 197.1 %all-gather.6.cloned.1.call-start = ((), (), s32[]{:S(2)}) async-start(), calls=%async_computation.1 | async-start | bytes 9437184 | tf_op jit(solution)/shard_map/all_gather | solution.py:48
  10.6 481.1 %reduce-scatter.2.cloned.1.call-start = ((), (), s32[]{:S(2)}) async-start(), calls=%async_computation.4 | async-start | bytes 18874368 | tf_op jit(solution)/shard_map/reduce_scatter | solution.py:55
  26.4 0.7 copy-start.5
  26.5 0.7 copy-start.4
  26.5 0.8 copy-start.2
  26.5 18.7 %copy-start.3 = (bf16[512,1024]{1,0:T(8,128)(2,1)S(1)}, bf16[512,1024]{1,0:T(8,128)(2,1)}, u32[]{:S(2)}) copy-start(bf16[512,1024]{1,0:T(8,128)(2,1)} %param.13) | copy-start | bytes 3145732
  221.4 273.6 %copy-start.1 = (bf16[512,1024]{1,0:T(8,128)(2,1)S(1)}, bf16[512,1024]{1,0:T(8,128)(2,1)}, u32[]{:S(2)}) copy-start(bf16[512,1024]{1,0:T(8,128)(2,1)} %param.14) | copy-start | bytes 3145732
Sparse Core Ops, SparseCore 0:
  9.6 16.3 all-gather.11
  27.5 14.8 all-gather.7
  43.9 14.8 all-gather.13
  60.2 14.8 all-gather.9
  77.1 129.8 all-gather.5
  210.7 280.9 reduce-scatter.1
where the time goes:
time: 502 us
  waiting for transfers between devices  394 us (78%)
  blocking collectives  44.7 us (9%)
  matrix products  34 us (7%)
  local copies, waits for them, and re-layouts  14.3 us (3%)
  between operations  14.2 us (3%)
    reduce_scatter x1, waiting for transfers between devices, local(): lax.psum_scatter(lax.dot_general(output_weight, context, (((0,), (1,)), (...  269 us
    all_gather x1, waiting for transfers between devices, local(): lax.all_gather(tokens, 'tensor', axis=1, tiled=True)  84.5 us
    psum x1, blocking collectives, local(): low_q, low_o = lax.psum((part_q, part_o), 'tensor')  44.7 us
    dot_general x1, matrix products, local(): lax.dot_general(output_weight, context, (((0,), (1,)), ((), ())), preferr...  15.8 us
    dot_general x1, matrix products, local(): jnp.dot(lax.all_gather(tokens, 'tensor', axis=1, tiled=True), query_weigh...  14.4 us
    all_gather x1, waiting for transfers between devices, local(): lax.all_gather(store_bq, 'replica', axis=0, tiled=True)  13.5 us
    all_gather x1, waiting for transfers between devices, local(): lax.all_gather(store_bo, 'replica', axis=0, tiled=True)  13.2 us
    all_gather x1, waiting for transfers between devices, local(): lax.all_gather(store_aq, 'replica', axis=0, tiled=True)  11.1 us
  transfers between devices with their start and end apart: 6, of which 5 were waited for; matrix products, arithmetic and copies ran while one was open for 9% of the time, Pallas kernels for 0%

commit v1 on v0

v1 whole, which is shorter than its diff:
```python
import jax
import jax.numpy as jnp
from jax import lax
from jax.sharding import PartitionSpec as P

REQUEST_LENGTH = 256
SPLIT = 256

adapter_scale = 0.5

SUM_SCALE = 8.0
DOWN_SCALE = 16.0

BF16 = jnp.bfloat16
F16 = jnp.float16
F32 = jnp.float32


def z_pairs(*pairs):
    return [(2 * a + y, 2 * b + y) for a, b in pairs for y in range(2)]


INNER = z_pairs((1, 2), (2, 1))
OUTWARD = z_pairs((2, 3), (1, 0))
INWARD = z_pairs((0, 1), (3, 2))
SIDES = z_pairs((0, 1), (1, 0), (2, 3), (3, 2))
Y_SWAP = [(t, t ^ 1) for t in range(8)]
FAR = z_pairs((0, 2), (2, 0), (1, 3), (3, 1))


def send(value, pairs):
    return lax.ppermute(value, "tensor", pairs)


def other_replica(value):
    return lax.ppermute(value, "replica", [(0, 1), (1, 0)])


def dot(a, b):
    return jnp.dot(a, b, preferred_element_type=F32)


def pick(z, table):
    return jnp.asarray(table, jnp.int32)[z]


def by_z(z, table):
    out = jnp.int32(table[0])
    for i in range(1, 4):
        out = jnp.where(z == i, jnp.int32(table[i]), out)
    return out


def plan(token_count, replica, rows, packed):
    per = rows // REQUEST_LENGTH
    mine = lax.dynamic_slice_in_dim(token_count, replica * per, per)
    theirs = lax.dynamic_slice_in_dim(token_count, (1 - replica) * per, per)
    n_mine, n_theirs = jnp.sum(mine), jnp.sum(theirs)
    spare = rows - packed
    first = packed - spare
    length = jnp.arange(rows, dtype=jnp.int32) % REQUEST_LENGTH
    request = jnp.arange(rows, dtype=jnp.int32) // REQUEST_LENGTH
    start = jnp.cumsum(mine) - mine
    start_of = jnp.zeros((rows,), jnp.int32)
    count_of = jnp.zeros((rows,), jnp.int32)
    for i in range(per):
        start_of = jnp.where(request == i, start[i], start_of)
        count_of = jnp.where(request == i, mine[i], count_of)
    position = jnp.where(length < count_of, start_of + length, -1)
    here = jnp.where(position < packed, position, -1)
    there = jnp.where(position >= packed, position - packed + n_theirs - first, -1)
    pack_here = (jnp.arange(packed, dtype=jnp.int32)[:, None] == here[None, :]).astype(BF16)
    pack_there = (jnp.arange(spare, dtype=jnp.int32)[:, None] == there[None, :]).astype(BF16)
    unpack = jnp.concatenate([pack_here, pack_there], axis=0).T
    slot = jnp.arange(packed, dtype=jnp.int32)
    own = slot < n_mine
    seat = jnp.where(own, slot, packed + slot - n_mine)
    bounds_mine, bounds_theirs = jnp.cumsum(mine), jnp.cumsum(theirs)
    index = jnp.zeros((packed,), jnp.int32)
    for i in range(per - 1):
        index = index + (seat >= jnp.where(own, bounds_mine[i], bounds_theirs[i])).astype(jnp.int32)
    request_of = jnp.where(own, replica, 1 - replica) * per + index
    return pack_here, pack_there, unpack, request_of


def fetch(stores, slots, replica):
    held = stores[0].shape[0]
    picked = []
    for table in stores:
        for i in range(slots.shape[0]):
            local = slots[i] - replica * held
            mine = (local >= 0) & (local < held)
            block = lax.dynamic_index_in_dim(table, jnp.clip(local, 0, held - 1), 0, keepdims=False)
            picked.append(jnp.where(mine, block, jnp.zeros_like(block)))
    blocks = jnp.stack(picked)
    blocks = blocks + other_replica(blocks)
    rank, width = blocks.shape[1:]
    return blocks.reshape(len(stores), slots.shape[0] * rank, width)


def fits(mesh):
    return mesh.shape["tensor"] == 8


def gather_z(x, z):
    edge = (z == 0) | (z == 3)
    near_in, near_out = send(x, INNER), send(x, OUTWARD)
    one = jnp.where(edge, near_out, near_in)
    two = send(jnp.where(edge, x, one), SIDES)
    mid = send(two, INNER)
    out = send(mid, OUTWARD)
    three = jnp.where(edge, out, mid)
    return [x, one, two, three]


ONE = (1, 2, 1, 2)
TWO = (2, 0, 3, 1)
THREE = (3, 3, 0, 0)


def narrow(value):
    return (value * SUM_SCALE).astype(F16)


def widen(value):
    return value.astype(F32) * (1.0 / SUM_SCALE)


def scatter_z(part, z):
    edge = (z == 0) | (z == 3)
    p_far = part(0)
    r1 = send(narrow(p_far), INWARD)
    r2 = send(narrow(p_far + widen(r1)), INNER)
    r3 = send(narrow(part(1) + widen(r2)), SIDES)
    p_near = part(2)
    r4a = send(narrow(p_near), INWARD)
    r4b = send(narrow(p_near + widen(r3)), INNER)
    return part(3) + jnp.where(edge, widen(r3), widen(r4a) + widen(r4b))


def exchange(
    tokens, context, query_weight, output_weight, sum_down, z, y
):
    packed, width = tokens.shape
    a_tok, b_tok = tokens[:SPLIT], tokens[SPLIT:]
    a_ctx, b_ctx = context[:SPLIT], context[SPLIT:]
    owners = (THREE, TWO, ONE, (0, 1, 2, 3))
    shards = ((0, 1, 2, 3), ONE, TWO, THREE)

    def out_block(first, count):
        return lax.dynamic_slice_in_dim(output_weight, first * width, count * width, axis=1)

    def in_block(first, count):
        return lax.dynamic_slice_in_dim(query_weight, first * width, count * width, axis=0)

    b_pair = send(b_tok, Y_SWAP)
    a_from_y = [
        send(narrow(dot(a_ctx, out_block(2 * by_z(z, o) + 1 - y, 1))), Y_SWAP) for o in owners
    ]
    a_line = gather_z(a_tok, z)
    b_sum = scatter_z(lambda i: dot(b_ctx, out_block(2 * by_z(z, owners[i]), 2)), z)
    a_sum = scatter_z(
        lambda i: dot(a_ctx, out_block(2 * by_z(z, owners[i]) + y, 1)) + widen(a_from_y[i]), z
    )
    b_both = jnp.concatenate(
        [jnp.where(y == 0, b_tok, b_pair), jnp.where(y == 0, b_pair, b_tok)], axis=1
    )
    b_line = gather_z(b_both, z)
    a_cross = [send(v, Y_SWAP) for v in a_line]
    b_mine = lax.dynamic_slice_in_dim(b_sum, y * width, width, axis=1)
    b_theirs = lax.dynamic_slice_in_dim(b_sum, (1 - y) * width, width, axis=1)
    b_sum = b_mine + widen(send(narrow(b_theirs), Y_SWAP))

    a_q = jnp.zeros((SPLIT, query_weight.shape[1]), F32)
    b_q = jnp.zeros((packed - SPLIT, query_weight.shape[1]), F32)
    for i in range(4):
        at = by_z(z, shards[i])
        a_q = a_q + dot(a_line[i], in_block(2 * at + y, 1)) + dot(a_cross[i], in_block(2 * at + 1 - y, 1))
        b_q = b_q + dot(b_line[i], in_block(2 * at, 2))
    return jnp.concatenate([a_q, b_q]), jnp.concatenate([a_sum, b_sum])


def sum_over_tensor(part):
    total = part
    for pairs in (Y_SWAP, SIDES, FAR):
        moved = send((total * DOWN_SCALE).astype(F16), pairs)
        total = (total * DOWN_SCALE).astype(F16).astype(F32) * (1.0 / DOWN_SCALE)
        total = total + moved.astype(F32) * (1.0 / DOWN_SCALE)
    return total


def make(mesh):
    grid = fits(mesh)

    def local(
        tokens, context, query_weight, output_weight,
        store_aq, store_bq, store_ao, store_bo,
        adapter_of, location, token_count,
    ):
        rows, width = tokens.shape
        rank = store_aq.shape[1]
        packed = rows * 3 // 4
        spare = rows - packed
        first = packed - spare
        replica = lax.axis_index("replica")
        at = lax.axis_index("tensor")
        z, y = at // 2, at % 2
        pack_here, pack_there, unpack, request_of = plan(token_count, replica, rows, packed)
        slots = jnp.take(location, adapter_of, axis=0)

        pack = jnp.concatenate([pack_here, pack_there])
        both = dot(pack, jnp.concatenate([tokens, context], axis=1)).astype(BF16)
        moved = other_replica(both[packed:])
        both = jnp.concatenate([both[:first], both[first:packed] + moved])
        tok, ctx = both[:, :width], both[:, width:]

        down_aq, up_bq, down_ao, up_bo = fetch((store_aq, store_bq, store_ao, store_bo), slots, replica)
        chosen = (
            request_of[:, None] == jnp.arange(slots.shape[0] * rank, dtype=jnp.int32)[None, :] // rank
        )

        def fold(wide):
            return jnp.where(chosen, wide, 0.0).reshape(packed, slots.shape[0], rank).sum(1)

        part_q = fold(lax.dot_general(tok, down_aq, (((1,), (1,)), ((), ())), preferred_element_type=F32))
        part_o = fold(lax.dot_general(ctx, down_ao, (((1,), (1,)), ((), ())), preferred_element_type=F32))
        parts = jnp.concatenate([part_q, part_o], axis=1)

        if grid:
            low = sum_over_tensor(parts)
            base_q, base_o = exchange(tok, ctx, query_weight, output_weight, low, z, y)
        else:
            low = lax.psum(parts, "tensor")
            base_q = dot(lax.all_gather(tok, "tensor", axis=1, tiled=True), query_weight)
            base_o = lax.psum_scatter(dot(ctx, output_weight), "tensor", scatter_dimension=1, tiled=True)
        low = low.astype(BF16)

        def up(narrow_rows, blocks):
            spread = jnp.where(chosen, jnp.tile(narrow_rows, (1, slots.shape[0])), jnp.zeros((), BF16))
            return dot(spread, blocks)

        queries = (base_q + adapter_scale * up(low[:, :rank], up_bq)).astype(BF16)
        attended = (base_o + adapter_scale * up(low[:, rank:], up_bo)).astype(BF16)
        result = jnp.concatenate([queries, attended], axis=1)
        back = other_replica(result[first:])
        out = dot(unpack, jnp.concatenate([result, back])).astype(BF16)
        return out[:, :width], out[:, width:]

    return local


def solution(mesh):
    return jax.shard_map(
        make(mesh),
        mesh=mesh,
        in_specs=(
            P(("groups", "replica"), "tensor"),
            P(("groups", "replica"), "tensor"),
            P(None, "tensor"),
            P("tensor", None),
            P(("groups", "replica"), None, "tensor"),
            P(("groups", "replica"), None, "tensor"),
            P(("groups", "replica"), None, "tensor"),
            P(("groups", "replica"), None, "tensor"),
            P("groups"),
            P("groups"),
            P("groups"),
        ),
        out_specs=(P(("groups", "replica"), "tensor"), P(("groups", "replica"), "tensor")),
        check_vma=False,
    )
```

time: 502 us -> 288 us (0.57)
  waiting for transfers between devices: 394 us -> 99.9 us
  starting transfers between devices: 0.23 us -> 61 us
  blocking collectives: 44.7 us -> 0 us
  other arithmetic: 0.25 us -> 44 us
  matrix products: 34 us -> 67.4 us
  between operations: 14.2 us -> 4.16 us
    reduce_scatter x1 -> x0, waiting for transfers between devices: 269 us -> none  [local(): lax.psum_scatter(lax.dot_general(output_weight, context, (((0,), (1,)), (...]
    all_gather x5 -> x0, waiting for transfers between devices: 122 us -> none  [the longest x1 84.5 us: local(): lax.all_gather(tokens, 'tensor', axis=1, tiled=True)]
    ppermute x0 -> x36, waiting for transfers between devices: none -> 99.9 us  [the longest x33 98 us: send(): return lax.ppermute(value, 'tensor', pairs)]
    ppermute x0 -> x36, starting transfers between devices: none -> 61 us  [the longest x33 60.4 us: send(): return lax.ppermute(value, 'tensor', pairs)]
    psum x1 -> x0, blocking collectives: 44.7 us -> none  [local(): low_q, low_o = lax.psum((part_q, part_o), 'tensor')]
    dot_general x6 -> x30, matrix products: 34 us -> 67.4 us  [the longest x28 63.7 us: dot(): return jnp.dot(a, b, preferred_element_type=F32)]
    unnamed x0 -> x16, other arithmetic: none -> 23.8 us
    gather x5 -> x1, local copies, waits for them, and re-layouts: 11.6 us -> 0.64 us  [local(): slots = jnp.take(location, adapter_of, axis=0)]
  transfers between devices with their start and end apart: 6 -> 36, of which waited for: 5 -> 13; matrix products, arithmetic and copies ran while one was open for 9% -> 36% of each run, Pallas kernels for 0% -> 0%
where the time goes in v1:
time: 288 us; the launch traced here: 286 us
  waiting for transfers between devices  99.9 us (35%)
  matrix products  67.4 us (23%)
  starting transfers between devices  61 us (21%)
  other arithmetic  44 us (15%)
  local copies, waits for them, and re-layouts  9.72 us (3%)
  between operations  4.16 us (1%)
    ppermute x33, waiting for transfers between devices, send(): return lax.ppermute(value, 'tensor', pairs)  98 us
    dot_general x28, matrix products, dot(): return jnp.dot(a, b, preferred_element_type=F32)  63.7 us
    ppermute x33, starting transfers between devices, send(): return lax.ppermute(value, 'tensor', pairs)  60.4 us
    unnamed x16, other arithmetic  23.8 us
  transfers between devices with their start and end apart: 36, of which 13 were waited for; matrix products, arithmetic and copies ran while one was open for 36% of the time, Pallas kernels for 0%

profile of v1, /device:TPU:0, one launch (start us, length us, event | category | flops | bytes accessed | tf_op | source)
XLA Modules:
  0.0 286.0 jit_solution(1829077674951426891)
XLA Ops:
  3.5 3.3 %compare_select_fusion.4 = (s32[512]{0:T(512)S(1)}, s32[512]{0:T(512)S(1)}) fusion(s32[]{:T(128)} %bitcast.5, s32[]{:T(128)} %bitcast.4, s32[]{:T(128)} %bitcast.1, s32[]{:T(128)} %bitcast, s32[]{:T(128)} %get-tuple-element.19), kind=kLoop, calls=%fused_computation.194 | loop fusion | flops 14336 | bytes 4116 | tf_op jit(solution)/shard_map/jit(_where)/select_n | solution.py:70
  47.3 3.3 %fusion.66 = f32[256,1024]{1,0:T(8,128)} fusion(bf16[8192,1024]{1,0:T(8,128)(2,1)} %param.13, s32[]{:T(128)S(6)} %select_n.488, bf16[512,2048]{1,0:T(8,128)(2,1)S(1)} %convolution_convert_fusion.1), kind=kOutput, calls=%fused_computation.61 | convolution fusion | flops 536870912 | bytes 3670020 | tf_op jit(solution)/shard_map/dot_general | solution.py:40
  50.6 3.3 %fusion.50 = f32[256,1024]{1,0:T(8,128)} fusion(bf16[1024,8192]{1,0:T(8,128)(2,1)} %param.14, s32[]{:T(128)S(6)} %select_n.488, bf16[512,2048]{1,0:T(8,128)(2,1)S(1)} %convolution_convert_fusion.1), kind=kOutput, calls=%fused_computation.45 | convolution fusion | flops 536870912 | bytes 3670020 | tf_op jit(solution)/shard_map/dot_general | solution.py:40
  67.6 3.3 %fusion.112 = f16[256,1024]{1,0:T(8,128)(2,1)} fusion(bf16[1024,8192]{1,0:T(8,128)(2,1)} %param.14, s32[]{:T(128)S(6)} %select_n.489, bf16[512,2048]{1,0:T(8,128)(2,1)S(1)} %convolution_convert_fusion.1), kind=kOutput, calls=%fused_computation.85 | convolution fusion | flops 537395200 | bytes 3145732 | tf_op jit(solution)/shard_map/dot_general | solution.py:40
  79.4 6.4 %collective-permute-done.22 = f16[256,1024]{1,0:T(8,128)(2,1)S(1)} collective-permute-done((f16[256,1024]{1,0:T(8,128)(2,1)S(1)}, f16[256,1024]{1,0:T(8,128)(2,1)S(1)}, u32[]{:S(2)}, u32[]{:S(2)}) %collective-permute-start.22) | collective-permute-done | bytes 524320 | tf_op jit(solution)/shard_map/ppermute | solution.py:32
  90.7 22.2 %collective-permute-done.10 = bf16[128,1024]{1,0:T(8,128)(2,1)S(1)} collective-permute-done((bf16[128,1024]{1,0:T(8,128)(2,1)S(1)}, bf16[128,1024]{1,0:T(8,128)(2,1)S(1)}, u32[]{:S(2)}, u32[]{:S(2)}) %collective-permute-start.10) | collective-permute-done | bytes 262176 | tf_op jit(solution)/shard_map/ppermute | solution.py:32
  112.9 6.6 %collective-permute-start.4 = (bf16[256,1024]{1,0:T(8,128)(2,1)S(1)}, bf16[256,1024]{1,0:T(8,128)(2,1)S(1)}, u32[]{:S(2)}, u32[]{:S(2)}) collective-permute-start(bf16[256,1024]{1,0:T(8,128)(2,1)S(1)} %get-tuple-element.2), channel_id=1, source_target_pairs={{0,4},{2,6},{4,0},{6,2},{8,12},{10,14},{12,8},{14,10},{1,5},{3,7},... | collective-permute-start | bytes 1572872 | tf_op jit(solution)/shard_map/ppermute | solution.py:32
  123.9 8.0 %collective-permute-done.4 = bf16[256,1024]{1,0:T(8,128)(2,1)S(1)} collective-permute-done((bf16[256,1024]{1,0:T(8,128)(2,1)S(1)}, bf16[256,1024]{1,0:T(8,128)(2,1)S(1)}, u32[]{:S(2)}, u32[]{:S(2)}) %collective-permute-start.4) | collective-permute-done | bytes 524320 | tf_op jit(solution)/shard_map/ppermute | solution.py:32
  131.9 4.4 %collective-permute-start.29 = (f16[128,2048]{1,0:T(8,128)(2,1)S(1)}, f16[128,2048]{1,0:T(8,128)(2,1)S(1)}, u32[]{:S(2)}, u32[]{:S(2)}) collective-permute-start(f16[128,2048]{1,0:T(8,128)(2,1)S(1)} %get-tuple-element.30), channel_id=1, source_target_pairs={{0,4},{2,6},{12,8},{14,10},{1,5},{3,7},{13,9},{15,11},{16,20},{18,... | collective-permute-start | bytes 1572872 | tf_op jit(solution)/shard_map/ppermute | solution.py:32
  139.2 3.9 %collective-permute-done.23 = f16[256,1024]{1,0:T(8,128)(2,1)S(1)} collective-permute-done((f16[256,1024]{1,0:T(8,128)(2,1)S(1)}, f16[256,1024]{1,0:T(8,128)(2,1)S(1)}, u32[]{:S(2)}, u32[]{:S(2)}) %collective-permute-start.23) | collective-permute-done | bytes 524320 | tf_op jit(solution)/shard_map/ppermute | solution.py:32
  144.3 8.2 %collective-permute-done.29 = f16[128,2048]{1,0:T(8,128)(2,1)S(1)} collective-permute-done((f16[128,2048]{1,0:T(8,128)(2,1)S(1)}, f16[128,2048]{1,0:T(8,128)(2,1)S(1)}, u32[]{:S(2)}, u32[]{:S(2)}) %collective-permute-start.29) | collective-permute-done | bytes 524320 | tf_op jit(solution)/shard_map/ppermute | solution.py:32
  156.6 19.5 %collective-permute-done.5 = bf16[256,1024]{1,0:T(8,128)(2,1)S(1)} collective-permute-done((bf16[256,1024]{1,0:T(8,128)(2,1)S(1)}, bf16[256,1024]{1,0:T(8,128)(2,1)S(1)}, u32[]{:S(2)}, u32[]{:S(2)}) %collective-permute-start.5) | collective-permute-done | bytes 524320 | tf_op jit(solution)/shard_map/ppermute | solution.py:32
  178.9 3.8 %collective-permute-start.13 = (bf16[128,2048]{1,0:T(8,128)(2,1)S(1)}, bf16[128,2048]{1,0:T(8,128)(2,1)S(1)}, u32[]{:S(2)}, u32[]{:S(2)}) collective-permute-start(bf16[128,2048]{1,0:T(8,128)(2,1)S(1)} %broadcast_select_fusion), channel_id=1, source_target_pairs={{0,4},{2,6},{4,0},{6,2},{8,12},{10,14},{12,8},{14,10},{1,5},{3,7},... | collective-permute-start | bytes 1572872 | tf_op jit(solution)/shard_map/ppermute | solution.py:32
  185.2 3.9 %fusion.25 = f16[128,2048]{1,0:T(8,128)(2,1)} fusion(bf16[1024,8192]{1,0:T(8,128)(2,1)} %param.14, s32[]{:T(128)S(6)} %select_n.516, f16[128,2048]{1,0:T(8,128)(2,1)S(1)} %collective-permute-done.30, bf16[128,2048]{1,0:T(8,128)(2,1)S(1)} %slice_add_fusion), kind=kOutput, calls=%fused_computation.22 | convolution fusion | flops 538181632 | bytes 5505028 | tf_op jit(solution)/shard_map/dot_general | solution.py:40
  191.7 6.0 %collective-permute-start.25 = (f16[256,1024]{1,0:T(8,128)(2,1)}, f16[256,1024]{1,0:T(8,128)(2,1)}, u32[]{:S(2)}, u32[]{:S(2)}) collective-permute-start(f16[256,1024]{1,0:T(8,128)(2,1)} %multiply_convert_fusion.6), channel_id=1, source_target_pairs={{0,4},{2,6},{4,0},{6,2},{8,12},{10,14},{12,8},{14,10},{1,5},{3,7},... | collective-permute-start | bytes 1572872 | tf_op jit(solution)/shard_map/ppermute | solution.py:32
  199.2 4.7 %collective-permute-start.31 = (f16[128,2048]{1,0:T(8,128)(2,1)}, f16[128,2048]{1,0:T(8,128)(2,1)}, u32[]{:S(2)}, u32[]{:S(2)}) collective-permute-start(f16[128,2048]{1,0:T(8,128)(2,1)} %fusion.25), channel_id=1, source_target_pairs={{0,4},{2,6},{4,0},{6,2},{8,12},{10,14},{12,8},{14,10},{1,5},{3,7},... | collective-permute-start | bytes 1572872 | tf_op jit(solution)/shard_map/ppermute | solution.py:32
  205.2 3.3 %add.337 = bf16[16,64,1024]{2,1,0:T(8,128)(2,1)S(1)} add(bf16[16,64,1024]{2,1,0:T(8,128)(2,1)} %select_dynamic-update-slice_fusion, bf16[16,64,1024]{2,1,0:T(8,128)(2,1)} %collective-permute-done.16) | non-fusion elementwise | flops 1048576 | bytes 6291456 | tf_op jit(solution)/shard_map/add | solution.py:96
  216.3 5.8 %collective-permute-done.31 = f16[128,2048]{1,0:T(8,128)(2,1)} collective-permute-done((f16[128,2048]{1,0:T(8,128)(2,1)}, f16[128,2048]{1,0:T(8,128)(2,1)}, u32[]{:S(2)}, u32[]{:S(2)}) %collective-permute-start.31) | collective-permute-done | bytes 524320 | tf_op jit(solution)/shard_map/ppermute | solution.py:32
  222.4 3.3 %multiply_convert_fusion.1 = (f16[128,2048]{1,0:T(8,128)(2,1)S(1)}, f16[128,2048]{1,0:T(8,128)(2,1)S(1)}) fusion(f16[128,2048]{1,0:T(8,128)(2,1)} %collective-permute-done.31, bf16[1024,8192]{1,0:T(8,128)(2,1)} %param.14, s32[]{:T(128)S(6)} %select_n.514, bf16[128,2048]{1,0:T(8,128)(2,1)S(1)} %slice_add_fusion), kind=kOutput, calls=%fused_computation.92 | convolution fusion | flops 538705920 | bytes 6029316 | tf_op jit(solution)/shard_map/dot_general | solution.py:40
  227.4 4.4 %collective-permute-start.32 = (f16[128,2048]{1,0:T(8,128)(2,1)S(1)}, f16[128,2048]{1,0:T(8,128)(2,1)S(1)}, u32[]{:S(2)}, u32[]{:S(2)}) collective-permute-start(f16[128,2048]{1,0:T(8,128)(2,1)S(1)} %get-tuple-element.12), channel_id=1, source_target_pairs={{0,4},{2,6},{12,8},{14,10},{1,5},{3,7},{13,9},{15,11},{16,20},{18,... | collective-permute-start | bytes 1572872 | tf_op jit(solution)/shard_map/ppermute | solution.py:32
  234.7 5.9 %collective-permute-done.18 = f16[384,128]{0,1:T(8,128)(2,1)S(1)} collective-permute-done((f16[384,128]{0,1:T(8,128)(2,1)S(1)}, f16[384,128]{0,1:T(8,128)(2,1)S(1)}, u32[]{:S(2)}, u32[]{:S(2)}) %collective-permute-start.18) | collective-permute-done | bytes 98336 | tf_op jit(solution)/shard_map/ppermute | solution.py:32
  241.4 5.2 %collective-permute-start.19 = (f16[384,128]{0,1:T(8,128)(2,1)S(1)}, f16[384,128]{0,1:T(8,128)(2,1)S(1)}, u32[]{:S(2)}, u32[]{:S(2)}) collective-permute-start(f16[384,128]{0,1:T(8,128)(2,1)S(1)} %add_convert_fusion), channel_id=1, source_target_pairs={{0,8},{2,10},{8,0},{10,2},{4,12},{6,14},{12,4},{14,6},{1,9},{3,11}... | collective-permute-start | bytes 294920 | tf_op jit(solution)/shard_map/ppermute | solution.py:32
  247.7 13.0 %collective-permute-done.19 = f16[384,128]{0,1:T(8,128)(2,1)S(1)} collective-permute-done((f16[384,128]{0,1:T(8,128)(2,1)S(1)}, f16[384,128]{0,1:T(8,128)(2,1)S(1)}, u32[]{:S(2)}, u32[]{:S(2)}) %collective-permute-start.19) | collective-permute-done | bytes 98336 | tf_op jit(solution)/shard_map/ppermute | solution.py:32
  265.0 3.3 %fusion.16 = f32[128,2048]{1,0:T(8,128)S(1)} fusion(bf16[1024,8192]{1,0:T(8,128)(2,1)} %param.14, s32[]{:T(128)S(6)} %select_n.511, f16[128,2048]{1,0:T(8,128)(2,1)S(1)} %collective-permute-done.33, f16[128,2048]{1,0:T(8,128)(2,1)S(1)} %collective-permute-done.32, f16[128,2048]{1,0:T(8,128)(2,1)} %collective-permute-done.31, pred[]{:T(512)S(6)} %or.2, ...), kind=kOutput, calls=%fused_computation.19 | convolution fusion | flops 538968064 | bytes 7077893 | tf_op jit(solution)/shard_map/dot_general | solution.py:40
  (179 shorter events, 126.9 us)
Async XLA Ops:
  10.7 60.2 %collective-permute-start.1 = (bf16[256,1024]{1,0:T(8,128)(2,1)}, bf16[256,1024]{1,0:T(8,128)(2,1)}, u32[]{:S(2)}, u32[]{:S(2)}) collective-permute-start(bf16[256,1024]{1,0:T(8,128)(2,1)} %slice.126), channel_id=1, source_target_pairs={{8,12},{10,14},{4,0},{6,2},{9,13},{11,15},{5,1},{7,3},{24,28},{26,... | collective-permute-start | bytes 1572872 | tf_op jit(solution)/shard_map/ppermute | solution.py:32
  12.0 59.0 %collective-permute-start.2 = (bf16[256,1024]{1,0:T(8,128)(2,1)}, bf16[256,1024]{1,0:T(8,128)(2,1)}, u32[]{:S(2)}, u32[]{:S(2)}) collective-permute-start(bf16[256,1024]{1,0:T(8,128)(2,1)} %slice.126), channel_id=1, source_target_pairs={{4,8},{6,10},{8,4},{10,6},{5,9},{7,11},{9,5},{11,7},{20,24},{22,26... | collective-permute-start | bytes 1572872 | tf_op jit(solution)/shard_map/ppermute | solution.py:32
  13.4 123.7 %collective-permute-start = (bf16[256,1024]{1,0:T(8,128)(2,1)}, bf16[256,1024]{1,0:T(8,128)(2,1)S(1)}, u32[]{:S(2)}, u32[]{:S(2)}) collective-permute-start(bf16[256,1024]{1,0:T(8,128)(2,1)} %slice.126), channel_id=1, source_target_pairs={{0,2},{2,0},{4,6},{6,4},{8,10},{10,8},{12,14},{14,12},{1,3},{3,1},... | collective-permute-start | bytes 1572872 | tf_op jit(solution)/shard_map/ppermute | solution.py:32
  17.3 57.0 %collective-permute-start.9 = (bf16[128,2048]{1,0:T(8,128)(2,1)}, bf16[128,2048]{1,0:T(8,128)(2,1)S(1)}, u32[]{:S(2)}, u32[]{:S(2)}) collective-permute-start(bf16[128,2048]{1,0:T(8,128)(2,1)} %slice.128), channel_id=1, source_target_pairs={{0,1},{1,0},{2,3},{3,2},{4,5},{5,4},{6,7},{7,6},{8,9},{9,8},{10,11... | collective-permute-start | bytes 1572872 | tf_op jit(solution)/shard_map/ppermute | solution.py:36
  46.6 157.3 %collective-permute-start.16 = (bf16[16,64,1024]{2,1,0:T(8,128)(2,1)}, bf16[16,64,1024]{2,1,0:T(8,128)(2,1)}, u32[]{:S(2)}, u32[]{:S(2)}) collective-permute-start(bf16[16,64,1024]{2,1,0:T(8,128)(2,1)} %select_dynamic-update-slice_fusion), channel_id=1, source_target_pairs={{0,1},{1,0},{2,3},{3,2},{4,5},{5,4},{6,7},{7,6},{8,9},{9,8},{10,11... | collective-permute-start | bytes 6291464 | tf_op jit(solution)/shard_map/ppermute | solution.py:36
  71.0 107.5 %collective-permute-start.21 = (f16[256,1024]{1,0:T(8,128)(2,1)S(1)}, f16[256,1024]{1,0:T(8,128)(2,1)S(1)}, u32[]{:S(2)}, u32[]{:S(2)}) collective-permute-start(f16[256,1024]{1,0:T(8,128)(2,1)S(1)} %copy-done.13), channel_id=1, source_target_pairs={{0,2},{2,0},{4,6},{6,4},{8,10},{10,8},{12,14},{14,12},{1,3},{3,1},... | collective-permute-start | bytes 1572872 | tf_op jit(solution)/shard_map/ppermute | solution.py:32
  75.0 44.6 %collective-permute-start.3 = (bf16[256,1024]{1,0:T(8,128)(2,1)S(1)}, bf16[256,1024]{1,0:T(8,128)(2,1)S(1)}, u32[]{:S(2)}, u32[]{:S(2)}) collective-permute-start(bf16[256,1024]{1,0:T(8,128)(2,1)S(1)} %get-tuple-element.3), channel_id=1, source_target_pairs={{0,2},{2,0},{4,6},{6,4},{8,10},{10,8},{12,14},{14,12},{1,3},{3,1},... | collective-permute-start | bytes 1572872 | tf_op jit(solution)/shard_map/ppermute | solution.py:32
  85.8 27.1 %collective-permute-start.10 = (bf16[128,1024]{1,0:T(8,128)(2,1)S(1)}, bf16[128,1024]{1,0:T(8,128)(2,1)S(1)}, u32[]{:S(2)}, u32[]{:S(2)}) collective-permute-start(bf16[128,1024]{1,0:T(8,128)(2,1)S(1)} %slice.129), channel_id=1, source_target_pairs={{0,2},{2,0},{4,6},{6,4},{8,10},{10,8},{12,14},{14,12},{1,3},{3,1},... | collective-permute-start | bytes 786440 | tf_op jit(solution)/shard_map/ppermute | solution.py:32
  112.9 19.0 %collective-permute-start.4 = (bf16[256,1024]{1,0:T(8,128)(2,1)S(1)}, bf16[256,1024]{1,0:T(8,128)(2,1)S(1)}, u32[]{:S(2)}, u32[]{:S(2)}) collective-permute-start(bf16[256,1024]{1,0:T(8,128)(2,1)S(1)} %get-tuple-element.2), channel_id=1, source_target_pairs={{0,4},{2,6},{4,0},{6,2},{8,12},{10,14},{12,8},{14,10},{1,5},{3,7},... | collective-permute-start | bytes 1572872 | tf_op jit(solution)/shard_map/ppermute | solution.py:32
  119.6 23.5 %collective-permute-start.23 = (f16[256,1024]{1,0:T(8,128)(2,1)S(1)}, f16[256,1024]{1,0:T(8,128)(2,1)S(1)}, u32[]{:S(2)}, u32[]{:S(2)}) collective-permute-start(f16[256,1024]{1,0:T(8,128)(2,1)S(1)} %get-tuple-element.32), channel_id=1, source_target_pairs={{0,4},{2,6},{12,8},{14,10},{1,5},{3,7},{13,9},{15,11},{16,20},{18,... | collective-permute-start | bytes 1572872 | tf_op jit(solution)/shard_map/ppermute | solution.py:32
  131.9 20.6 %collective-permute-start.29 = (f16[128,2048]{1,0:T(8,128)(2,1)S(1)}, f16[128,2048]{1,0:T(8,128)(2,1)S(1)}, u32[]{:S(2)}, u32[]{:S(2)}) collective-permute-start(f16[128,2048]{1,0:T(8,128)(2,1)S(1)} %get-tuple-element.30), channel_id=1, source_target_pairs={{0,4},{2,6},{12,8},{14,10},{1,5},{3,7},{13,9},{15,11},{16,20},{18,... | collective-permute-start | bytes 1572872 | tf_op jit(solution)/shard_map/ppermute | solution.py:32
  137.1 16.1 %collective-permute-start.11 = (bf16[128,2048]{1,0:T(8,128)(2,1)S(1)}, bf16[128,2048]{1,0:T(8,128)(2,1)S(1)}, u32[]{:S(2)}, u32[]{:S(2)}) collective-permute-start(bf16[128,2048]{1,0:T(8,128)(2,1)S(1)} %pad_maximum_fusion.3), channel_id=1, source_target_pairs={{8,12},{10,14},{4,0},{6,2},{9,13},{11,15},{5,1},{7,3},{24,28},{26,... | collective-permute-start | bytes 1572872 | tf_op jit(solution)/shard_map/ppermute | solution.py:32
  152.5 74.9 %collective-permute-start.26 = (f16[256,1024]{1,0:T(8,128)(2,1)}, f16[256,1024]{1,0:T(8,128)(2,1)}, u32[]{:S(2)}, u32[]{:S(2)}) collective-permute-start(f16[256,1024]{1,0:T(8,128)(2,1)} %fusion.103), channel_id=1, source_target_pairs={{0,2},{2,0},{4,6},{6,4},{8,10},{10,8},{12,14},{14,12},{1,3},{3,1},... | collective-permute-start | bytes 1572872 | tf_op jit(solution)/shard_map/ppermute | solution.py:32
  153.2 25.7 %collective-permute-start.24 = (f16[256,1024]{1,0:T(8,128)(2,1)S(1)}, f16[256,1024]{1,0:T(8,128)(2,1)S(1)}, u32[]{:S(2)}, u32[]{:S(2)}) collective-permute-start(f16[256,1024]{1,0:T(8,128)(2,1)S(1)} %multiply_convert_fusion.7), channel_id=1, source_target_pairs={{4,8},{6,10},{8,4},{10,6},{5,9},{7,11},{9,5},{11,7},{20,24},{22,26... | collective-permute-start | bytes 1572872 | tf_op jit(solution)/shard_map/ppermute | solution.py:32
  153.9 22.1 %collective-permute-start.5 = (bf16[256,1024]{1,0:T(8,128)(2,1)S(1)}, bf16[256,1024]{1,0:T(8,128)(2,1)S(1)}, u32[]{:S(2)}, u32[]{:S(2)}) collective-permute-start(bf16[256,1024]{1,0:T(8,128)(2,1)S(1)} %collective-permute-done.4), channel_id=1, source_target_pairs={{0,2},{2,0},{4,6},{6,4},{8,10},{10,8},{12,14},{14,12},{1,3},{3,1},... | collective-permute-start | bytes 1572872 | tf_op jit(solution)/shard_map/ppermute | solution.py:32
  178.5 94.4 %collective-permute-start.20 = (f16[256,1024]{1,0:T(8,128)(2,1)}, f16[256,1024]{1,0:T(8,128)(2,1)}, u32[]{:S(2)}, u32[]{:S(2)}) collective-permute-start(f16[256,1024]{1,0:T(8,128)(2,1)} %fusion.112), channel_id=1, source_target_pairs={{0,2},{2,0},{4,6},{6,4},{8,10},{10,8},{12,14},{14,12},{1,3},{3,1},... | collective-permute-start | bytes 1572872 | tf_op jit(solution)/shard_map/ppermute | solution.py:32
  183.8 15.4 %collective-permute-start.6 = (bf16[256,1024]{1,0:T(8,128)(2,1)S(1)}, bf16[256,1024]{1,0:T(8,128)(2,1)}, u32[]{:S(2)}, u32[]{:S(2)}) collective-permute-start(bf16[256,1024]{1,0:T(8,128)(2,1)S(1)} %collective-permute-done.4), channel_id=1, source_target_pairs={{4,8},{6,10},{8,4},{10,6},{5,9},{7,11},{9,5},{11,7},{20,24},{22,26... | collective-permute-start | bytes 1572872 | tf_op jit(solution)/shard_map/ppermute | solution.py:32
  191.7 40.1 %collective-permute-start.25 = (f16[256,1024]{1,0:T(8,128)(2,1)}, f16[256,1024]{1,0:T(8,128)(2,1)}, u32[]{:S(2)}, u32[]{:S(2)}) collective-permute-start(f16[256,1024]{1,0:T(8,128)(2,1)} %multiply_convert_fusion.6), channel_id=1, source_target_pairs={{0,4},{2,6},{4,0},{6,2},{8,12},{10,14},{12,8},{14,10},{1,5},{3,7},... | collective-permute-start | bytes 1572872 | tf_op jit(solution)/shard_map/ppermute | solution.py:32
  199.2 22.9 %collective-permute-start.31 = (f16[128,2048]{1,0:T(8,128)(2,1)}, f16[128,2048]{1,0:T(8,128)(2,1)}, u32[]{:S(2)}, u32[]{:S(2)}) collective-permute-start(f16[128,2048]{1,0:T(8,128)(2,1)} %fusion.25), channel_id=1, source_target_pairs={{0,4},{2,6},{4,0},{6,2},{8,12},{10,14},{12,8},{14,10},{1,5},{3,7},... | collective-permute-start | bytes 1572872 | tf_op jit(solution)/shard_map/ppermute | solution.py:32
  203.9 37.4 %collective-permute-start.7 = (bf16[256,1024]{1,0:T(8,128)(2,1)}, bf16[256,1024]{1,0:T(8,128)(2,1)}, u32[]{:S(2)}, u32[]{:S(2)}) collective-permute-start(bf16[256,1024]{1,0:T(8,128)(2,1)} %collective-permute-done.6), channel_id=1, source_target_pairs={{8,12},{10,14},{4,0},{6,2},{9,13},{11,15},{5,1},{7,3},{24,28},{26,... | collective-permute-start | bytes 1572872 | tf_op jit(solution)/shard_map/ppermute | solution.py:32
  226.7 34.7 %collective-permute-start.14 = (bf16[128,2048]{1,0:T(8,128)(2,1)S(1)}, bf16[128,2048]{1,0:T(8,128)(2,1)S(1)}, u32[]{:S(2)}, u32[]{:S(2)}) collective-permute-start(bf16[128,2048]{1,0:T(8,128)(2,1)S(1)} %copy-done.10), channel_id=1, source_target_pairs={{4,8},{6,10},{8,4},{10,6},{5,9},{7,11},{9,5},{11,7},{20,24},{22,26... | collective-permute-start | bytes 1572872 | tf_op jit(solution)/shard_map/ppermute | solution.py:32
  227.4 35.3 %collective-permute-start.32 = (f16[128,2048]{1,0:T(8,128)(2,1)S(1)}, f16[128,2048]{1,0:T(8,128)(2,1)S(1)}, u32[]{:S(2)}, u32[]{:S(2)}) collective-permute-start(f16[128,2048]{1,0:T(8,128)(2,1)S(1)} %get-tuple-element.12), channel_id=1, source_target_pairs={{0,4},{2,6},{12,8},{14,10},{1,5},{3,7},{13,9},{15,11},{16,20},{18,... | collective-permute-start | bytes 1572872 | tf_op jit(solution)/shard_map/ppermute | solution.py:32
  240.6 22.9 %collective-permute-start.33 = (f16[128,2048]{1,0:T(8,128)(2,1)S(1)}, f16[128,2048]{1,0:T(8,128)(2,1)S(1)}, u32[]{:S(2)}, u32[]{:S(2)}) collective-permute-start(f16[128,2048]{1,0:T(8,128)(2,1)S(1)} %get-tuple-element.13), channel_id=1, source_target_pairs={{4,8},{6,10},{8,4},{10,6},{5,9},{7,11},{9,5},{11,7},{20,24},{22,26... | collective-permute-start | bytes 1572872 | tf_op jit(solution)/shard_map/ppermute | solution.py:32
  241.4 19.3 %collective-permute-start.19 = (f16[384,128]{0,1:T(8,128)(2,1)S(1)}, f16[384,128]{0,1:T(8,128)(2,1)S(1)}, u32[]{:S(2)}, u32[]{:S(2)}) collective-permute-start(f16[384,128]{0,1:T(8,128)(2,1)S(1)} %add_convert_fusion), channel_id=1, source_target_pairs={{0,8},{2,10},{8,0},{10,2},{4,12},{6,14},{12,4},{14,6},{1,9},{3,11}... | collective-permute-start | bytes 294920 | tf_op jit(solution)/shard_map/ppermute | solution.py:32
  (32 other events, 443.4 us)

commit v2 on v1

v2 whole, which is shorter than its diff:
```python
import functools

import jax
import jax.numpy as jnp
from jax import lax
from jax.experimental import pallas as pl
from jax.experimental.pallas import tpu as pltpu
from jax.sharding import PartitionSpec as P

REQUEST_LENGTH = 256

adapter_scale = 0.5

SUM_SCALE = 8.0
DOWN_SCALE = 16.0

BF16 = jnp.bfloat16
F16 = jnp.float16
F32 = jnp.float32
I32 = jnp.int32

VMEM_LIMIT = 48 * 1024 * 1024


def z_pairs(*pairs):
    return [(2 * a + y, 2 * b + y) for a, b in pairs for y in range(2)]


INNER = z_pairs((1, 2), (2, 1))
OUTWARD = z_pairs((2, 3), (1, 0))
INWARD = z_pairs((0, 1), (3, 2))
SIDES = z_pairs((0, 1), (1, 0), (2, 3), (3, 2))
Y_SWAP = [(t, t ^ 1) for t in range(8)]
FAR = z_pairs((0, 2), (2, 0), (1, 3), (3, 1))

OWN = (0, 1, 2, 3)
ONE = (1, 2, 1, 2)
TWO = (2, 0, 3, 1)
THREE = (3, 3, 0, 0)


def send(value, pairs):
    return lax.ppermute(value, "tensor", pairs)


def other_replica(value):
    return lax.ppermute(value, "replica", [(0, 1), (1, 0)])


def dot(a, b):
    return jnp.dot(a, b, preferred_element_type=F32)


def dot_t(a, b):
    return lax.dot_general(a, b, (((1,), (1,)), ((), ())), preferred_element_type=F32)


def by_z(z, table):
    out = I32(table[0])
    for i in range(1, 4):
        out = jnp.where(z == i, I32(table[i]), out)
    return out


def whole(shape):
    return pl.BlockSpec(shape, lambda *_: (0,) * len(shape))


def params(n=1):
    return pltpu.CompilerParams(
        dimension_semantics=("arbitrary",) * n, vmem_limit_bytes=VMEM_LIMIT
    )


def iota(shape, dim):
    return lax.broadcasted_iota(I32, shape, dim)


def pack_kernel(counts, x_ref, a_ref, b_ref, spare_ref):
    rows = x_ref.shape[0]
    first, spare = a_ref.shape[0], spare_ref.shape[0]
    packed = first + b_ref.shape[0]
    c_a, n_mine = counts[0], counts[0] + counts[1]
    n_theirs = counts[2] + counts[3]

    def take(position, live):
        home = jnp.where(position < c_a, position, REQUEST_LENGTH + position - c_a)
        hot = iota((position.shape[0], rows), 1) == jnp.where(live, home, -1)
        return dot(hot.astype(F32).astype(BF16), x_ref[...]).astype(BF16)

    slot = iota((packed, 1), 0)
    here = take(slot, slot < n_mine)
    a_ref[...] = here[:first]
    b_ref[...] = here[first:]
    seat = iota((spare, 1), 0) + first - n_theirs
    spare_ref[...] = take(packed + seat, seat >= 0)


def pack(counts, x, packed):
    rows, width = x.shape
    spare = rows - packed
    first = packed - spare
    shapes = [(first, width), (packed - first, width), (spare, width)]
    return pl.pallas_call(
        pack_kernel,
        grid_spec=pltpu.PrefetchScalarGridSpec(
            num_scalar_prefetch=1,
            grid=(1,),
            in_specs=[whole(x.shape)],
            out_specs=[whole(s) for s in shapes],
        ),
        out_shape=[jax.ShapeDtypeStruct(s, BF16) for s in shapes],
        compiler_params=params(),
        name="pack_rows",
    )(counts, x)


def unpack_kernel(counts, qa, qb, qc, oa, ob, oc, q_ref, o_ref):
    rows = q_ref.shape[0]
    first = qa.shape[0]
    packed = first + qb.shape[0]
    c_a, c_b = counts[0], counts[1]
    n_theirs = counts[2] + counts[3]
    row = iota((rows, 1), 0)
    late = row >= REQUEST_LENGTH
    offset = jnp.where(late, row - REQUEST_LENGTH, row)
    position = offset + jnp.where(late, c_a, 0)
    target = jnp.where(position < packed, position, position + n_theirs - first)
    target = jnp.where(offset < jnp.where(late, c_b, c_a), target, -1)
    hot = (iota((rows, rows), 1) == target).astype(F32).astype(BF16)
    for a, b, c, out in ((qa, qb, qc, q_ref), (oa, ob, oc, o_ref)):
        out[...] = (
            dot(hot[:, :first], a[...]) + dot(hot[:, first:packed], b[...]) + dot(hot[:, packed:], c[...])
        ).astype(BF16)


def unpack(counts, rows, parts):
    width = parts[0].shape[1]
    shape = (rows, width)
    return pl.pallas_call(
        unpack_kernel,
        grid_spec=pltpu.PrefetchScalarGridSpec(
            num_scalar_prefetch=1,
            grid=(1,),
            in_specs=[whole(p.shape) for p in parts],
            out_specs=[whole(shape)] * 2,
        ),
        out_shape=[jax.ShapeDtypeStruct(shape, BF16)] * 2,
        compiler_params=params(),
        name="unpack_rows",
    )(counts, *parts)


def request_of(counts, slot, packed):
    c_a, n_mine, d_a = counts[0], counts[0] + counts[1], counts[2]
    replica = counts[4]
    own = slot < n_mine
    seat = jnp.where(own, slot, packed + slot - n_mine)
    mine = 2 * replica + (seat >= c_a).astype(I32)
    theirs = 2 * (1 - replica) + (seat >= d_a).astype(I32)
    return jnp.where(own, mine, theirs)


def fetch_kernel(adapter_of, location, replica, *refs):
    stores, out = refs[:4], refs[4]
    held = pl.num_programs(0)
    del held
    i = pl.program_id(0)
    slot = location[adapter_of[i]] - replica[0] * replica[1]
    mine = (slot >= 0) & (slot < replica[1])
    for k, table in enumerate(stores):
        block = table[0]
        out[k] = jnp.where(mine, block, jnp.zeros_like(block))


def fetch(stores, adapter_of, location, replica):
    held, rank, width = stores[0].shape
    requests = adapter_of.shape[0]

    def at(i, adapter_of, location, replica):
        slot = location[adapter_of[i]] - replica[0] * held
        return jnp.clip(slot, 0, held - 1), 0, 0

    return pl.pallas_call(
        fetch_kernel,
        grid_spec=pltpu.PrefetchScalarGridSpec(
            num_scalar_prefetch=3,
            grid=(requests,),
            in_specs=[pl.BlockSpec((1, rank, width), at)] * 4,
            out_specs=pl.BlockSpec((4, rank, width), lambda i, *_: (0, i, 0)),
        ),
        out_shape=jax.ShapeDtypeStruct((4, requests * rank, width), BF16),
        compiler_params=params(),
        name="fetch_blocks",
    )(adapter_of, location, jnp.stack([replica, I32(held)]), *stores)


def down_kernel(counts, xa, xb, va, vb, own, other, out, blocks):
    rank = out.shape[1] // 2
    width = xa.shape[1]
    requests = own.shape[1] // rank
    first, packed = xa.shape[0], out.shape[0]
    blocks[...] = jnp.zeros_like(blocks)
    who = request_of(counts, iota((packed, 1), 0), packed)
    total = [jnp.zeros((first, 2 * rank), F32), jnp.zeros((packed - first, 2 * rank), F32)]
    for i in range(requests):
        rows = pl.ds(i * rank, rank)
        blocks[:rank, :width] = own[0, rows] + other[0, rows]
        blocks[rank:, width:] = own[1, rows] + other[1, rows]
        for k, (x, v, lo, hi) in enumerate(((xa, va, 0, first), (xb, vb, first, packed))):
            got = dot_t(x[...], blocks[:, :width]) + dot_t(v[...], blocks[:, width:])
            total[k] = total[k] + jnp.where(who[lo:hi] == i, got, 0.0)
    out[:first] = total[0]
    out[first:] = total[1]


def down(counts, xa, xb, va, vb, own, other):
    requests_rank, width = own.shape[1:]
    rank = requests_rank // 4
    packed = xa.shape[0] + xb.shape[0]
    half = (2, requests_rank, width)
    return pl.pallas_call(
        down_kernel,
        grid_spec=pltpu.PrefetchScalarGridSpec(
            num_scalar_prefetch=1,
            grid=(1,),
            in_specs=[whole(v.shape) for v in (xa, xb, va, vb)] + [whole(half)] * 2,
            out_specs=whole((packed, 2 * rank)),
            scratch_shapes=[pltpu.VMEM((2 * rank, 2 * width), BF16)],
        ),
        out_shape=jax.ShapeDtypeStruct((packed, 2 * rank), F32),
        compiler_params=params(),
        name="down_rows",
    )(counts, xa, xb, va, vb, own, other)


def up_kernel(counts, low, own, other, q_ref, o_ref, blocks):
    packed, both = low.shape
    rank = both // 2
    width = q_ref.shape[1]
    requests = own.shape[1] // rank
    blocks[...] = jnp.zeros_like(blocks)
    who = request_of(counts, iota((packed, 1), 0), packed)
    rows_low = low[...].astype(BF16).astype(F32)
    for i in range(requests):
        rows = pl.ds(i * rank, rank)
        blocks[pl.ds(2 * i * rank, rank), :width] = own[0, rows] + other[0, rows]
        blocks[pl.ds((2 * i + 1) * rank, rank), width:] = own[1, rows] + other[1, rows]
    wide = jnp.concatenate(
        [jnp.where(who == i, rows_low, 0.0).astype(BF16) for i in range(requests)], axis=1
    )
    q_ref[...] = adapter_scale * dot(wide, blocks[:, :width])
    o_ref[...] = adapter_scale * dot(wide, blocks[:, width:])


def up(counts, low, own, other):
    packed, both = low.shape
    requests_rank, width = own.shape[1:]
    half = (2, requests_rank, width)
    return pl.pallas_call(
        up_kernel,
        grid_spec=pltpu.PrefetchScalarGridSpec(
            num_scalar_prefetch=1,
            grid=(1,),
            in_specs=[whole(low.shape)]
            + [pl.BlockSpec(half, lambda *_: (1, 0, 0))] * 2,
            out_specs=[whole((packed, width))] * 2,
            scratch_shapes=[pltpu.VMEM((2 * requests_rank, 2 * width), BF16)],
        ),
        out_shape=[jax.ShapeDtypeStruct((packed, width), F32)] * 2,
        compiler_params=params(),
        name="up_rows",
    )(counts, low, own, other)


def shares_kernel(where, a_ref, b_ref, w_ref, cross_ref, own_ref, both_ref):
    j = pl.program_id(0)
    got = dot(a_ref[...], w_ref[...])
    both_ref[...] = dot(b_ref[...], w_ref[...])

    @pl.when(j < pl.num_programs(0) // 2)
    def _():
        cross_ref[...] = got

    @pl.when(j >= pl.num_programs(0) // 2)
    def _():
        own_ref[...] = got


def shares(owner, y, a, b, weight):
    width = a.shape[1]
    step = width // 2

    def column(j, where):
        return 2 * jnp.where(j < 2, 1 - where[1], where[1]) + j % 2

    return pl.pallas_call(
        shares_kernel,
        grid_spec=pltpu.PrefetchScalarGridSpec(
            num_scalar_prefetch=1,
            grid=(4,),
            in_specs=[
                whole(a.shape),
                whole(b.shape),
                pl.BlockSpec((width, step), lambda j, where: (0, 4 * where[0] + column(j, where))),
            ],
            out_specs=[
                pl.BlockSpec((a.shape[0], step), lambda j, where: (0, jnp.minimum(j, 1))),
                pl.BlockSpec((a.shape[0], step), lambda j, where: (0, jnp.maximum(j - 2, 0))),
                pl.BlockSpec((b.shape[0], step), lambda j, where: (0, column(j, where))),
            ],
        ),
        out_shape=[
            jax.ShapeDtypeStruct((a.shape[0], width), F32),
            jax.ShapeDtypeStruct((a.shape[0], width), F32),
            jax.ShapeDtypeStruct((b.shape[0], 2 * width), F32),
        ],
        compiler_params=params(),
        cost_estimate=pl.CostEstimate(
            flops=4 * (a.shape[0] + b.shape[0]) * width * width,
            bytes_accessed=4 * width * width + 2 * width * (a.shape[0] + b.shape[0]),
            transcendentals=0,
        ),
        name="shares",
    )(jnp.stack([owner, y]), a, b, weight)


def add_kernel(count, *refs):
    refs = refs[1:]
    pieces, weights, start, out = refs[:count], refs[count : 2 * count], refs[2 * count], refs[-1]
    total = start[...]
    for x, w in zip(pieces, weights):
        total = total + dot(x[...], w[...])
    out[...] = total


def add_products(start, pieces, at, weight):
    rows, columns = start.shape
    step = columns // 4
    count = len(pieces)

    def rows_of(i, depth, width):
        return pl.BlockSpec((depth, step), lambda j, at, i=i: (at[i], j))

    return pl.pallas_call(
        functools.partial(add_kernel, count),
        grid_spec=pltpu.PrefetchScalarGridSpec(
            num_scalar_prefetch=1,
            grid=(4,),
            in_specs=[whole(p.shape) for p in pieces]
            + [rows_of(i, p.shape[1], step) for i, p in enumerate(pieces)]
            + [pl.BlockSpec((rows, step), lambda j, at: (0, j))],
            out_specs=pl.BlockSpec((rows, step), lambda j, at: (0, j)),
        ),
        out_shape=jax.ShapeDtypeStruct((rows, columns), F32),
        compiler_params=params(),
        cost_estimate=pl.CostEstimate(
            flops=sum(2 * rows * columns * p.shape[1] for p in pieces),
            bytes_accessed=sum(2 * columns * p.shape[1] + 2 * rows * p.shape[1] for p in pieces),
            transcendentals=0,
        ),
        name="add_products",
    )(jnp.stack(at), *pieces, *([weight] * count), start)


def gather_z(x, edge):
    near_in, near_out = send(x, INNER), send(x, OUTWARD)
    one = jnp.where(edge, near_out, near_in)
    two = send(jnp.where(edge, x, one), SIDES)
    mid = send(two, INNER)
    out = send(mid, OUTWARD)
    three = jnp.where(edge, out, mid)
    return [x, one, two, three]


def narrow(value):
    return (value * SUM_SCALE).astype(F16)


def widen(value):
    return value.astype(F32) * (1.0 / SUM_SCALE)


def scatter_z(part, edge):
    r1 = send(narrow(part[0]), INWARD)
    r2 = send(narrow(part[0] + widen(r1)), INNER)
    r3 = send(narrow(part[1] + widen(r2)), SIDES)
    r4a = send(narrow(part[2]), INWARD)
    r4b = send(narrow(part[2] + widen(r3)), INNER)
    return part[3] + jnp.where(edge, widen(r3), widen(r4a) + widen(r4b))


def exchange(a_tok, b_tok, a_ctx, b_ctx, query_weight, output_weight, z, y):
    width = a_tok.shape[1]
    edge = (z == 0) | (z == 3)
    owners = [by_z(z, table) for table in (THREE, TWO, ONE, OWN)]
    shards = [by_z(z, table) for table in (OWN, ONE, TWO, THREE)]

    a_line = gather_z(a_tok, edge)
    b_pair = send(b_tok, Y_SWAP)
    parts = [shares(owner, y, a_ctx, b_ctx, output_weight) for owner in owners]
    a_from_y = [send(narrow(cross), Y_SWAP) for cross, _, _ in parts]
    b_sum = scatter_z([both for _, _, both in parts], edge)
    a_sum = scatter_z([own + widen(got) for (_, own, _), got in zip(parts, a_from_y)], edge)
    b_both = jnp.concatenate(
        [jnp.where(y == 0, b_tok, b_pair), jnp.where(y == 0, b_pair, b_tok)], axis=1
    )
    b_line = gather_z(b_both, edge)
    a_cross = [send(v, Y_SWAP) for v in a_line]
    low_half, high_half = b_sum[:, :width], b_sum[:, width:]
    b_mine = jnp.where(y == 0, low_half, high_half)
    b_theirs = jnp.where(y == 0, high_half, low_half)
    b_sum = b_mine + widen(send(narrow(b_theirs), Y_SWAP))

    columns = query_weight.shape[1]
    a_q = jnp.zeros((a_tok.shape[0], columns), F32)
    b_q = jnp.zeros((b_tok.shape[0], columns), F32)
    a_q = add_products(a_q, a_line, [2 * s + y for s in shards], query_weight)
    a_q = add_products(a_q, a_cross, [2 * s + 1 - y for s in shards], query_weight)
    b_q = add_products(b_q, b_line, shards, query_weight)
    return a_q, b_q, a_sum, b_sum


def sum_over_tensor(part):
    total = part
    for pairs in (Y_SWAP, SIDES, FAR):
        mine = (total * DOWN_SCALE).astype(F16)
        moved = send(mine, pairs)
        total = (mine.astype(F32) + moved.astype(F32)) * (1.0 / DOWN_SCALE)
    return total


def make(mesh):
    grid = mesh.shape["tensor"] == 8

    def local(
        tokens, context, query_weight, output_weight,
        store_aq, store_bq, store_ao, store_bo,
        adapter_of, location, token_count,
    ):
        rows, width = tokens.shape
        per = rows // REQUEST_LENGTH
        packed = rows * 3 // 4
        spare = rows - packed
        first = packed - spare
        replica = lax.axis_index("replica")
        at = lax.axis_index("tensor")
        z, y = at // 2, at % 2
        flip = jnp.where(replica == 0, token_count, jnp.roll(token_count, per))
        counts = jnp.concatenate([flip, replica[None]]).astype(I32)

        tok_a, tok_b, tok_c = pack(counts, tokens, packed)
        ctx_a, ctx_b, ctx_c = pack(counts, context, packed)
        tok_b = tok_b + other_replica(tok_c)
        ctx_b = ctx_b + other_replica(ctx_c)

        own = fetch((store_aq, store_ao, store_bq, store_bo), adapter_of, location, replica)
        other = other_replica(own)
        parts = down(counts, tok_a, tok_b, ctx_a, ctx_b, own, other)

        if grid:
            low = sum_over_tensor(parts)
            q_a, q_b, o_a, o_b = exchange(
                tok_a, tok_b, ctx_a, ctx_b, query_weight, output_weight, z, y
            )
        else:
            low = lax.psum(parts, "tensor")
            tok = jnp.concatenate([tok_a, tok_b])
            ctx = jnp.concatenate([ctx_a, ctx_b])
            base_q = dot(lax.all_gather(tok, "tensor", axis=1, tiled=True), query_weight)
            base_o = lax.psum_scatter(
                dot(ctx, output_weight), "tensor", scatter_dimension=1, tiled=True
            )
            q_a, q_b, o_a, o_b = base_q[:first], base_q[first:], base_o[:first], base_o[first:]

        up_q, up_o = up(counts, low, own, other)
        q_a, q_b = (q_a + up_q[:first]).astype(BF16), (q_b + up_q[first:]).astype(BF16)
        o_a, o_b = (o_a + up_o[:first]).astype(BF16), (o_b + up_o[first:]).astype(BF16)
        return tuple(
            unpack(counts, rows, (q_a, q_b, other_replica(q_b), o_a, o_b, other_replica(o_b)))
        )

    return local


def solution(mesh):
    return jax.shard_map(
        make(mesh),
        mesh=mesh,
        in_specs=(
            P(("groups", "replica"), "tensor"),
            P(("groups", "replica"), "tensor"),
            P(None, "tensor"),
            P("tensor", None),
            P(("groups", "replica"), None, "tensor"),
            P(("groups", "replica"), None, "tensor"),
            P(("groups", "replica"), None, "tensor"),
            P(("groups", "replica"), None, "tensor"),
            P("groups"),
            P("groups"),
            P("groups"),
        ),
        out_specs=(P(("groups", "replica"), "tensor"), P(("groups", "replica"), "tensor")),
        check_vma=False,
    )
```

time: 288 us -> 192 us (0.67)
  matrix products: 67.4 us -> 0 us
  Pallas kernels: 0 us -> 57.7 us
  waiting for transfers between devices: 99.9 us -> 53.4 us
  other arithmetic: 44 us -> 13.8 us
  local copies, waits for them, and re-layouts: 9.72 us -> 4.44 us
    dot_general x30 -> x0, matrix products: 67.4 us -> none  [the longest x28 63.7 us: dot(): return jnp.dot(a, b, preferred_element_type=F32)]
    pallas_call x0 -> x13, Pallas kernels: none -> 57.7 us  [the longest x4 20.8 us: shares(): pl.pallas_call(shares_kernel, grid_spec=pltpu.PrefetchScalarGridSpec(num_...]
    ppermute x33, waiting for transfers between devices: 98 us -> 53.4 us  [send(): return lax.ppermute(value, 'tensor', pairs)]
    unnamed x16 -> x0, other arithmetic: 23.8 us -> none
    slice x9 -> x1, local copies, waits for them, and re-layouts: 6.19 us -> 0.8 us  [local(): flip = jnp.where(replica == 0, token_count, jnp.roll(token_count, per))]
    add x5 -> x3, other arithmetic: 6.88 us -> 3.49 us  [the longest x1 1.37 us: scatter_z(): return part[3] + jnp.where(edge, widen(r3), widen(r4a) + widen(r4b))]
    another operation x4 -> x6, other arithmetic: 3.37 us -> 0.45 us  [the longest x3 0.23 us: add_products(): jnp.stack(at)]
  transfers between devices with their start and end apart: 36 -> 38, of which waited for: 13 -> 9; matrix products, arithmetic and copies ran while one was open for 36% -> 7% of each run, Pallas kernels for 0% -> 28%
where the time goes in v2:
time: 192 us; the launch traced here: 191 us
  starting transfers between devices  59.9 us (31%)
  Pallas kernels  57.7 us (30%)
  waiting for transfers between devices  53.4 us (28%)
  other arithmetic  13.8 us (7%)
  local copies, waits for them, and re-layouts  4.44 us (2%)
    ppermute x33, starting transfers between devices, send(): return lax.ppermute(value, 'tensor', pairs)  58.8 us
    ppermute x33, waiting for transfers between devices, send(): return lax.ppermute(value, 'tensor', pairs)  53.4 us
    pallas_call x4, Pallas kernels, shares(): pl.pallas_call(shares_kernel, grid_spec=pltpu.PrefetchScalarGridSpec(num_...  20.8 us
    pallas_call x3, Pallas kernels, add_products(): pl.pallas_call(functools.partial(add_kernel, count), grid_spec=pltpu.Pref...  20.2 us
    convert_element_type x13, other arithmetic, narrow(): return (value * SUM_SCALE).astype(F16)  4.4 us
    pallas_call x2, Pallas kernels, pack(): pl.pallas_call(pack_kernel, grid_spec=pltpu.PrefetchScalarGridSpec(num_sc...  3.92 us
  transfers between devices with their start and end apart: 38, of which 9 were waited for; matrix products, arithmetic and copies ran while one was open for 7% of the time, Pallas kernels for 28%

profile of v2, /device:TPU:0, one launch (start us, length us, event | category | flops | bytes accessed | tf_op | source)
XLA Modules:
  0.0 190.6 jit_solution(15752454635282838751)
XLA Ops:
  12.1 3.1 %fetch_blocks.1.own = bf16[4,256,1024]{2,1,0:T(8,128)(2,1)S(1)} custom-call(s32[4]{0:T(128)S(1)} %copy-done.10, s32[32]{0:T(128)S(1)} %copy-done.11, s32[2]{0:T(128)S(1)} %pad_add_fusion.3.replica, bf16[16,64,1024]{2,1,0:T(8,128)(2,1)S(1)} %copy-done, bf16[16,64,1024]{2,1,0:T(8,128)(2,1)} %refs_1_.1, bf16[16,64,1024]{2,1,0:T(8,128)(2,1)} %refs_2_.1, ...), custom_call_target="tpu_custom_call" | custom-call | tf_op jit(solution)/shard_map/fetch_blocks/pallas_call | solution.py:184
  16.9 3.0 %collective-permute-start.15 = (bf16[128,1024]{1,0:T(8,128)(2,1)S(1)}, bf16[128,1024]{1,0:T(8,128)(2,1)}, u32[]{:S(2)}, u32[]{:S(2)}) collective-permute-start(bf16[128,1024]{1,0:T(8,128)(2,1)S(1)} %add.112.xb), channel_id=1, source_target_pairs={{0,2},{2,0},{4,6},{6,4},{8,10},{10,8},{12,14},{14,12},{1,3},{3,1},... | collective-permute-start | bytes 786440 | tf_op jit(solution)/shard_map/ppermute | solution.py:43
  21.0 5.2 %shares.7 = (f32[256,1024]{1,0:T(8,128)S(1)}, f32[256,1024]{1,0:T(8,128)S(1)}, f32[128,2048]{1,0:T(8,128)S(1)}) custom-call(s32[2]{0:T(128)S(1)} %get-tuple-element.57.where, bf16[256,1024]{1,0:T(8,128)(2,1)S(1)} %get-tuple-element.25.va.a_ref, bf16[128,1024]{1,0:T(8,128)(2,1)S(1)} %add.113.vb.b_ref, bf16[1024,8192]{1,0:T(8,128)(2,1)} %w_ref.7), custom_call_target="tpu_custom_call" | custom-call | flops 1610612736 | bytes 4980736 | tf_op jit(solution)/shard_map/shares/pallas_call | solution.py:297
  26.3 5.2 %shares.6 = (f32[256,1024]{1,0:T(8,128)S(1)}, f32[256,1024]{1,0:T(8,128)S(1)}, f32[128,2048]{1,0:T(8,128)S(1)}) custom-call(s32[2]{0:T(128)S(1)} %get-tuple-element.56.where, bf16[256,1024]{1,0:T(8,128)(2,1)S(1)} %get-tuple-element.25.va.a_ref, bf16[128,1024]{1,0:T(8,128)(2,1)S(1)} %add.113.vb.b_ref, bf16[1024,8192]{1,0:T(8,128)(2,1)} %w_ref.7), custom_call_target="tpu_custom_call" | custom-call | flops 1610612736 | bytes 4980736 | tf_op jit(solution)/shard_map/shares/pallas_call | solution.py:297
  31.8 6.3 %collective-permute-start.31 = (f16[128,2048]{1,0:T(8,128)(2,1)S(1)}, f16[128,2048]{1,0:T(8,128)(2,1)S(1)}, u32[]{:S(2)}, u32[]{:S(2)}) collective-permute-start(f16[128,2048]{1,0:T(8,128)(2,1)S(1)} %multiply_convert_fusion.4), channel_id=1, source_target_pairs={{0,4},{2,6},{12,8},{14,10},{1,5},{3,7},{13,9},{15,11},{16,20},{18,... | collective-permute-start | bytes 1572872 | tf_op jit(solution)/shard_map/ppermute | solution.py:43
  38.1 5.2 %shares.5 = (f32[256,1024]{1,0:T(8,128)S(1)}, f32[256,1024]{1,0:T(8,128)S(1)}, f32[128,2048]{1,0:T(8,128)S(1)}) custom-call(s32[2]{0:T(128)S(1)} %get-tuple-element.55.where, bf16[256,1024]{1,0:T(8,128)(2,1)S(1)} %get-tuple-element.25.va.a_ref, bf16[128,1024]{1,0:T(8,128)(2,1)S(1)} %add.113.vb.b_ref, bf16[1024,8192]{1,0:T(8,128)(2,1)} %w_ref.7), custom_call_target="tpu_custom_call" | custom-call | flops 1610612736 | bytes 4980736 | tf_op jit(solution)/shard_map/shares/pallas_call | solution.py:297
  44.3 5.2 %shares.4 = (f32[256,1024]{1,0:T(8,128)S(1)}, f32[256,1024]{1,0:T(8,128)S(1)}, f32[128,2048]{1,0:T(8,128)S(1)}) custom-call(s32[2]{0:T(128)S(1)} %get-tuple-element.54.where, bf16[256,1024]{1,0:T(8,128)(2,1)S(1)} %get-tuple-element.25.va.a_ref, bf16[128,1024]{1,0:T(8,128)(2,1)S(1)} %add.113.vb.b_ref, bf16[1024,8192]{1,0:T(8,128)(2,1)} %w_ref.7), custom_call_target="tpu_custom_call" | custom-call | flops 1610612736 | bytes 4980736 | tf_op jit(solution)/shard_map/shares/pallas_call | solution.py:297
  54.5 9.9 %collective-permute-done.24 = f16[256,1024]{1,0:T(8,128)(2,1)S(1)} collective-permute-done((f16[256,1024]{1,0:T(8,128)(2,1)S(1)}, f16[256,1024]{1,0:T(8,128)(2,1)S(1)}, u32[]{:S(2)}, u32[]{:S(2)}) %collective-permute-start.24) | collective-permute-done | bytes 524320 | tf_op jit(solution)/shard_map/ppermute | solution.py:43
  69.2 7.6 %collective-permute-done.25 = f16[256,1024]{1,0:T(8,128)(2,1)S(1)} collective-permute-done((f16[256,1024]{1,0:T(8,128)(2,1)S(1)}, f16[256,1024]{1,0:T(8,128)(2,1)S(1)}, u32[]{:S(2)}, u32[]{:S(2)}) %collective-permute-start.25) | collective-permute-done | bytes 524320 | tf_op jit(solution)/shard_map/ppermute | solution.py:43
  80.2 3.5 %collective-permute-done.16 = bf16[128,2048]{1,0:T(8,128)(2,1)S(1)} collective-permute-done((bf16[128,2048]{1,0:T(8,128)(2,1)S(1)}, bf16[128,2048]{1,0:T(8,128)(2,1)S(1)}, u32[]{:S(2)}, u32[]{:S(2)}) %collective-permute-start.16) | collective-permute-done | bytes 524320 | tf_op jit(solution)/shard_map/ppermute | solution.py:43
  86.0 6.9 %collective-permute-done.33 = f16[128,2048]{1,0:T(8,128)(2,1)S(1)} collective-permute-done((f16[128,2048]{1,0:T(8,128)(2,1)S(1)}, f16[128,2048]{1,0:T(8,128)(2,1)S(1)}, u32[]{:S(2)}, u32[]{:S(2)}) %collective-permute-start.33) | collective-permute-done | bytes 524320 | tf_op jit(solution)/shard_map/ppermute | solution.py:43
  94.5 2.7 %collective-permute-start.18 = (bf16[128,2048]{1,0:T(8,128)(2,1)}, bf16[128,2048]{1,0:T(8,128)(2,1)S(1)}, u32[]{:S(2)}, u32[]{:S(2)}) collective-permute-start(bf16[128,2048]{1,0:T(8,128)(2,1)} %get-tuple-element.42), channel_id=1, source_target_pairs={{0,4},{2,6},{4,0},{6,2},{8,12},{10,14},{12,8},{14,10},{1,5},{3,7},... | collective-permute-start | bytes 1572872 | tf_op jit(solution)/shard_map/ppermute | solution.py:43
  97.3 8.2 %collective-permute-start.34 = (f16[128,2048]{1,0:T(8,128)(2,1)S(1)}, f16[128,2048]{1,0:T(8,128)(2,1)S(1)}, u32[]{:S(2)}, u32[]{:S(2)}) collective-permute-start(f16[128,2048]{1,0:T(8,128)(2,1)S(1)} %get-tuple-element.48), channel_id=1, source_target_pairs={{0,4},{2,6},{12,8},{14,10},{1,5},{3,7},{13,9},{15,11},{16,20},{18,... | collective-permute-start | bytes 1572872 | tf_op jit(solution)/shard_map/ppermute | solution.py:43
  107.2 3.6 %down_rows.1 = f32[384,128]{1,0:T(8,128)S(1)} custom-call(s32[5]{0:T(128)S(1)} %pad_add_fusion.counts, bf16[256,1024]{1,0:T(8,128)(2,1)S(1)} %get-tuple-element.22.refs_1_.xa, bf16[128,1024]{1,0:T(8,128)(2,1)S(1)} %add.112.xb, bf16[256,1024]{1,0:T(8,128)(2,1)S(1)} %get-tuple-element.25.va.a_ref, bf16[128,1024]{1,0:T(8,128)(2,1)S(1)} %add.113.vb.b_ref, ...), custom_call_target="tpu_custom_call" | custom-call | tf_op jit(solution)/shard_map/down_rows/pallas_call | solution.py:222
  112.5 3.0 %collective-permute-done.12 = f16[384,128]{1,0:T(8,128)(2,1)S(1)} collective-permute-done((f16[384,128]{1,0:T(8,128)(2,1)S(1)}, f16[384,128]{1,0:T(8,128)(2,1)S(1)}, u32[]{:S(2)}, u32[]{:S(2)}) %collective-permute-start.12) | collective-permute-done | bytes 98336 | tf_op jit(solution)/shard_map/ppermute | solution.py:43
  117.3 6.1 %add_products.3.refs_9_ = f32[256,1024]{1,0:T(8,128)S(1)} custom-call(s32[4]{0:T(128)S(1)} %pad_add_fusion.2.refs_0_, bf16[256,1024]{1,0:T(8,128)(2,1)S(1)} %get-tuple-element.22.refs_1_.xa, bf16[256,1024]{1,0:T(8,128)(2,1)S(1)} %get-tuple-element.45.refs_2_, bf16[256,1024]{1,0:T(8,128)(2,1)S(1)} %collective-permute-done.4.refs_3_, ...), custom_call_target="tpu_custom_call" | custom-call | flops 2147483648 | bytes 10485760 | tf_op jit(solution)/shard_map/add_products/pallas_call | solution.py:345
  126.5 3.5 %collective-permute-start.27 = (f16[256,1024]{1,0:T(8,128)(2,1)S(1)}, f16[256,1024]{1,0:T(8,128)(2,1)S(1)}, u32[]{:S(2)}, u32[]{:S(2)}) collective-permute-start(f16[256,1024]{1,0:T(8,128)(2,1)S(1)} %multiply_convert_fusion.8), channel_id=1, source_target_pairs={{0,4},{2,6},{4,0},{6,2},{8,12},{10,14},{12,8},{14,10},{1,5},{3,7},... | collective-permute-start | bytes 1572872 | tf_op jit(solution)/shard_map/ppermute | solution.py:43
  131.4 6.9 %collective-permute-done.28 = f16[256,1024]{1,0:T(8,128)(2,1)S(1)} collective-permute-done((f16[256,1024]{1,0:T(8,128)(2,1)S(1)}, f16[256,1024]{1,0:T(8,128)(2,1)S(1)}, u32[]{:S(2)}, u32[]{:S(2)}) %collective-permute-start.28) | collective-permute-done | bytes 524320 | tf_op jit(solution)/shard_map/ppermute | solution.py:43
  147.0 2.8 %collective-permute-start.8 = (bf16[256,1024]{1,0:T(8,128)(2,1)S(1)}, bf16[256,1024]{1,0:T(8,128)(2,1)S(1)}, u32[]{:S(2)}, u32[]{:S(2)}) collective-permute-start(bf16[256,1024]{1,0:T(8,128)(2,1)S(1)} %broadcast_select_fusion.3.refs_4_), channel_id=1, source_target_pairs={{0,2},{2,0},{4,6},{6,4},{8,10},{10,8},{12,14},{14,12},{1,3},{3,1},... | collective-permute-start | bytes 1572872 | tf_op jit(solution)/shard_map/ppermute | solution.py:43
  149.9 2.8 %up_rows.1 = (f32[384,1024]{1,0:T(8,128)S(1)}, f32[384,1024]{1,0:T(8,128)S(1)}) custom-call(s32[5]{0:T(128)S(1)} %pad_add_fusion.counts, f32[384,128]{1,0:T(8,128)S(1)} %add_multiply_fusion.low, bf16[4,256,1024]{2,1,0:T(8,128)(2,1)S(1)} %fetch_blocks.1.own, bf16[4,256,1024]{2,1,0:T(8,128)(2,1)} %collective-permute-done.11.other), custom_call_target="tpu_custom_call" | custom-call | tf_op jit(solution)/shard_map/up_rows/pallas_call | solution.py:260
  153.6 8.0 %add_products.5 = f32[128,1024]{1,0:T(8,128)S(1)} custom-call(s32[4]{0:T(128)S(1)} %pad_add_fusion.4.refs_0_, bf16[128,2048]{1,0:T(8,128)(2,1)S(1)} %pad_maximum_fusion.refs_1_, bf16[128,2048]{1,0:T(8,128)(2,1)S(1)} %get-tuple-element.43.refs_2_, bf16[128,2048]{1,0:T(8,128)(2,1)S(1)} %collective-permute-done.18.refs_3_, ...), custom_call_target="tpu_custom_call" | custom-call | flops 2147483648 | bytes 18874368 | tf_op jit(solution)/shard_map/add_products/pallas_call | solution.py:345
  161.7 13.3 %collective-permute-done.36 = f16[128,1024]{1,0:T(8,128)(2,1)S(1)} collective-permute-done((f16[128,1024]{1,0:T(8,128)(2,1)S(1)}, f16[128,1024]{1,0:T(8,128)(2,1)S(1)}, u32[]{:S(2)}, u32[]{:S(2)}) %collective-permute-start.36) | collective-permute-done | bytes 262176 | tf_op jit(solution)/shard_map/ppermute | solution.py:43
  180.4 6.1 %add_products.4 = f32[256,1024]{1,0:T(8,128)S(1)} custom-call(s32[4]{0:T(128)S(1)} %pad_add_fusion.1.refs_0_, bf16[256,1024]{1,0:T(8,128)(2,1)S(1)} %collective-permute-done.refs_1_, bf16[256,1024]{1,0:T(8,128)(2,1)S(1)} %collective-permute-done.3.refs_2_, bf16[256,1024]{1,0:T(8,128)(2,1)S(1)} %collective-permute-done.5.refs_3_, ...), custom_call_target="tpu_custom_call" | custom-call | flops 2147483648 | bytes 10485760 | tf_op jit(solution)/shard_map/add_products/pallas_call | solution.py:345
  187.4 3.3 %unpack_rows.1 = (bf16[512,1024]{1,0:T(8,128)(2,1)}, bf16[512,1024]{1,0:T(8,128)(2,1)}) custom-call(s32[5]{0:T(128)S(1)} %pad_add_fusion.counts, bf16[256,1024]{1,0:T(8,128)(2,1)S(1)} %add_convert_fusion.1.qa, bf16[128,1024]{1,0:T(8,128)(2,1)S(1)} %add_convert_fusion.3.qb, bf16[128,1024]{1,0:T(8,128)(2,1)S(1)} %collective-permute-done.21.qc, ...), custom_call_target="tpu_custom_call" | custom-call | tf_op jit(solution)/shard_map/unpack_rows/pallas_call | solution.py:140
  (140 shorter events, 57.6 us)
Async XLA Ops:
  5.6 45.1 %collective-permute-start.2 = (bf16[256,1024]{1,0:T(8,128)(2,1)S(1)}, bf16[256,1024]{1,0:T(8,128)(2,1)}, u32[]{:S(2)}, u32[]{:S(2)}) collective-permute-start(bf16[256,1024]{1,0:T(8,128)(2,1)S(1)} %get-tuple-element.22.refs_1_.xa), channel_id=1, source_target_pairs={{4,8},{6,10},{8,4},{10,6},{5,9},{7,11},{9,5},{11,7},{20,24},{22,26... | collective-permute-start | bytes 1572872 | tf_op jit(solution)/shard_map/ppermute | solution.py:43
  7.1 44.1 %collective-permute-start.1 = (bf16[256,1024]{1,0:T(8,128)(2,1)S(1)}, bf16[256,1024]{1,0:T(8,128)(2,1)}, u32[]{:S(2)}, u32[]{:S(2)}) collective-permute-start(bf16[256,1024]{1,0:T(8,128)(2,1)S(1)} %get-tuple-element.22.refs_1_.xa), channel_id=1, source_target_pairs={{8,12},{10,14},{4,0},{6,2},{9,13},{11,15},{5,1},{7,3},{24,28},{26,... | collective-permute-start | bytes 1572872 | tf_op jit(solution)/shard_map/ppermute | solution.py:43
  15.3 90.5 %collective-permute-start.11 = (bf16[4,256,1024]{2,1,0:T(8,128)(2,1)S(1)}, bf16[4,256,1024]{2,1,0:T(8,128)(2,1)}, u32[]{:S(2)}, u32[]{:S(2)}) collective-permute-start(bf16[4,256,1024]{2,1,0:T(8,128)(2,1)S(1)} %fetch_blocks.1.own), channel_id=1, source_target_pairs={{0,1},{1,0},{2,3},{3,2},{4,5},{5,4},{6,7},{7,6},{8,9},{9,8},{10,11... | collective-permute-start | bytes 6291464 | tf_op jit(solution)/shard_map/ppermute | solution.py:47
  16.9 36.6 %collective-permute-start.15 = (bf16[128,1024]{1,0:T(8,128)(2,1)S(1)}, bf16[128,1024]{1,0:T(8,128)(2,1)}, u32[]{:S(2)}, u32[]{:S(2)}) collective-permute-start(bf16[128,1024]{1,0:T(8,128)(2,1)S(1)} %add.112.xb), channel_id=1, source_target_pairs={{0,2},{2,0},{4,6},{6,4},{8,10},{10,8},{12,14},{14,12},{1,3},{3,1},... | collective-permute-start | bytes 786440 | tf_op jit(solution)/shard_map/ppermute | solution.py:43
  31.8 20.6 %collective-permute-start.31 = (f16[128,2048]{1,0:T(8,128)(2,1)S(1)}, f16[128,2048]{1,0:T(8,128)(2,1)S(1)}, u32[]{:S(2)}, u32[]{:S(2)}) collective-permute-start(f16[128,2048]{1,0:T(8,128)(2,1)S(1)} %multiply_convert_fusion.4), channel_id=1, source_target_pairs={{0,4},{2,6},{12,8},{14,10},{1,5},{3,7},{13,9},{15,11},{16,20},{18,... | collective-permute-start | bytes 1572872 | tf_op jit(solution)/shard_map/ppermute | solution.py:43
  50.7 13.7 %collective-permute-start.24 = (f16[256,1024]{1,0:T(8,128)(2,1)S(1)}, f16[256,1024]{1,0:T(8,128)(2,1)S(1)}, u32[]{:S(2)}, u32[]{:S(2)}) collective-permute-start(f16[256,1024]{1,0:T(8,128)(2,1)S(1)} %multiply_convert_fusion.11), channel_id=1, source_target_pairs={{0,2},{2,0},{4,6},{6,4},{8,10},{10,8},{12,14},{14,12},{1,3},{3,1},... | collective-permute-start | bytes 1572872 | tf_op jit(solution)/shard_map/ppermute | solution.py:43
  52.3 14.6 %collective-permute-start.4 = (bf16[256,1024]{1,0:T(8,128)(2,1)S(1)}, bf16[256,1024]{1,0:T(8,128)(2,1)S(1)}, u32[]{:S(2)}, u32[]{:S(2)}) collective-permute-start(bf16[256,1024]{1,0:T(8,128)(2,1)S(1)} %get-tuple-element.44), channel_id=1, source_target_pairs={{0,4},{2,6},{4,0},{6,2},{8,12},{10,14},{12,8},{14,10},{1,5},{3,7},... | collective-permute-start | bytes 1572872 | tf_op jit(solution)/shard_map/ppermute | solution.py:43
  52.6 15.6 %collective-permute-start.32 = (f16[128,2048]{1,0:T(8,128)(2,1)S(1)}, f16[128,2048]{1,0:T(8,128)(2,1)S(1)}, u32[]{:S(2)}, u32[]{:S(2)}) collective-permute-start(f16[128,2048]{1,0:T(8,128)(2,1)S(1)} %multiply_convert_fusion.3), channel_id=1, source_target_pairs={{4,8},{6,10},{8,4},{10,6},{5,9},{7,11},{9,5},{11,7},{20,24},{22,26... | collective-permute-start | bytes 1572872 | tf_op jit(solution)/shard_map/ppermute | solution.py:43
  66.9 16.8 %collective-permute-start.16 = (bf16[128,2048]{1,0:T(8,128)(2,1)S(1)}, bf16[128,2048]{1,0:T(8,128)(2,1)S(1)}, u32[]{:S(2)}, u32[]{:S(2)}) collective-permute-start(bf16[128,2048]{1,0:T(8,128)(2,1)S(1)} %pad_maximum_fusion.refs_1_), channel_id=1, source_target_pairs={{8,12},{10,14},{4,0},{6,2},{9,13},{11,15},{5,1},{7,3},{24,28},{26,... | collective-permute-start | bytes 1572872 | tf_op jit(solution)/shard_map/ppermute | solution.py:43
  68.2 17.2 %collective-permute-start.6 = (bf16[256,1024]{1,0:T(8,128)(2,1)S(1)}, bf16[256,1024]{1,0:T(8,128)(2,1)S(1)}, u32[]{:S(2)}, u32[]{:S(2)}) collective-permute-start(bf16[256,1024]{1,0:T(8,128)(2,1)S(1)} %collective-permute-done.4.refs_3_), channel_id=1, source_target_pairs={{4,8},{6,10},{8,4},{10,6},{5,9},{7,11},{9,5},{11,7},{20,24},{22,26... | collective-permute-start | bytes 1572872 | tf_op jit(solution)/shard_map/ppermute | solution.py:43
  76.8 16.1 %collective-permute-start.33 = (f16[128,2048]{1,0:T(8,128)(2,1)S(1)}, f16[128,2048]{1,0:T(8,128)(2,1)S(1)}, u32[]{:S(2)}, u32[]{:S(2)}) collective-permute-start(f16[128,2048]{1,0:T(8,128)(2,1)S(1)} %multiply_convert_fusion.2), channel_id=1, source_target_pairs={{0,4},{2,6},{4,0},{6,2},{8,12},{10,14},{12,8},{14,10},{1,5},{3,7},... | collective-permute-start | bytes 1572872 | tf_op jit(solution)/shard_map/ppermute | solution.py:43
  79.6 14.9 %collective-permute-start.23 = (f16[256,1024]{1,0:T(8,128)(2,1)S(1)}, f16[256,1024]{1,0:T(8,128)(2,1)S(1)}, u32[]{:S(2)}, u32[]{:S(2)}) collective-permute-start(f16[256,1024]{1,0:T(8,128)(2,1)S(1)} %multiply_convert_fusion.12), channel_id=1, source_target_pairs={{0,2},{2,0},{4,6},{6,4},{8,10},{10,8},{12,14},{14,12},{1,3},{3,1},... | collective-permute-start | bytes 1572872 | tf_op jit(solution)/shard_map/ppermute | solution.py:43
  85.5 91.1 %collective-permute-start = (bf16[256,1024]{1,0:T(8,128)(2,1)S(1)}, bf16[256,1024]{1,0:T(8,128)(2,1)S(1)}, u32[]{:S(2)}, u32[]{:S(2)}) collective-permute-start(bf16[256,1024]{1,0:T(8,128)(2,1)S(1)} %get-tuple-element.22.refs_1_.xa), channel_id=1, source_target_pairs={{0,2},{2,0},{4,6},{6,4},{8,10},{10,8},{12,14},{14,12},{1,3},{3,1},... | collective-permute-start | bytes 1572872 | tf_op jit(solution)/shard_map/ppermute | solution.py:43
  92.9 17.9 %collective-permute-start.7 = (bf16[256,1024]{1,0:T(8,128)(2,1)S(1)}, bf16[256,1024]{1,0:T(8,128)(2,1)S(1)}, u32[]{:S(2)}, u32[]{:S(2)}) collective-permute-start(bf16[256,1024]{1,0:T(8,128)(2,1)S(1)} %collective-permute-done.6), channel_id=1, source_target_pairs={{8,12},{10,14},{4,0},{6,2},{9,13},{11,15},{5,1},{7,3},{24,28},{26,... | collective-permute-start | bytes 1572872 | tf_op jit(solution)/shard_map/ppermute | solution.py:43
  94.5 30.5 %collective-permute-start.18 = (bf16[128,2048]{1,0:T(8,128)(2,1)}, bf16[128,2048]{1,0:T(8,128)(2,1)S(1)}, u32[]{:S(2)}, u32[]{:S(2)}) collective-permute-start(bf16[128,2048]{1,0:T(8,128)(2,1)} %get-tuple-element.42), channel_id=1, source_target_pairs={{0,4},{2,6},{4,0},{6,2},{8,12},{10,14},{12,8},{14,10},{1,5},{3,7},... | collective-permute-start | bytes 1572872 | tf_op jit(solution)/shard_map/ppermute | solution.py:43
  97.3 28.4 %collective-permute-start.34 = (f16[128,2048]{1,0:T(8,128)(2,1)S(1)}, f16[128,2048]{1,0:T(8,128)(2,1)S(1)}, u32[]{:S(2)}, u32[]{:S(2)}) collective-permute-start(f16[128,2048]{1,0:T(8,128)(2,1)S(1)} %get-tuple-element.48), channel_id=1, source_target_pairs={{0,4},{2,6},{12,8},{14,10},{1,5},{3,7},{13,9},{15,11},{16,20},{18,... | collective-permute-start | bytes 1572872 | tf_op jit(solution)/shard_map/ppermute | solution.py:43
  105.8 20.8 %collective-permute-start.35 = (f16[128,2048]{1,0:T(8,128)(2,1)S(1)}, f16[128,2048]{1,0:T(8,128)(2,1)}, u32[]{:S(2)}, u32[]{:S(2)}) collective-permute-start(f16[128,2048]{1,0:T(8,128)(2,1)S(1)} %get-tuple-element.49), channel_id=1, source_target_pairs={{4,8},{6,10},{8,4},{10,6},{5,9},{7,11},{9,5},{11,7},{20,24},{22,26... | collective-permute-start | bytes 1572872 | tf_op jit(solution)/shard_map/ppermute | solution.py:43
  123.4 14.9 %collective-permute-start.28 = (f16[256,1024]{1,0:T(8,128)(2,1)S(1)}, f16[256,1024]{1,0:T(8,128)(2,1)S(1)}, u32[]{:S(2)}, u32[]{:S(2)}) collective-permute-start(f16[256,1024]{1,0:T(8,128)(2,1)S(1)} %multiply_convert_fusion.7), channel_id=1, source_target_pairs={{0,2},{2,0},{4,6},{6,4},{8,10},{10,8},{12,14},{14,12},{1,3},{3,1},... | collective-permute-start | bytes 1572872 | tf_op jit(solution)/shard_map/ppermute | solution.py:43
  125.1 54.0 %collective-permute-start.3 = (bf16[256,1024]{1,0:T(8,128)(2,1)S(1)}, bf16[256,1024]{1,0:T(8,128)(2,1)S(1)}, u32[]{:S(2)}, u32[]{:S(2)}) collective-permute-start(bf16[256,1024]{1,0:T(8,128)(2,1)S(1)} %get-tuple-element.45.refs_2_), channel_id=1, source_target_pairs={{0,2},{2,0},{4,6},{6,4},{8,10},{10,8},{12,14},{14,12},{1,3},{3,1},... | collective-permute-start | bytes 1572872 | tf_op jit(solution)/shard_map/ppermute | solution.py:43
  125.7 14.2 %collective-permute-start.19 = (bf16[128,2048]{1,0:T(8,128)(2,1)S(1)}, bf16[128,2048]{1,0:T(8,128)(2,1)S(1)}, u32[]{:S(2)}, u32[]{:S(2)}) collective-permute-start(bf16[128,2048]{1,0:T(8,128)(2,1)S(1)} %collective-permute-done.18.refs_3_), channel_id=1, source_target_pairs={{4,8},{6,10},{8,4},{10,6},{5,9},{7,11},{9,5},{11,7},{20,24},{22,26... | collective-permute-start | bytes 1572872 | tf_op jit(solution)/shard_map/ppermute | solution.py:43
  126.5 14.8 %collective-permute-start.27 = (f16[256,1024]{1,0:T(8,128)(2,1)S(1)}, f16[256,1024]{1,0:T(8,128)(2,1)S(1)}, u32[]{:S(2)}, u32[]{:S(2)}) collective-permute-start(f16[256,1024]{1,0:T(8,128)(2,1)S(1)} %multiply_convert_fusion.8), channel_id=1, source_target_pairs={{0,4},{2,6},{4,0},{6,2},{8,12},{10,14},{12,8},{14,10},{1,5},{3,7},... | collective-permute-start | bytes 1572872 | tf_op jit(solution)/shard_map/ppermute | solution.py:43
  138.4 41.5 %collective-permute-start.5 = (bf16[256,1024]{1,0:T(8,128)(2,1)S(1)}, bf16[256,1024]{1,0:T(8,128)(2,1)S(1)}, u32[]{:S(2)}, u32[]{:S(2)}) collective-permute-start(bf16[256,1024]{1,0:T(8,128)(2,1)S(1)} %collective-permute-done.4.refs_3_), channel_id=1, source_target_pairs={{0,2},{2,0},{4,6},{6,4},{8,10},{10,8},{12,14},{14,12},{1,3},{3,1},... | collective-permute-start | bytes 1572872 | tf_op jit(solution)/shard_map/ppermute | solution.py:43
  147.0 32.9 %collective-permute-start.8 = (bf16[256,1024]{1,0:T(8,128)(2,1)S(1)}, bf16[256,1024]{1,0:T(8,128)(2,1)S(1)}, u32[]{:S(2)}, u32[]{:S(2)}) collective-permute-start(bf16[256,1024]{1,0:T(8,128)(2,1)S(1)} %broadcast_select_fusion.3.refs_4_), channel_id=1, source_target_pairs={{0,2},{2,0},{4,6},{6,4},{8,10},{10,8},{12,14},{14,12},{1,3},{3,1},... | collective-permute-start | bytes 1572872 | tf_op jit(solution)/shard_map/ppermute | solution.py:43
  152.6 22.3 %collective-permute-start.36 = (f16[128,1024]{1,0:T(8,128)(2,1)S(1)}, f16[128,1024]{1,0:T(8,128)(2,1)S(1)}, u32[]{:S(2)}, u32[]{:S(2)}) collective-permute-start(f16[128,1024]{1,0:T(8,128)(2,1)S(1)} %multiply_convert_fusion.14), channel_id=1, source_target_pairs={{0,2},{2,0},{4,6},{6,4},{8,10},{10,8},{12,14},{14,12},{1,3},{3,1},... | collective-permute-start | bytes 786440 | tf_op jit(solution)/shard_map/ppermute | solution.py:43
  (31 other events, 320.6 us)

commit v3 on v0

v3 whole, which is shorter than its diff:
```python
import functools

import jax
import jax.numpy as jnp
from jax import lax
from jax.experimental import pallas as pl
from jax.experimental.pallas import tpu as pltpu
from jax.sharding import PartitionSpec as P

REQUEST_LENGTH = 256


adapter_scale = 0.5

SUM_SCALE = 8.0
DOWN_SCALE = 16.0

BF16 = jnp.bfloat16
F16 = jnp.float16
F32 = jnp.float32
I32 = jnp.int32

SMALL = 16 * 1024 * 1024
LARGE = 48 * 1024 * 1024


def ring_order(size):
    if size == 8:
        return [0, 2, 4, 6, 7, 5, 3, 1]
    return list(range(size))


def send(value, pairs, name):
    with jax.named_scope(name):
        return lax.ppermute(value, "tensor", pairs)


def other_replica(value):
    return lax.ppermute(value, "replica", [(0, 1), (1, 0)])


def dot(a, b):
    return jnp.dot(a, b, preferred_element_type=F32)


def dot_t(a, b):
    return lax.dot_general(a, b, (((1,), (1,)), ((), ())), preferred_element_type=F32)


def look_up(index, table):
    out = I32(table[0])
    for i, entry in enumerate(table[1:], 1):
        out = jnp.where(index == i, I32(entry), out)
    return out


def whole(shape):
    return pl.BlockSpec(shape, lambda *_: (0,) * len(shape))


def params(limit=SMALL):
    return pltpu.CompilerParams(dimension_semantics=("arbitrary",), vmem_limit_bytes=limit)


def iota(shape, dim):
    return lax.broadcasted_iota(I32, shape, dim)


def lengths(counts, place):
    mine, theirs = 2 * place[0], 2 - 2 * place[0]
    return counts[mine], counts[mine + 1], counts[theirs], counts[theirs + 1]


def select_rows(home, x):
    hot = iota((home.shape[0], x.shape[0]), 1) == home
    return dot(hot.astype(F32).astype(BF16), x[...])


def home_of(position, live, c_a):
    home = jnp.where(position < c_a, position, REQUEST_LENGTH + position - c_a)
    return jnp.where(live, home, -1)


def spare_kernel(counts, place, x_ref, v_ref, out):
    rows, spare = x_ref.shape[0], out.shape[0] // 2
    packed = rows - spare
    c_a, c_b, d_a, d_b = lengths(counts, place)
    seat = iota((spare, 1), 0) + packed - spare - d_a - d_b
    home = home_of(packed + seat, seat >= 0, c_a)
    out[:spare] = select_rows(home, x_ref).astype(BF16)
    out[spare:] = select_rows(home, v_ref).astype(BF16)


def spare_rows(counts, place, x, v, spare):
    shape = (2 * spare, x.shape[1])
    return pl.pallas_call(
        spare_kernel,
        grid_spec=pltpu.PrefetchScalarGridSpec(
            num_scalar_prefetch=2,
            grid=(1,),
            in_specs=[whole(x.shape)] * 2,
            out_specs=whole(shape),
        ),
        out_shape=jax.ShapeDtypeStruct(shape, BF16),
        compiler_params=params(),
        name="spare_rows",
    )(counts, place, x, v)


def pack_kernel(counts, place, x_ref, moved_ref, out):
    packed, spare = out.shape[0], moved_ref.shape[0]
    first = packed - spare
    c_a, c_b, _, _ = lengths(counts, place)
    slot = iota((packed, 1), 0)
    here = select_rows(home_of(slot, slot < c_a + c_b, c_a), x_ref)
    out[:first] = here[:first].astype(BF16)
    out[first:] = (here[first:] + moved_ref[...].astype(F32)).astype(BF16)


def pack(counts, place, x, moved, which):
    rows, width = x.shape
    spare = moved.shape[0] // 2
    shape = (rows - spare, width)
    return pl.pallas_call(
        pack_kernel,
        grid_spec=pltpu.PrefetchScalarGridSpec(
            num_scalar_prefetch=2,
            grid=(1,),
            in_specs=[whole(x.shape), pl.BlockSpec((spare, width), lambda *_: (which, 0))],
            out_specs=whole(shape),
        ),
        out_shape=jax.ShapeDtypeStruct(shape, BF16),
        compiler_params=params(),
        name="pack_rows",
    )(counts, place, x, moved)


def unpack_kernel(counts, place, x_ref, spare_ref, out):
    rows = out.shape[0]
    packed, spare = x_ref.shape[0], spare_ref.shape[0]
    first = packed - spare
    c_a, c_b, d_a, d_b = lengths(counts, place)
    n_theirs = d_a + d_b
    row = iota((rows, 1), 0)
    late = row >= REQUEST_LENGTH
    offset = jnp.where(late, row - REQUEST_LENGTH, row)
    position = offset + jnp.where(late, c_a, 0)
    target = jnp.where(position < packed, position, position + n_theirs - first)
    target = jnp.where(offset < jnp.where(late, c_b, c_a), target, -1)
    hot = (iota((rows, rows), 1) == target).astype(F32).astype(BF16)
    out[...] = (dot(hot[:, :packed], x_ref[...]) + dot(hot[:, packed:], spare_ref[...])).astype(BF16)


def unpack(counts, place, rows, parts):
    shape = (rows, parts[0].shape[1])
    return pl.pallas_call(
        unpack_kernel,
        grid_spec=pltpu.PrefetchScalarGridSpec(
            num_scalar_prefetch=2,
            grid=(1,),
            in_specs=[whole(p.shape) for p in parts],
            out_specs=whole(shape),
        ),
        out_shape=jax.ShapeDtypeStruct(shape, BF16),
        compiler_params=params(),
        name="unpack_rows",
    )(counts, place, *parts)


def request_of(counts, place, slot, packed):
    c_a, c_b, d_a, _ = lengths(counts, place)
    n_mine, replica = c_a + c_b, place[0]
    own = slot < n_mine
    seat = jnp.where(own, slot, packed + slot - n_mine)
    mine = 2 * replica + (seat >= c_a).astype(I32)
    theirs = 2 * (1 - replica) + (seat >= d_a).astype(I32)
    return jnp.where(own, mine, theirs)


def fetch_kernel(held, adapter_of, location, place, *refs):
    stores, out = refs[:4], refs[4]
    slot = location[adapter_of[pl.program_id(0)]] - place[0] * held
    mine = (slot >= 0) & (slot < held)
    for k, table in enumerate(stores):
        block = table[0]
        out[k] = jnp.where(mine, block, jnp.zeros_like(block))


def fetch(stores, adapter_of, location, place):
    held, rank, width = stores[0].shape
    requests = adapter_of.shape[0]

    def at(i, adapter_of, location, place):
        slot = location[adapter_of[i]] - place[0] * held
        return jnp.clip(slot, 0, held - 1), 0, 0

    return pl.pallas_call(
        functools.partial(fetch_kernel, held),
        grid_spec=pltpu.PrefetchScalarGridSpec(
            num_scalar_prefetch=3,
            grid=(requests,),
            in_specs=[pl.BlockSpec((1, rank, width), at)] * 4,
            out_specs=pl.BlockSpec((4, rank, width), lambda i, *_: (0, i, 0)),
        ),
        out_shape=jax.ShapeDtypeStruct((4, requests * rank, width), BF16),
        compiler_params=params(LARGE),
        name="fetch_blocks",
    )(adapter_of, location, place, *stores)


def down_kernel(counts, place, x, v, own, other, out, blocks):
    rank = out.shape[1] // 2
    packed, width = x.shape
    requests = own.shape[1] // rank
    blocks[...] = jnp.zeros_like(blocks)
    who = request_of(counts, place, iota((packed, 1), 0), packed)
    total = jnp.zeros(out.shape, F32)
    for i in range(requests):
        rows = pl.ds(i * rank, rank)
        blocks[:rank, :width] = own[0, rows] + other[0, rows]
        blocks[rank:, width:] = own[1, rows] + other[1, rows]
        got = dot_t(x[...], blocks[:, :width]) + dot_t(v[...], blocks[:, width:])
        total = total + jnp.where(who == i, got, 0.0)
    out[...] = total


def down(counts, place, x, v, own, other):
    requests_rank, width = own.shape[1:]
    rank = requests_rank // 4
    packed = x.shape[0]
    half = (2, requests_rank, width)
    return pl.pallas_call(
        down_kernel,
        grid_spec=pltpu.PrefetchScalarGridSpec(
            num_scalar_prefetch=2,
            grid=(1,),
            in_specs=[whole(v.shape) for v in (x, v)] + [whole(half)] * 2,
            out_specs=whole((packed, 2 * rank)),
            scratch_shapes=[pltpu.VMEM((2 * rank, 2 * width), BF16)],
        ),
        out_shape=jax.ShapeDtypeStruct((packed, 2 * rank), F32),
        compiler_params=params(),
        name="down_rows",
    )(counts, place, x, v, own, other)


def up_kernel(counts, place, low, own, other, q_ref, o_ref, blocks):
    packed, both = low.shape
    rank = both // 2
    width = q_ref.shape[1]
    requests = own.shape[1] // rank
    blocks[...] = jnp.zeros_like(blocks)
    who = request_of(counts, place, iota((packed, 1), 0), packed)
    rows_low = low[...].astype(BF16).astype(F32)
    for i in range(requests):
        rows = pl.ds(i * rank, rank)
        blocks[pl.ds(2 * i * rank, rank), :width] = own[0, rows] + other[0, rows]
        blocks[pl.ds((2 * i + 1) * rank, rank), width:] = own[1, rows] + other[1, rows]
    wide = jnp.concatenate(
        [jnp.where(who == i, rows_low, 0.0).astype(BF16) for i in range(requests)], axis=1
    )
    q_ref[...] = adapter_scale * dot(wide, blocks[:, :width])
    o_ref[...] = adapter_scale * dot(wide, blocks[:, width:])


def up(counts, place, low, own, other):
    packed, both = low.shape
    requests_rank, width = own.shape[1:]
    half = (2, requests_rank, width)
    return pl.pallas_call(
        up_kernel,
        grid_spec=pltpu.PrefetchScalarGridSpec(
            num_scalar_prefetch=2,
            grid=(1,),
            in_specs=[whole(low.shape)]
            + [pl.BlockSpec(half, lambda *_: (1, 0, 0))] * 2,
            out_specs=[whole((packed, width))] * 2,
            scratch_shapes=[pltpu.VMEM((2 * requests_rank, 2 * width), BF16)],
        ),
        out_shape=[jax.ShapeDtypeStruct((packed, width), F32)] * 2,
        compiler_params=params(),
        name="up_rows",
    )(counts, place, low, own, other)


def shares_kernel(where, x_ref, w_ref, out):
    out[0] = dot(x_ref[...], w_ref[...])


def shares(where, start, count, x, weight):
    rows, width = x.shape
    return pl.pallas_call(
        shares_kernel,
        grid_spec=pltpu.PrefetchScalarGridSpec(
            num_scalar_prefetch=1,
            grid=(count,),
            in_specs=[
                whole(x.shape),
                pl.BlockSpec((width, width), lambda i, where: (0, where[start + i])),
            ],
            out_specs=pl.BlockSpec((1, rows, width), lambda i, where: (i, 0, 0)),
        ),
        out_shape=jax.ShapeDtypeStruct((count, rows, width), F32),
        compiler_params=params(LARGE),
        name="shares",
    )(where, x, weight)


def add_kernel(pieces, where, *refs):
    xs, ws, extra, out = refs[:pieces], refs[pieces : 2 * pieces], refs[2 * pieces : -1], refs[-1]
    total = dot(xs[0][...], ws[0][...])
    for x, w in zip(xs[1:], ws[1:]):
        total = total + dot(x[...], w[...])
    for more in extra:
        total = total + more[...]
    out[...] = total.astype(out.dtype)


def add_products(where, pieces, at, weight, addends, dtype=F32):
    rows, width = pieces[0].shape
    columns = weight.shape[1]
    step = columns // 2

    def rows_of(i):
        return pl.BlockSpec((width, step), lambda j, where: (where[at[i]], j))

    tall = pl.BlockSpec((rows, step), lambda j, where: (0, j))
    return pl.pallas_call(
        functools.partial(add_kernel, len(pieces)),
        grid_spec=pltpu.PrefetchScalarGridSpec(
            num_scalar_prefetch=1,
            grid=(2,),
            in_specs=[whole(p.shape) for p in pieces]
            + [rows_of(i) for i in range(len(pieces))]
            + [tall] * len(addends),
            out_specs=tall,
        ),
        out_shape=jax.ShapeDtypeStruct((rows, columns), dtype),
        compiler_params=params(LARGE),
        name="add_products",
    )(where, *pieces, *([weight] * len(pieces)), *addends)


def narrow(value):
    return (value * SUM_SCALE).astype(F16)


def widen(value):
    return value.astype(F32) * (1.0 / SUM_SCALE)


def tie(value, *others):
    return lax.optimization_barrier((value, others))[0]


def swap_down(total, bit, size):
    mine = (total * DOWN_SCALE).astype(F16)
    moved = send(mine, [(t, t ^ bit) for t in range(size)], "down_swap")
    return (mine.astype(F32) + moved.astype(F32)) * (1.0 / DOWN_SCALE)


def make(mesh):
    size = mesh.shape["tensor"]
    order = ring_order(size)
    steps = size // 2
    following = [(order[p], order[(p + 1) % size]) for p in range(size)]
    preceding = [(b, a) for a, b in following]
    offsets = [0] + [sign * d for d in range(1, steps) for sign in (1, -1)] + [steps]
    place_of = [order.index(t) for t in range(size)]

    def local(
        tokens, context, query_weight, output_weight,
        store_aq, store_bq, store_ao, store_bo,
        adapter_of, location, token_count,
    ):
        rows, width = tokens.shape
        packed = rows * 3 // 4
        spare = rows - packed
        half = packed // 2
        at = lax.axis_index("tensor")
        place = jnp.stack([lax.axis_index("replica")]).astype(I32)
        counts = token_count
        where = jnp.stack(
            [look_up(at, [order[(p + d) % size] for p in place_of]) for d in offsets]
        )

        moved = other_replica(spare_rows(counts, place, tokens, context, spare))
        mine = fetch((store_aq, store_ao, store_bq, store_bo), adapter_of, location, place)
        tok = pack(counts, place, tokens, tie(moved, mine), 0)
        ahead, behind = send(tok, following, "gather_up_1"), send(tok, preceding, "gather_down_1")
        ctx = pack(counts, place, tie(context, tok), moved, 1)
        far = narrow(shares(where, size - 1, 1, ctx, output_weight)[0])
        up_sum = send(far[:half], following, "scatter_up_1")
        down_sum = send(far[half:], preceding, "scatter_down_1")
        theirs = other_replica(mine)
        near = list(shares(where, size - 3, 2, tie(ctx, far), output_weight))

        q, bit = None, 1
        for step in range(1, steps):
            up_sum, down_sum = lax.optimization_barrier((tie(up_sum, near), down_sum))
            up_share, down_share = near[0], near[1]
            if step == 1:
                up_out = jnp.concatenate([up_share[:half] + widen(up_sum), up_share[half:]])
                down_out = jnp.concatenate([down_share[:half], down_share[half:] + widen(down_sum)])
            else:
                up_out, down_out = up_share + widen(up_sum), down_share + widen(down_sum)
            up_out, down_out = narrow(up_out), narrow(down_out)
            up_sum = send(up_out, following, f"scatter_up_{step + 1}")
            down_sum = send(down_out, preceding, f"scatter_down_{step + 1}")
            got_up, got_down = lax.optimization_barrier((tie(ahead, up_out, down_out), behind))
            if step < steps - 1:
                ahead = send(got_up, following, f"gather_up_{step + 1}")
                behind = send(got_down, preceding, f"gather_down_{step + 1}")
            else:
                ahead = send(got_up[:half], following, f"gather_up_{step + 1}")
                behind = send(got_down[half:], preceding, f"gather_down_{step + 1}")
            ready = got_up
            if step == 1:
                theirs = tie(theirs, up_out)
                parts = down(counts, place, tok, ctx, tie(mine, ready), theirs)
                ready = parts
            if bit < size:
                parts = swap_down(tie(parts, ready), bit, size)
                bit *= 2
            if step == 1:
                rest = shares(where, 0, size - 3, tie(ctx, ready), output_weight)
                ready = rest
                pieces, at_pieces, sofar = [tok, got_down, got_up], [0, 1, 2], []
            else:
                pieces, at_pieces, sofar = [got_down, got_up], [2 * step - 1, 2 * step], [q]
            pieces[0] = tie(pieces[0], ready)
            q = add_products(where, pieces, at_pieces, query_weight, sofar)
            d = steps - step - 1
            near = [tie(rest[2 * d - 1], q), rest[2 * d]]
        while bit < size:
            parts = swap_down(tie(parts, q), bit, size)
            bit *= 2
        up_q, up_o = up(counts, place, tie(parts, q), mine, theirs)
        got_up, got_down = lax.optimization_barrier((tie(ahead, up_q), behind))
        last = jnp.concatenate([got_up, got_down])
        q = add_products(where, [last], [size - 1], query_weight, [q, up_q], BF16)
        q_m = other_replica(q[packed - spare :])
        up_sum, down_sum = lax.optimization_barrier((tie(up_sum, q), down_sum))
        o = (rest[0] + widen(up_sum) + widen(down_sum) + up_o).astype(BF16)
        o_m = other_replica(o[packed - spare :])
        queries = unpack(counts, place, rows, (q, tie(q_m, o)))
        attended = unpack(counts, place, rows, (o, tie(o_m, queries)))
        return queries, attended

    return local


def solution(mesh):
    return jax.shard_map(
        make(mesh),
        mesh=mesh,
        in_specs=(
            P(("groups", "replica"), "tensor"),
            P(("groups", "replica"), "tensor"),
            P(None, "tensor"),
            P("tensor", None),
            P(("groups", "replica"), None, "tensor"),
            P(("groups", "replica"), None, "tensor"),
            P(("groups", "replica"), None, "tensor"),
            P(("groups", "replica"), None, "tensor"),
            P("groups"),
            P("groups"),
            P("groups"),
        ),
        out_specs=(P(("groups", "replica"), "tensor"), P(("groups", "replica"), "tensor")),
        check_vma=False,
    )
```

time: 502 us -> 159 us (0.32)
  waiting for transfers between devices: 394 us -> 65.7 us
  Pallas kernels: 0 us -> 56.2 us
  blocking collectives: 44.7 us -> 0 us
  matrix products: 34 us -> 0 us
  starting transfers between devices: 0.23 us -> 21.1 us
  between operations: 14.2 us -> 1.18 us
  local copies, waits for them, and re-layouts: 14.3 us -> 5.89 us
  other arithmetic: 0.25 us -> 7.13 us
    reduce_scatter x1 -> x0, waiting for transfers between devices: 269 us -> none  [local(): lax.psum_scatter(lax.dot_general(output_weight, context, (((0,), (1,)), (...]
    all_gather x5 -> x0, waiting for transfers between devices: 122 us -> none  [the longest x1 84.5 us: local(): lax.all_gather(tokens, 'tensor', axis=1, tiled=True)]
    ppermute x0 -> x23, waiting for transfers between devices: none -> 65.7 us  [the longest x19 65.7 us: send(): return lax.ppermute(value, 'tensor', pairs)]
    pallas_call x0 -> x15, Pallas kernels: none -> 56.2 us  [the longest x3 18.9 us: shares(): pl.pallas_call(shares_kernel, grid_spec=pltpu.PrefetchScalarGridSpec(num_...]
    psum x1 -> x0, blocking collectives: 44.7 us -> none  [local(): low_q, low_o = lax.psum((part_q, part_o), 'tensor')]
    dot_general x6 -> x0, matrix products: 34 us -> none  [the longest x1 15.8 us: local(): lax.dot_general(output_weight, context, (((0,), (1,)), ((), ())), preferr...]
    ppermute x0 -> x23, starting transfers between devices: none -> 21.1 us  [the longest x19 20 us: send(): return lax.ppermute(value, 'tensor', pairs)]
    gather x5 -> x0, local copies, waits for them, and re-layouts: 11.6 us -> none  [the longest x4 11 us: local(): fetched = [jnp.take(table, my_slots, axis=0) for table in everything]]
  transfers between devices with their start and end apart: 6 -> 23, of which waited for: 5 -> 9; matrix products, arithmetic and copies ran while one was open for 9% -> 6% of each run, Pallas kernels for 0% -> 33%
where the time goes in v3:
time: 159 us; the launch traced here: 157 us
  waiting for transfers between devices  65.7 us (41%)
  Pallas kernels  56.2 us (35%)
  starting transfers between devices  21.1 us (13%)
  other arithmetic  7.13 us (4%)
  local copies, waits for them, and re-layouts  5.89 us (4%)
    ppermute x19, waiting for transfers between devices, send(): return lax.ppermute(value, 'tensor', pairs)  65.7 us
    ppermute x19, starting transfers between devices, send(): return lax.ppermute(value, 'tensor', pairs)  20 us
    pallas_call x3, Pallas kernels, shares(): pl.pallas_call(shares_kernel, grid_spec=pltpu.PrefetchScalarGridSpec(num_...  18.9 us
    pallas_call x4, Pallas kernels, add_products(): pl.pallas_call(functools.partial(add_kernel, len(pieces)), grid_spec=pltp...  17 us
    pallas_call x2, Pallas kernels, unpack(): pl.pallas_call(unpack_kernel, grid_spec=pltpu.PrefetchScalarGridSpec(num_...  4.95 us
    convert_element_type x7, other arithmetic, narrow(): return (value * SUM_SCALE).astype(F16)  4.55 us
    pallas_call x2, Pallas kernels, pack(): pl.pallas_call(pack_kernel, grid_spec=pltpu.PrefetchScalarGridSpec(num_sc...  4.15 us
    pallas_call x1, Pallas kernels, down(): pl.pallas_call(down_kernel, grid_spec=pltpu.PrefetchScalarGridSpec(num_sc...  3.57 us
  transfers between devices with their start and end apart: 23, of which 9 were waited for; matrix products, arithmetic and copies ran while one was open for 6% of the time, Pallas kernels for 33%

profile of v3, /device:TPU:0, one launch (start us, length us, event | category | flops | bytes accessed | tf_op | source)
XLA Modules:
  0.0 157.2 jit_solution(862196448396963328)
XLA Ops:
  6.0 3.1 %fetch_blocks.1.own = bf16[4,256,1024]{2,1,0:T(8,128)(2,1)S(1)} custom-call(s32[4]{0:T(128)S(1)} %copy-done.7, s32[32]{0:T(128)S(1)} %copy-done.8, s32[1]{0:T(128)} %bitcast.place, bf16[16,64,1024]{2,1,0:T(8,128)(2,1)S(1)} %copy-done.4, bf16[16,64,1024]{2,1,0:T(8,128)(2,1)} %refs_1_.2, bf16[16,64,1024]{2,1,0:T(8,128)(2,1)} %refs_2_.3, ...), custom_call_target="tpu_custom_call" | custom-call | tf_op jit(solution)/shard_map/fetch_blocks/pallas_call | solution.py:197
  13.7 3.1 %shares.4 = f32[1,384,1024]{2,1,0:T(8,128)S(1)} custom-call(s32[8]{0:T(128)S(1)} %stack.39.where, bf16[384,1024]{1,0:T(8,128)(2,1)S(1)} %pack_rows.3.x_ref.v, bf16[1024,8192]{1,0:T(8,128)(2,1)} %w_ref.5), custom_call_target="tpu_custom_call" | custom-call | tf_op jit(solution)/shard_map/shares/pallas_call | solution.py:292
  17.1 2.7 %collective-permute-start.2 = (f16[192,1024]{1,0:T(8,128)(2,1)S(1)}, f16[192,1024]{1,0:T(8,128)(2,1)S(1)}, u32[]{:S(2)}, u32[]{:S(2)}) collective-permute-start(f16[192,1024]{1,0:T(8,128)(2,1)S(1)} %get-tuple-element.91), channel_id=1, source_target_pairs={{0,4},{4,8},{8,12},{12,14},{14,10},{10,6},{6,2},{2,0},{1,5},{5,9},... | collective-permute-start | bytes 1179656 | tf_op jit(solution)/shard_map/scatter_up_1/ppermute | solution.py:35
  21.8 4.2 %shares.3 = f32[2,384,1024]{2,1,0:T(8,128)S(1)} custom-call(s32[8]{0:T(128)S(1)} %stack.39.where, bf16[384,1024]{1,0:T(8,128)(2,1)S(1)} %pack_rows.3.x_ref.v, bf16[1024,8192]{1,0:T(8,128)(2,1)} %w_ref.5), custom_call_target="tpu_custom_call" | custom-call | tf_op jit(solution)/shard_map/shares/pallas_call | solution.py:292
  26.2 3.5 %collective-permute-done.2 = f16[192,1024]{1,0:T(8,128)(2,1)S(1)} collective-permute-done((f16[192,1024]{1,0:T(8,128)(2,1)S(1)}, f16[192,1024]{1,0:T(8,128)(2,1)S(1)}, u32[]{:S(2)}, u32[]{:S(2)}) %collective-permute-start.2) | collective-permute-done | bytes 393248 | tf_op jit(solution)/shard_map/scatter_up_1/ppermute | solution.py:35
  29.7 2.1 %collective-permute-done.3 = f16[192,1024]{1,0:T(8,128)(2,1)S(1)} collective-permute-done((f16[192,1024]{1,0:T(8,128)(2,1)S(1)}, f16[192,1024]{1,0:T(8,128)(2,1)S(1)}, u32[]{:S(2)}, u32[]{:S(2)}) %collective-permute-start.3) | collective-permute-done | bytes 393248 | tf_op jit(solution)/shard_map/scatter_down_1/ppermute | solution.py:35
  34.5 12.0 %collective-permute-done.1.refs_2_ = bf16[384,1024]{1,0:T(8,128)(2,1)S(1)} collective-permute-done((bf16[384,1024]{1,0:T(8,128)(2,1)S(1)}, bf16[384,1024]{1,0:T(8,128)(2,1)S(1)}, u32[]{:S(2)}, u32[]{:S(2)}) %collective-permute-start.1) | collective-permute-done | bytes 786464 | tf_op jit(solution)/shard_map/gather_up_1/ppermute | solution.py:35
  46.5 2.1 %collective-permute-done.4.refs_1_ = bf16[384,1024]{1,0:T(8,128)(2,1)S(1)} collective-permute-done((bf16[384,1024]{1,0:T(8,128)(2,1)S(1)}, bf16[384,1024]{1,0:T(8,128)(2,1)S(1)}, u32[]{:S(2)}, u32[]{:S(2)}) %collective-permute-start.4) | collective-permute-done | bytes 786464 | tf_op jit(solution)/shard_map/gather_down_1/ppermute | solution.py:35
  50.6 3.6 %down_rows.1 = f32[384,128]{1,0:T(8,128)S(1)} custom-call(s32[4]{0:T(128)S(1)} %copy-done.6, s32[1]{0:T(128)} %bitcast.place, bf16[384,1024]{1,0:T(8,128)(2,1)S(1)} %pack_rows.2.x.refs_0_, bf16[384,1024]{1,0:T(8,128)(2,1)S(1)} %pack_rows.3.x_ref.v, bf16[4,256,1024]{2,1,0:T(8,128)(2,1)S(1)} %fetch_blocks.1.own, bf16[4,256,1024]{2,1,0:T(8,128)(2,1)} %collective-permute-done.6.other), custom_call_target="tpu_custom_call" | custom-call | tf_op jit(solution)/shard_map/down_rows/pallas_call | solution.py:232
  54.2 11.6 %shares.5 = f32[5,384,1024]{2,1,0:T(8,128)} custom-call(s32[8]{0:T(128)S(1)} %stack.39.where, bf16[384,1024]{1,0:T(8,128)(2,1)S(1)} %pack_rows.3.x_ref.v, bf16[1024,8192]{1,0:T(8,128)(2,1)} %w_ref.5), custom_call_target="tpu_custom_call" | custom-call | tf_op jit(solution)/shard_map/shares/pallas_call | solution.py:292
  65.8 5.4 %add_products.4.refs_4_ = f32[384,1024]{1,0:T(8,128)S(1)} custom-call(s32[8]{0:T(128)S(1)} %stack.39.where, bf16[384,1024]{1,0:T(8,128)(2,1)S(1)} %pack_rows.2.x.refs_0_, bf16[384,1024]{1,0:T(8,128)(2,1)S(1)} %collective-permute-done.4.refs_1_, bf16[384,1024]{1,0:T(8,128)(2,1)S(1)} %collective-permute-done.1.refs_2_, bf16[8192,1024]{1,0:T(8,128)(2,1)} %refs_1_.3, ...), custom_call_target="tpu_custom_call" | custom-call | tf_op jit(solution)/shard_map/add_products/pallas_call | solution.py:328
  71.2 2.3 %slice_bitcast_fusion.2 = (f32[384,1024]{1,0:T(8,128)S(1)}, f32[384,1024]{1,0:T(8,128)S(1)}) fusion(f32[5,384,1024]{2,1,0:T(8,128)} %shares.5), kind=kLoop, calls=%fused_computation.6 | loop fusion | bytes 6291456 | tf_op jit(solution)/shard_map/squeeze | solution.py:434
  77.8 2.4 %collective-permute-done.5.refs_1_ = bf16[384,1024]{1,0:T(8,128)(2,1)S(1)} collective-permute-done((bf16[384,1024]{1,0:T(8,128)(2,1)S(1)}, bf16[384,1024]{1,0:T(8,128)(2,1)S(1)}, u32[]{:S(2)}, u32[]{:S(2)}) %collective-permute-start.5) | collective-permute-done | bytes 786464 | tf_op jit(solution)/shard_map/gather_up_2/ppermute | solution.py:35
  84.3 4.3 %add_products.5.refs_4_ = f32[384,1024]{1,0:T(8,128)S(1)} custom-call(s32[8]{0:T(128)S(1)} %stack.39.where, bf16[384,1024]{1,0:T(8,128)(2,1)S(1)} %collective-permute-done.9.refs_0_, bf16[384,1024]{1,0:T(8,128)(2,1)S(1)} %collective-permute-done.5.refs_1_, bf16[8192,1024]{1,0:T(8,128)(2,1)} %refs_1_.3, bf16[8192,1024]{1,0:T(8,128)(2,1)} %refs_1_.3, ...), custom_call_target="tpu_custom_call" | custom-call | tf_op jit(solution)/shard_map/add_products/pallas_call | solution.py:328
  88.6 10.6 %collective-permute-done.15 = f16[384,128]{1,0:T(8,128)(2,1)S(1)} collective-permute-done((f16[384,128]{1,0:T(8,128)(2,1)S(1)}, f16[384,128]{1,0:T(8,128)(2,1)S(1)}, u32[]{:S(2)}, u32[]{:S(2)}) %collective-permute-start.15) | collective-permute-done | bytes 98336 | tf_op jit(solution)/shard_map/down_swap/ppermute | solution.py:35
  101.4 2.1 %collective-permute-start.21 = (f16[384,1024]{1,0:T(8,128)(2,1)S(1)}, f16[384,1024]{1,0:T(8,128)(2,1)S(1)}, u32[]{:S(2)}, u32[]{:S(2)}) collective-permute-start(f16[384,1024]{1,0:T(8,128)(2,1)S(1)} %multiply_convert_fusion), channel_id=1, source_target_pairs={{4,0},{8,4},{12,8},{14,12},{10,14},{6,10},{2,6},{0,2},{5,1},{9,5},... | collective-permute-start | bytes 2359304 | tf_op jit(solution)/shard_map/scatter_down_4/ppermute | solution.py:35
  103.5 14.6 %collective-permute-done.16 = f16[384,128]{1,0:T(8,128)(2,1)S(1)} collective-permute-done((f16[384,128]{1,0:T(8,128)(2,1)S(1)}, f16[384,128]{1,0:T(8,128)(2,1)S(1)}, u32[]{:S(2)}, u32[]{:S(2)}) %collective-permute-start.16) | collective-permute-done | bytes 98336 | tf_op jit(solution)/shard_map/down_swap/ppermute | solution.py:35
  120.3 2.6 %collective-permute-start.17 = (f16[384,128]{1,0:T(8,128)(2,1)S(1)}, f16[384,128]{1,0:T(8,128)(2,1)S(1)}, u32[]{:S(2)}, u32[]{:S(2)}) collective-permute-start(f16[384,128]{1,0:T(8,128)(2,1)S(1)} %multiply_convert_fusion.5), channel_id=1, source_target_pairs={{0,8},{2,10},{4,12},{6,14},{8,0},{10,2},{12,4},{14,6},{1,9},{3,11}... | collective-permute-start | bytes 294920 | tf_op jit(solution)/shard_map/down_swap/ppermute | solution.py:35
  123.0 4.3 %add_products.6.refs_2_ = f32[384,1024]{1,0:T(8,128)S(1)} custom-call(s32[8]{0:T(128)S(1)} %stack.39.where, bf16[384,1024]{1,0:T(8,128)(2,1)S(1)} %collective-permute-done.13.refs_0_, bf16[384,1024]{1,0:T(8,128)(2,1)S(1)} %collective-permute-done.10.refs_1_, bf16[8192,1024]{1,0:T(8,128)(2,1)} %refs_1_.3, bf16[8192,1024]{1,0:T(8,128)(2,1)} %refs_1_.3, ...), custom_call_target="tpu_custom_call" | custom-call | tf_op jit(solution)/shard_map/add_products/pallas_call | solution.py:328
  127.3 16.4 %collective-permute-done.17 = f16[384,128]{1,0:T(8,128)(2,1)S(1)} collective-permute-done((f16[384,128]{1,0:T(8,128)(2,1)S(1)}, f16[384,128]{1,0:T(8,128)(2,1)S(1)}, u32[]{:S(2)}, u32[]{:S(2)}) %collective-permute-start.17) | collective-permute-done | bytes 98336 | tf_op jit(solution)/shard_map/down_swap/ppermute | solution.py:35
  143.6 2.8 %up_rows.1 = (f32[384,1024]{1,0:T(8,128)S(1)}, f32[384,1024]{1,0:T(8,128)S(1)}) custom-call(s32[4]{0:T(128)S(1)} %copy-done.6, s32[1]{0:T(128)} %bitcast.place, f32[384,128]{1,0:T(8,128)S(1)} %add_multiply_fusion.low, bf16[4,256,1024]{2,1,0:T(8,128)(2,1)S(1)} %fetch_blocks.1.own, bf16[4,256,1024]{2,1,0:T(8,128)(2,1)} %collective-permute-done.6.other), custom_call_target="tpu_custom_call" | custom-call | tf_op jit(solution)/shard_map/up_rows/pallas_call | solution.py:270
  146.5 3.0 %add_products.7.x_ref = bf16[384,1024]{1,0:T(8,128)(2,1)S(1)} custom-call(s32[8]{0:T(128)S(1)} %stack.39.where, bf16[384,1024]{1,0:T(8,128)(2,1)S(1)} %pad_maximum_fusion.refs_0_, bf16[8192,1024]{1,0:T(8,128)(2,1)} %refs_1_.3, f32[384,1024]{1,0:T(8,128)S(1)} %add_products.6.refs_2_, f32[384,1024]{1,0:T(8,128)S(1)} %get-tuple-element.74.refs_3_), custom_call_target="tpu_custom_call" | custom-call | tf_op jit(solution)/shard_map/add_products/pallas_call | solution.py:328
  152.3 2.5 %unpack_rows.2 = bf16[512,1024]{1,0:T(8,128)(2,1)} custom-call(s32[4]{0:T(128)S(1)} %copy-done.6, s32[1]{0:T(128)} %bitcast.place, bf16[384,1024]{1,0:T(8,128)(2,1)S(1)} %add_products.7.x_ref, bf16[128,1024]{1,0:T(8,128)(2,1)S(1)} %collective-permute-done.19.spare_ref), custom_call_target="tpu_custom_call" | custom-call | tf_op jit(solution)/shard_map/unpack_rows/pallas_call | solution.py:156
  154.8 2.5 %unpack_rows.3 = bf16[512,1024]{1,0:T(8,128)(2,1)} custom-call(s32[4]{0:T(128)S(1)} %copy-done.6, s32[1]{0:T(128)} %bitcast.place, bf16[384,1024]{1,0:T(8,128)(2,1)S(1)} %fusion.3.x_ref, bf16[128,1024]{1,0:T(8,128)(2,1)S(1)} %collective-permute-done.22.spare_ref), custom_call_target="tpu_custom_call" | custom-call | tf_op jit(solution)/shard_map/unpack_rows/pallas_call | solution.py:156
  (79 shorter events, 32.5 us)
Async XLA Ops:
  0.6 5.4 %copy-start.8 = (s32[32]{0:T(128)S(1)}, s32[32]{0:T(128)}, u32[]{:S(2)}) copy-start(s32[32]{0:T(128)} %location.1) | copy-start | bytes 388
  5.6 3.9 %collective-permute-start = (bf16[256,1024]{1,0:T(8,128)(2,1)}, bf16[256,1024]{1,0:T(8,128)(2,1)}, u32[]{:S(2)}, u32[]{:S(2)}) collective-permute-start(bf16[256,1024]{1,0:T(8,128)(2,1)} %spare_rows.1), channel_id=1, source_target_pairs={{0,1},{1,0},{2,3},{3,2},{4,5},{5,4},{6,7},{7,6},{8,9},{9,8},{10,11... | collective-permute-start | bytes 1572872 | tf_op jit(solution)/shard_map/ppermute | solution.py:39
  9.2 41.4 %collective-permute-start.6 = (bf16[4,256,1024]{2,1,0:T(8,128)(2,1)S(1)}, bf16[4,256,1024]{2,1,0:T(8,128)(2,1)}, u32[]{:S(2)}, u32[]{:S(2)}) collective-permute-start(bf16[4,256,1024]{2,1,0:T(8,128)(2,1)S(1)} %fetch_blocks.1.own), channel_id=1, source_target_pairs={{0,1},{1,0},{2,3},{3,2},{4,5},{5,4},{6,7},{7,6},{8,9},{9,8},{10,11... | collective-permute-start | bytes 6291464 | tf_op jit(solution)/shard_map/ppermute | solution.py:39
  17.1 12.6 %collective-permute-start.2 = (f16[192,1024]{1,0:T(8,128)(2,1)S(1)}, f16[192,1024]{1,0:T(8,128)(2,1)S(1)}, u32[]{:S(2)}, u32[]{:S(2)}) collective-permute-start(f16[192,1024]{1,0:T(8,128)(2,1)S(1)} %get-tuple-element.91), channel_id=1, source_target_pairs={{0,4},{4,8},{8,12},{12,14},{14,10},{10,6},{6,2},{2,0},{1,5},{5,9},... | collective-permute-start | bytes 1179656 | tf_op jit(solution)/shard_map/scatter_up_1/ppermute | solution.py:35
  19.8 12.0 %collective-permute-start.3 = (f16[192,1024]{1,0:T(8,128)(2,1)S(1)}, f16[192,1024]{1,0:T(8,128)(2,1)S(1)}, u32[]{:S(2)}, u32[]{:S(2)}) collective-permute-start(f16[192,1024]{1,0:T(8,128)(2,1)S(1)} %get-tuple-element.90), channel_id=1, source_target_pairs={{4,0},{8,4},{12,8},{14,12},{10,14},{6,10},{2,6},{0,2},{5,1},{9,5},... | collective-permute-start | bytes 1179656 | tf_op jit(solution)/shard_map/scatter_down_1/ppermute | solution.py:35
  19.8 28.8 %collective-permute-start.4 = (bf16[384,1024]{1,0:T(8,128)(2,1)S(1)}, bf16[384,1024]{1,0:T(8,128)(2,1)S(1)}, u32[]{:S(2)}, u32[]{:S(2)}) collective-permute-start(bf16[384,1024]{1,0:T(8,128)(2,1)S(1)} %pack_rows.2.x.refs_0_), channel_id=1, source_target_pairs={{4,0},{8,4},{12,8},{14,12},{10,14},{6,10},{2,6},{0,2},{5,1},{9,5},... | collective-permute-start | bytes 2359304 | tf_op jit(solution)/shard_map/gather_down_1/ppermute | solution.py:35
  21.7 24.8 %collective-permute-start.1 = (bf16[384,1024]{1,0:T(8,128)(2,1)S(1)}, bf16[384,1024]{1,0:T(8,128)(2,1)S(1)}, u32[]{:S(2)}, u32[]{:S(2)}) collective-permute-start(bf16[384,1024]{1,0:T(8,128)(2,1)S(1)} %pack_rows.2.x.refs_0_), channel_id=1, source_target_pairs={{0,4},{4,8},{8,12},{12,14},{14,10},{10,6},{6,2},{2,0},{1,5},{5,9},... | collective-permute-start | bytes 2359304 | tf_op jit(solution)/shard_map/gather_up_1/ppermute | solution.py:35
  32.2 41.3 %collective-permute-start.7 = (f16[384,1024]{1,0:T(8,128)(2,1)S(1)}, f16[384,1024]{1,0:T(8,128)(2,1)S(1)}, u32[]{:S(2)}, u32[]{:S(2)}) collective-permute-start(f16[384,1024]{1,0:T(8,128)(2,1)S(1)} %fusion.4), channel_id=1, source_target_pairs={{0,4},{4,8},{8,12},{12,14},{14,10},{10,6},{6,2},{2,0},{1,5},{5,9},... | collective-permute-start | bytes 2359304 | tf_op jit(solution)/shard_map/scatter_up_2/ppermute | solution.py:35
  34.0 39.5 %collective-permute-start.8 = (f16[384,1024]{1,0:T(8,128)(2,1)S(1)}, f16[384,1024]{1,0:T(8,128)(2,1)S(1)}, u32[]{:S(2)}, u32[]{:S(2)}) collective-permute-start(f16[384,1024]{1,0:T(8,128)(2,1)S(1)} %fusion.5), channel_id=1, source_target_pairs={{4,0},{8,4},{12,8},{14,12},{10,14},{6,10},{2,6},{0,2},{5,1},{9,5},... | collective-permute-start | bytes 2359304 | tf_op jit(solution)/shard_map/scatter_down_2/ppermute | solution.py:35
  48.6 31.6 %collective-permute-start.5 = (bf16[384,1024]{1,0:T(8,128)(2,1)S(1)}, bf16[384,1024]{1,0:T(8,128)(2,1)S(1)}, u32[]{:S(2)}, u32[]{:S(2)}) collective-permute-start(bf16[384,1024]{1,0:T(8,128)(2,1)S(1)} %collective-permute-done.1.refs_2_), channel_id=1, source_target_pairs={{0,4},{4,8},{8,12},{12,14},{14,10},{10,6},{6,2},{2,0},{1,5},{5,9},... | collective-permute-start | bytes 2359304 | tf_op jit(solution)/shard_map/gather_up_2/ppermute | solution.py:35
  50.2 32.1 %collective-permute-start.9 = (bf16[384,1024]{1,0:T(8,128)(2,1)S(1)}, bf16[384,1024]{1,0:T(8,128)(2,1)S(1)}, u32[]{:S(2)}, u32[]{:S(2)}) collective-permute-start(bf16[384,1024]{1,0:T(8,128)(2,1)S(1)} %collective-permute-done.4.refs_1_), channel_id=1, source_target_pairs={{4,0},{8,4},{12,8},{14,12},{10,14},{6,10},{2,6},{0,2},{5,1},{9,5},... | collective-permute-start | bytes 2359304 | tf_op jit(solution)/shard_map/gather_down_2/ppermute | solution.py:35
  75.3 24.1 %collective-permute-start.12 = (f16[384,1024]{1,0:T(8,128)(2,1)S(1)}, f16[384,1024]{1,0:T(8,128)(2,1)S(1)}, u32[]{:S(2)}, u32[]{:S(2)}) collective-permute-start(f16[384,1024]{1,0:T(8,128)(2,1)S(1)} %multiply_convert_fusion.2), channel_id=1, source_target_pairs={{4,0},{8,4},{12,8},{14,12},{10,14},{6,10},{2,6},{0,2},{5,1},{9,5},... | collective-permute-start | bytes 2359304 | tf_op jit(solution)/shard_map/scatter_down_3/ppermute | solution.py:35
  75.7 23.7 %collective-permute-start.11 = (f16[384,1024]{1,0:T(8,128)(2,1)S(1)}, f16[384,1024]{1,0:T(8,128)(2,1)S(1)}, u32[]{:S(2)}, u32[]{:S(2)}) collective-permute-start(f16[384,1024]{1,0:T(8,128)(2,1)S(1)} %multiply_convert_fusion.3), channel_id=1, source_target_pairs={{0,4},{4,8},{8,12},{12,14},{14,10},{10,6},{6,2},{2,0},{1,5},{5,9},... | collective-permute-start | bytes 2359304 | tf_op jit(solution)/shard_map/scatter_up_3/ppermute | solution.py:35
  77.7 21.4 %collective-permute-start.15 = (f16[384,128]{1,0:T(8,128)(2,1)S(1)}, f16[384,128]{1,0:T(8,128)(2,1)S(1)}, u32[]{:S(2)}, u32[]{:S(2)}) collective-permute-start(f16[384,128]{1,0:T(8,128)(2,1)S(1)} %multiply_convert_fusion.7), channel_id=1, source_target_pairs={{0,2},{2,0},{4,6},{6,4},{8,10},{10,8},{12,14},{14,12},{1,3},{3,1},... | collective-permute-start | bytes 294920 | tf_op jit(solution)/shard_map/down_swap/ppermute | solution.py:35
  82.3 35.9 %collective-permute-start.13 = (bf16[384,1024]{1,0:T(8,128)(2,1)S(1)}, bf16[384,1024]{1,0:T(8,128)(2,1)S(1)}, u32[]{:S(2)}, u32[]{:S(2)}) collective-permute-start(bf16[384,1024]{1,0:T(8,128)(2,1)S(1)} %collective-permute-done.9.refs_0_), channel_id=1, source_target_pairs={{4,0},{8,4},{12,8},{14,12},{10,14},{6,10},{2,6},{0,2},{5,1},{9,5},... | collective-permute-start | bytes 2359304 | tf_op jit(solution)/shard_map/gather_down_3/ppermute | solution.py:35
  82.3 35.8 %collective-permute-start.10 = (bf16[384,1024]{1,0:T(8,128)(2,1)S(1)}, bf16[384,1024]{1,0:T(8,128)(2,1)S(1)}, u32[]{:S(2)}, u32[]{:S(2)}) collective-permute-start(bf16[384,1024]{1,0:T(8,128)(2,1)S(1)} %collective-permute-done.5.refs_1_), channel_id=1, source_target_pairs={{0,4},{4,8},{8,12},{12,14},{14,10},{10,6},{6,2},{2,0},{1,5},{5,9},... | collective-permute-start | bytes 2359304 | tf_op jit(solution)/shard_map/gather_up_3/ppermute | solution.py:35
  99.2 18.9 %collective-permute-start.16 = (f16[384,128]{1,0:T(8,128)(2,1)S(1)}, f16[384,128]{1,0:T(8,128)(2,1)S(1)}, u32[]{:S(2)}, u32[]{:S(2)}) collective-permute-start(f16[384,128]{1,0:T(8,128)(2,1)S(1)} %multiply_convert_fusion.6), channel_id=1, source_target_pairs={{0,4},{2,6},{4,0},{6,2},{8,12},{10,14},{12,8},{14,10},{1,5},{3,7},... | collective-permute-start | bytes 294920 | tf_op jit(solution)/shard_map/down_swap/ppermute | solution.py:35
  101.4 48.3 %collective-permute-start.21 = (f16[384,1024]{1,0:T(8,128)(2,1)S(1)}, f16[384,1024]{1,0:T(8,128)(2,1)S(1)}, u32[]{:S(2)}, u32[]{:S(2)}) collective-permute-start(f16[384,1024]{1,0:T(8,128)(2,1)S(1)} %multiply_convert_fusion), channel_id=1, source_target_pairs={{4,0},{8,4},{12,8},{14,12},{10,14},{6,10},{2,6},{0,2},{5,1},{9,5},... | collective-permute-start | bytes 2359304 | tf_op jit(solution)/shard_map/scatter_down_4/ppermute | solution.py:35
  103.5 46.2 %collective-permute-start.20 = (f16[384,1024]{1,0:T(8,128)(2,1)S(1)}, f16[384,1024]{1,0:T(8,128)(2,1)S(1)}, u32[]{:S(2)}, u32[]{:S(2)}) collective-permute-start(f16[384,1024]{1,0:T(8,128)(2,1)S(1)} %multiply_convert_fusion.1), channel_id=1, source_target_pairs={{0,4},{4,8},{8,12},{12,14},{14,10},{10,6},{6,2},{2,0},{1,5},{5,9},... | collective-permute-start | bytes 2359304 | tf_op jit(solution)/shard_map/scatter_up_4/ppermute | solution.py:35
  118.2 28.2 %collective-permute-start.14 = (bf16[192,1024]{1,0:T(8,128)(2,1)S(1)}, bf16[192,1024]{1,0:T(8,128)(2,1)S(1)}, u32[]{:S(2)}, u32[]{:S(2)}) collective-permute-start(bf16[192,1024]{1,0:T(8,128)(2,1)S(1)} %slice.83), channel_id=1, source_target_pairs={{0,4},{4,8},{8,12},{12,14},{14,10},{10,6},{6,2},{2,0},{1,5},{5,9},... | collective-permute-start | bytes 1179656 | tf_op jit(solution)/shard_map/gather_up_4/ppermute | solution.py:35
  118.3 28.2 %collective-permute-start.18 = (bf16[192,1024]{1,0:T(8,128)(2,1)S(1)}, bf16[192,1024]{1,0:T(8,128)(2,1)S(1)}, u32[]{:S(2)}, u32[]{:S(2)}) collective-permute-start(bf16[192,1024]{1,0:T(8,128)(2,1)S(1)} %slice.84), channel_id=1, source_target_pairs={{4,0},{8,4},{12,8},{14,12},{10,14},{6,10},{2,6},{0,2},{5,1},{9,5},... | collective-permute-start | bytes 1179656 | tf_op jit(solution)/shard_map/gather_down_4/ppermute | solution.py:35
  120.3 23.3 %collective-permute-start.17 = (f16[384,128]{1,0:T(8,128)(2,1)S(1)}, f16[384,128]{1,0:T(8,128)(2,1)S(1)}, u32[]{:S(2)}, u32[]{:S(2)}) collective-permute-start(f16[384,128]{1,0:T(8,128)(2,1)S(1)} %multiply_convert_fusion.5), channel_id=1, source_target_pairs={{0,8},{2,10},{4,12},{6,14},{8,0},{10,2},{12,4},{14,6},{1,9},{3,11}... | collective-permute-start | bytes 294920 | tf_op jit(solution)/shard_map/down_swap/ppermute | solution.py:35
  149.6 2.7 %collective-permute-start.19 = (bf16[128,1024]{1,0:T(8,128)(2,1)S(1)}, bf16[128,1024]{1,0:T(8,128)(2,1)S(1)}, u32[]{:S(2)}, u32[]{:S(2)}) collective-permute-start(bf16[128,1024]{1,0:T(8,128)(2,1)S(1)} %slice.98), channel_id=1, source_target_pairs={{0,1},{1,0},{2,3},{3,2},{4,5},{5,4},{6,7},{7,6},{8,9},{9,8},{10,11... | collective-permute-start | bytes 786440 | tf_op jit(solution)/shard_map/ppermute | solution.py:39
  151.7 3.0 %collective-permute-start.22 = (bf16[128,1024]{1,0:T(8,128)(2,1)S(1)}, bf16[128,1024]{1,0:T(8,128)(2,1)S(1)}, u32[]{:S(2)}, u32[]{:S(2)}) collective-permute-start(bf16[128,1024]{1,0:T(8,128)(2,1)S(1)} %slice.100), channel_id=1, source_target_pairs={{0,1},{1,0},{2,3},{3,2},{4,5},{5,4},{6,7},{7,6},{8,9},{9,8},{10,11... | collective-permute-start | bytes 786440 | tf_op jit(solution)/shard_map/ppermute | solution.py:39
  (8 other events, 20.7 us)

commit v4 on v3

--- a/solution.py
+++ b/solution.py
@@ -102,7 +102,7 @@
             out_specs=whole(shape),
         ),
         out_shape=jax.ShapeDtypeStruct(shape, BF16),
-        compiler_params=params(),
+        compiler_params=params(LARGE),
         name="spare_rows",
     )(counts, place, x, v)
 
@@ -130,7 +130,7 @@
             out_specs=whole(shape),
         ),
         out_shape=jax.ShapeDtypeStruct(shape, BF16),
-        compiler_params=params(),
+        compiler_params=params(LARGE),
         name="pack_rows",
     )(counts, place, x, moved)
 
@@ -178,7 +178,7 @@
 
 
 def fetch_kernel(held, adapter_of, location, place, *refs):
-    stores, out = refs[:4], refs[4]
+    stores, out = refs[:4], refs[-1]
     slot = location[adapter_of[pl.program_id(0)]] - place[0] * held
     mine = (slot >= 0) & (slot < held)
     for k, table in enumerate(stores):
@@ -186,7 +186,7 @@
         out[k] = jnp.where(mine, block, jnp.zeros_like(block))
 
 
-def fetch(stores, adapter_of, location, place):
+def fetch(stores, adapter_of, location, place, after):
     held, rank, width = stores[0].shape
     requests = adapter_of.shape[0]
 
@@ -199,13 +199,13 @@
         grid_spec=pltpu.PrefetchScalarGridSpec(
             num_scalar_prefetch=3,
             grid=(requests,),
-            in_specs=[pl.BlockSpec((1, rank, width), at)] * 4,
+            in_specs=[pl.BlockSpec((1, rank, width), at)] * 4 + [pl.BlockSpec(memory_space=pl.ANY)],
             out_specs=pl.BlockSpec((4, rank, width), lambda i, *_: (0, i, 0)),
         ),
         out_shape=jax.ShapeDtypeStruct((4, requests * rank, width), BF16),
         compiler_params=params(LARGE),
         name="fetch_blocks",
-    )(adapter_of, location, place, *stores)
+    )(adapter_of, location, place, *stores, after)
 
 
 def down_kernel(counts, place, x, v, own, other, out, blocks):
@@ -353,9 +353,12 @@
     return lax.optimization_barrier((value, others))[0]
 
 
-def swap_down(total, bit, size):
+def swap(total, bit, size):
     mine = (total * DOWN_SCALE).astype(F16)
-    moved = send(mine, [(t, t ^ bit) for t in range(size)], "down_swap")
+    return send(mine, [(t, t ^ bit) for t in range(size)], f"down_sums_{bit}"), mine
+
+
+def meet(moved, mine):
     return (mine.astype(F32) + moved.astype(F32)) * (1.0 / DOWN_SCALE)
 
 
@@ -384,21 +387,46 @@
             [look_up(at, [order[(p + d) % size] for p in place_of]) for d in offsets]
         )
 
-        moved = other_replica(spare_rows(counts, place, tokens, context, spare))
-        mine = fetch((store_aq, store_ao, store_bq, store_bo), adapter_of, location, place)
-        tok = pack(counts, place, tokens, tie(moved, mine), 0)
+        handed = spare_rows(counts, place, tokens, context, spare)
+        moved = other_replica(handed)
+        tok = pack(counts, place, tokens, moved, 0)
         ahead, behind = send(tok, following, "gather_up_1"), send(tok, preceding, "gather_down_1")
-        ctx = pack(counts, place, tie(context, tok), moved, 1)
-        far = narrow(shares(where, size - 1, 1, ctx, output_weight)[0])
+        ctx = pack(counts, tie(place, tok), context, moved, 1)
+        stores = (store_aq, store_ao, store_bq, store_bo)
+        mine = fetch(stores, adapter_of, location, place, ctx)
+        theirs = other_replica(mine)
+        far = narrow(shares(tie(where, mine), size - 1, 1, ctx, output_weight)[0])
         up_sum = send(far[:half], following, "scatter_up_1")
         down_sum = send(far[half:], preceding, "scatter_down_1")
-        theirs = other_replica(mine)
-        near = list(shares(where, size - 3, 2, tie(ctx, far), output_weight))
-
-        q, bit = None, 1
+        parts = down(counts, place, tok, tie(ctx, far), mine, theirs)
+        bits = [1 << i for i in range(size.bit_length() - 1)]
+        swapped = swap(parts, bits.pop(0), size)
+        near = shares(tie(where, parts), size - 3, 2, ctx, output_weight)
+
+        q, ready = None, near
         for step in range(1, steps):
-            up_sum, down_sum = lax.optimization_barrier((tie(up_sum, near), down_sum))
+            got_up, got_down = lax.optimization_barrier((tie(ahead, ready), behind))
+            if step < steps - 1:
+                ahead = send(got_up, following, f"gather_up_{step + 1}")
+                behind = send(got_down, preceding, f"gather_down_{step + 1}")
+            else:
+                ahead = send(got_up[:half], following, f"gather_up_{step + 1}")
+                behind = send(got_down[half:], preceding, f"gather_down_{step + 1}")
+            if step == 1:
+                rest = shares(where, 0, size - 3, tie(ctx, got_up, got_down), output_weight)
+                pieces, at_pieces, sofar = [tok, got_down, got_up], [0, 1, 2], []
+            else:
+                pieces, at_pieces, sofar = [got_down, got_up], [2 * step - 1, 2 * step], [q]
+            q = add_products(tie(where, rest), pieces, at_pieces, query_weight, sofar)
+            up_sum, down_sum, swapped = lax.optimization_barrier((tie(up_sum, q), down_sum, swapped))
+            if swapped is not None:
+                parts = meet(*swapped)
+                swapped = None
+            if bits:
+                swapped = swap(tie(parts, up_sum), bits.pop(0), size)
             up_share, down_share = near[0], near[1]
+            d = steps - step - 1
+            near = rest[2 * d - 1], rest[2 * d]
             if step == 1:
                 up_out = jnp.concatenate([up_share[:half] + widen(up_sum), up_share[half:]])
                 down_out = jnp.concatenate([down_share[:half], down_share[half:] + widen(down_sum)])
@@ -407,44 +435,21 @@
             up_out, down_out = narrow(up_out), narrow(down_out)
             up_sum = send(up_out, following, f"scatter_up_{step + 1}")
             down_sum = send(down_out, preceding, f"scatter_down_{step + 1}")
-            got_up, got_down = lax.optimization_barrier((tie(ahead, up_out, down_out), behind))
-            if step < steps - 1:
-                ahead = send(got_up, following, f"gather_up_{step + 1}")
-                behind = send(got_down, preceding, f"gather_down_{step + 1}")
-            else:
-                ahead = send(got_up[:half], following, f"gather_up_{step + 1}")
-                behind = send(got_down[half:], preceding, f"gather_down_{step + 1}")
-            ready = got_up
-            if step == 1:
-                theirs = tie(theirs, up_out)
-                parts = down(counts, place, tok, ctx, tie(mine, ready), theirs)
-                ready = parts
-            if bit < size:
-                parts = swap_down(tie(parts, ready), bit, size)
-                bit *= 2
-            if step == 1:
-                rest = shares(where, 0, size - 3, tie(ctx, ready), output_weight)
-                ready = rest
-                pieces, at_pieces, sofar = [tok, got_down, got_up], [0, 1, 2], []
-            else:
-                pieces, at_pieces, sofar = [got_down, got_up], [2 * step - 1, 2 * step], [q]
-            pieces[0] = tie(pieces[0], ready)
-            q = add_products(where, pieces, at_pieces, query_weight, sofar)
-            d = steps - step - 1
-            near = [tie(rest[2 * d - 1], q), rest[2 * d]]
-        while bit < size:
-            parts = swap_down(tie(parts, q), bit, size)
-            bit *= 2
-        up_q, up_o = up(counts, place, tie(parts, q), mine, theirs)
-        got_up, got_down = lax.optimization_barrier((tie(ahead, up_q), behind))
+            ready = (up_out, down_out)
+        got_up, got_down, swapped = lax.optimization_barrier((tie(ahead, ready), behind, swapped))
+        if swapped is not None:
+            parts = meet(*swapped)
+        for bit in bits:
+            parts = meet(*swap(parts, bit, size))
         last = jnp.concatenate([got_up, got_down])
+        up_q, up_o = up(counts, place, tie(parts, last), mine, theirs)
         q = add_products(where, [last], [size - 1], query_weight, [q, up_q], BF16)
         q_m = other_replica(q[packed - spare :])
-        up_sum, down_sum = lax.optimization_barrier((tie(up_sum, q), down_sum))
+        queries = unpack(counts, place, rows, (q, q_m))
+        up_sum, down_sum = lax.optimization_barrier((tie(up_sum, queries), down_sum))
         o = (rest[0] + widen(up_sum) + widen(down_sum) + up_o).astype(BF16)
         o_m = other_replica(o[packed - spare :])
-        queries = unpack(counts, place, rows, (q, tie(q_m, o)))
-        attended = unpack(counts, place, rows, (o, tie(o_m, queries)))
+        attended = unpack(counts, place, rows, (o, o_m))
         return queries, attended
 
     return local

time: 159 us -> 149 us (0.937)
  waiting for transfers between devices: 65.7 us -> 55 us
  starting transfers between devices: 21.1 us -> 25.2 us
  Pallas kernels: 56.2 us -> 53.5 us
    ppermute x19, waiting for transfers between devices: 65.7 us -> 50.5 us  [send(): return lax.ppermute(value, 'tensor', pairs)]
    ppermute x4, waiting for transfers between devices: 0.01 us -> 4.58 us  [other_replica(): return lax.ppermute(value, 'replica', [(0, 1), (1, 0)])]
    ppermute x19, starting transfers between devices: 20 us -> 24.4 us  [send(): return lax.ppermute(value, 'tensor', pairs)]
    squeeze x1 -> x0, local copies, waits for them, and re-layouts: 2.29 us -> none  [local(): near = [tie(rest[2 * d - 1], q), rest[2 * d]]]
    pallas_call x2, Pallas kernels: 4.15 us -> 2.24 us  [pack(): pl.pallas_call(pack_kernel, grid_spec=pltpu.PrefetchScalarGridSpec(num_sc...]
    unnamed x18 -> x21, local copies, waits for them, and re-layouts: 3.13 us -> 4.47 us
    convert_element_type x7 -> x5, other arithmetic: 4.55 us -> 5.63 us  [narrow(): return (value * SUM_SCALE).astype(F16)]
  transfers between devices with their start and end apart: 23 -> 23, of which waited for: 9 -> 17; matrix products, arithmetic and copies ran while one was open for 6% -> 4% of each run, Pallas kernels for 33% -> 30%
where the time goes in v4:
time: 149 us; the launch traced here: 148 us
  waiting for transfers between devices  55 us (37%)
  Pallas kernels  53.5 us (36%)
  starting transfers between devices  25.2 us (17%)
  other arithmetic  8.15 us (5%)
  local copies, waits for them, and re-layouts  4.98 us (3%)
    ppermute x19, waiting for transfers between devices, send(): return lax.ppermute(value, 'tensor', pairs)  50.5 us
    ppermute x19, starting transfers between devices, send(): return lax.ppermute(value, 'tensor', pairs)  24.4 us
    pallas_call x3, Pallas kernels, shares(): pl.pallas_call(shares_kernel, grid_spec=pltpu.PrefetchScalarGridSpec(num_...  18.9 us
    pallas_call x4, Pallas kernels, add_products(): pl.pallas_call(functools.partial(add_kernel, len(pieces)), grid_spec=pltp...  17 us
    convert_element_type x5, other arithmetic, narrow(): return (value * SUM_SCALE).astype(F16)  5.63 us
    pallas_call x2, Pallas kernels, unpack(): pl.pallas_call(unpack_kernel, grid_spec=pltpu.PrefetchScalarGridSpec(num_...  4.94 us
    ppermute x4, waiting for transfers between devices, other_replica(): return lax.ppermute(value, 'replica', [(0, 1), (1, 0)])  4.58 us
    unnamed x21, local copies, waits for them, and re-layouts  4.47 us
  transfers between devices with their start and end apart: 23, of which 17 were waited for; matrix products, arithmetic and copies ran while one was open for 4% of the time, Pallas kernels for 30%

profile of v4, /device:TPU:0, one launch (start us, length us, event | category | flops | bytes accessed | tf_op | source)
XLA Modules:
  0.0 148.0 jit_solution(12045802885640965233)
XLA Ops:
  10.4 3.1 %fetch_blocks.1.own = bf16[4,256,1024]{2,1,0:T(8,128)(2,1)S(1)} custom-call(s32[4]{0:T(128)S(1)} %copy-done.8, s32[32]{0:T(128)S(1)} %copy-done.9, s32[1]{0:T(128)} %bitcast.place, bf16[16,64,1024]{2,1,0:T(8,128)(2,1)S(1)} %copy-done.5, bf16[16,64,1024]{2,1,0:T(8,128)(2,1)} %refs_1_.2, bf16[16,64,1024]{2,1,0:T(8,128)(2,1)} %refs_2_.3, ...), custom_call_target="tpu_custom_call" | custom-call | tf_op jit(solution)/shard_map/fetch_blocks/pallas_call | solution.py:197
  13.9 3.0 %collective-permute-start.1 = (bf16[384,1024]{1,0:T(8,128)(2,1)}, bf16[384,1024]{1,0:T(8,128)(2,1)S(1)}, u32[]{:S(2)}, u32[]{:S(2)}) collective-permute-start(bf16[384,1024]{1,0:T(8,128)(2,1)} %copy-done), channel_id=1, source_target_pairs={{0,4},{4,8},{8,12},{12,14},{14,10},{10,6},{6,2},{2,0},{1,5},{5,9},... | collective-permute-start | bytes 2359304 | tf_op jit(solution)/shard_map/gather_up_1/ppermute | solution.py:35
  16.8 3.1 %shares.4 = f32[1,384,1024]{2,1,0:T(8,128)S(1)} custom-call(s32[8]{0:T(128)S(1)} %stack.39.where, bf16[384,1024]{1,0:T(8,128)(2,1)S(1)} %pack_rows.3.refs_4_.v.x_ref, bf16[1024,8192]{1,0:T(8,128)(2,1)} %w_ref.5), custom_call_target="tpu_custom_call" | custom-call | tf_op jit(solution)/shard_map/shares/pallas_call | solution.py:292
  22.4 3.6 %down_rows.1 = f32[384,128]{1,0:T(8,128)S(1)} custom-call(s32[4]{0:T(128)S(1)} %copy-done.7, s32[1]{0:T(128)} %bitcast.place, bf16[384,1024]{1,0:T(8,128)(2,1)S(1)} %copy-done.1, bf16[384,1024]{1,0:T(8,128)(2,1)S(1)} %pack_rows.3.refs_4_.v.x_ref, bf16[4,256,1024]{2,1,0:T(8,128)(2,1)S(1)} %fetch_blocks.1.own, bf16[4,256,1024]{2,1,0:T(8,128)(2,1)} %collective-permute-done.2.other), custom_call_target="tpu_custom_call" | custom-call | tf_op jit(solution)/shard_map/down_rows/pallas_call | solution.py:232
  26.0 4.2 %shares.3 = f32[2,384,1024]{2,1,0:T(8,128)S(1)} custom-call(s32[8]{0:T(128)S(1)} %stack.39.where, bf16[384,1024]{1,0:T(8,128)(2,1)S(1)} %pack_rows.3.refs_4_.v.x_ref, bf16[1024,8192]{1,0:T(8,128)(2,1)} %w_ref.5), custom_call_target="tpu_custom_call" | custom-call | tf_op jit(solution)/shard_map/shares/pallas_call | solution.py:292
  32.3 3.0 %collective-permute-done.1.refs_2_ = bf16[384,1024]{1,0:T(8,128)(2,1)S(1)} collective-permute-done((bf16[384,1024]{1,0:T(8,128)(2,1)}, bf16[384,1024]{1,0:T(8,128)(2,1)S(1)}, u32[]{:S(2)}, u32[]{:S(2)}) %collective-permute-start.1) | collective-permute-done | bytes 786464 | tf_op jit(solution)/shard_map/gather_up_1/ppermute | solution.py:35
  39.5 11.6 %shares.5 = f32[5,384,1024]{2,1,0:T(8,128)} custom-call(s32[8]{0:T(128)S(1)} %stack.39.where, bf16[384,1024]{1,0:T(8,128)(2,1)S(1)} %pack_rows.3.refs_4_.v.x_ref, bf16[1024,8192]{1,0:T(8,128)(2,1)} %w_ref.5), custom_call_target="tpu_custom_call" | custom-call | tf_op jit(solution)/shard_map/shares/pallas_call | solution.py:292
  51.1 5.4 %add_products.4.refs_4_ = f32[384,1024]{1,0:T(8,128)S(1)} custom-call(s32[8]{0:T(128)S(1)} %stack.39.where, bf16[384,1024]{1,0:T(8,128)(2,1)S(1)} %copy-done.1, bf16[384,1024]{1,0:T(8,128)(2,1)S(1)} %collective-permute-done.3.refs_1_, bf16[384,1024]{1,0:T(8,128)(2,1)S(1)} %collective-permute-done.1.refs_2_, bf16[8192,1024]{1,0:T(8,128)(2,1)} %refs_1_.3, ...), custom_call_target="tpu_custom_call" | custom-call | tf_op jit(solution)/shard_map/add_products/pallas_call | solution.py:328
  64.3 4.3 %add_products.5.refs_4_ = f32[384,1024]{1,0:T(8,128)S(1)} custom-call(s32[8]{0:T(128)S(1)} %stack.39.where, bf16[384,1024]{1,0:T(8,128)(2,1)S(1)} %collective-permute-done.8.refs_0_, bf16[384,1024]{1,0:T(8,128)(2,1)S(1)} %collective-permute-done.4.refs_1_, bf16[8192,1024]{1,0:T(8,128)(2,1)} %refs_1_.3, bf16[8192,1024]{1,0:T(8,128)(2,1)} %refs_1_.3, ...), custom_call_target="tpu_custom_call" | custom-call | tf_op jit(solution)/shard_map/add_products/pallas_call | solution.py:328
  69.1 10.5 %collective-permute-done.10 = f16[384,1024]{1,0:T(8,128)(2,1)S(1)} collective-permute-done((f16[384,1024]{1,0:T(8,128)(2,1)S(1)}, f16[384,1024]{1,0:T(8,128)(2,1)S(1)}, u32[]{:S(2)}, u32[]{:S(2)}) %collective-permute-start.10) | collective-permute-done | bytes 786464 | tf_op jit(solution)/shard_map/scatter_up_2/ppermute | solution.py:35
  81.7 2.6 %fusion.12 = (f16[384,1024]{1,0:T(8,128)(2,1)S(1)}, f16[384,1024]{1,0:T(8,128)(2,1)S(1)}) fusion(f32[5,384,1024]{2,1,0:T(8,128)} %shares.5, f16[384,1024]{1,0:T(8,128)(2,1)S(1)} %collective-permute-done.11, f16[384,1024]{1,0:T(8,128)(2,1)S(1)} %collective-permute-done.10), kind=kLoop, calls=%fused_computation.16 | loop fusion | flops 3932160 | bytes 6291456 | tf_op jit(solution)/shard_map/convert_element_type | solution.py:345
  86.4 2.7 %collective-permute-start.17 = (f16[384,128]{1,0:T(8,128)(2,1)S(1)}, f16[384,128]{1,0:T(8,128)(2,1)S(1)}, u32[]{:S(2)}, u32[]{:S(2)}) collective-permute-start(f16[384,128]{1,0:T(8,128)(2,1)S(1)} %multiply_convert_fusion.1), channel_id=1, source_target_pairs={{0,8},{2,10},{4,12},{6,14},{8,0},{10,2},{12,4},{14,6},{1,9},{3,11}... | collective-permute-start | bytes 294920 | tf_op jit(solution)/shard_map/down_sums_4/ppermute | solution.py:35
  89.1 7.4 %collective-permute-done.9.refs_1_ = bf16[384,1024]{1,0:T(8,128)(2,1)S(1)} collective-permute-done((bf16[384,1024]{1,0:T(8,128)(2,1)S(1)}, bf16[384,1024]{1,0:T(8,128)(2,1)S(1)}, u32[]{:S(2)}, u32[]{:S(2)}) %collective-permute-start.9) | collective-permute-done | bytes 786464 | tf_op jit(solution)/shard_map/gather_up_3/ppermute | solution.py:35
  98.6 4.3 %add_products.6.refs_2_ = f32[384,1024]{1,0:T(8,128)S(1)} custom-call(s32[8]{0:T(128)S(1)} %stack.39.where, bf16[384,1024]{1,0:T(8,128)(2,1)S(1)} %collective-permute-done.13.refs_0_, bf16[384,1024]{1,0:T(8,128)(2,1)S(1)} %collective-permute-done.9.refs_1_, bf16[8192,1024]{1,0:T(8,128)(2,1)} %refs_1_.3, bf16[8192,1024]{1,0:T(8,128)(2,1)} %refs_1_.3, ...), custom_call_target="tpu_custom_call" | custom-call | tf_op jit(solution)/shard_map/add_products/pallas_call | solution.py:328
  104.9 8.4 %collective-permute-done.15 = f16[384,1024]{1,0:T(8,128)(2,1)S(1)} collective-permute-done((f16[384,1024]{1,0:T(8,128)(2,1)S(1)}, f16[384,1024]{1,0:T(8,128)(2,1)S(1)}, u32[]{:S(2)}, u32[]{:S(2)}) %collective-permute-start.15) | collective-permute-done | bytes 786464 | tf_op jit(solution)/shard_map/scatter_up_3/ppermute | solution.py:35
  113.3 3.9 %collective-permute-done.17 = f16[384,128]{1,0:T(8,128)(2,1)S(1)} collective-permute-done((f16[384,128]{1,0:T(8,128)(2,1)S(1)}, f16[384,128]{1,0:T(8,128)(2,1)S(1)}, u32[]{:S(2)}, u32[]{:S(2)}) %collective-permute-start.17) | collective-permute-done | bytes 98336 | tf_op jit(solution)/shard_map/down_sums_4/ppermute | solution.py:35
  117.5 2.6 %fusion.6 = (f16[384,1024]{1,0:T(8,128)(2,1)S(1)}, f16[384,1024]{1,0:T(8,128)(2,1)S(1)}) fusion(f32[5,384,1024]{2,1,0:T(8,128)} %shares.5, f16[384,1024]{1,0:T(8,128)(2,1)S(1)} %collective-permute-done.16, f16[384,1024]{1,0:T(8,128)(2,1)S(1)} %collective-permute-done.15), kind=kLoop, calls=%fused_computation.8 | loop fusion | flops 3932160 | bytes 6291456 | tf_op jit(solution)/shard_map/convert_element_type | solution.py:345
  120.1 2.6 %collective-permute-start.20 = (f16[384,1024]{1,0:T(8,128)(2,1)S(1)}, f16[384,1024]{1,0:T(8,128)(2,1)S(1)}, u32[]{:S(2)}, u32[]{:S(2)}) collective-permute-start(f16[384,1024]{1,0:T(8,128)(2,1)S(1)} %get-tuple-element.83), channel_id=1, source_target_pairs={{0,4},{4,8},{8,12},{12,14},{14,10},{10,6},{6,2},{2,0},{1,5},{5,9},... | collective-permute-start | bytes 2359304 | tf_op jit(solution)/shard_map/scatter_up_4/ppermute | solution.py:35
  123.4 2.5 %collective-permute-done.18 = bf16[192,1024]{1,0:T(8,128)(2,1)S(1)} collective-permute-done((bf16[192,1024]{1,0:T(8,128)(2,1)S(1)}, bf16[192,1024]{1,0:T(8,128)(2,1)S(1)}, u32[]{:S(2)}, u32[]{:S(2)}) %collective-permute-start.18) | collective-permute-done | bytes 393248 | tf_op jit(solution)/shard_map/gather_down_4/ppermute | solution.py:35
  126.0 2.8 %up_rows.1 = (f32[384,1024]{1,0:T(8,128)S(1)}, f32[384,1024]{1,0:T(8,128)S(1)}) custom-call(s32[4]{0:T(128)S(1)} %copy-done.7, s32[1]{0:T(128)} %bitcast.place, f32[384,128]{1,0:T(8,128)S(1)} %add_multiply_fusion.low, bf16[4,256,1024]{2,1,0:T(8,128)(2,1)S(1)} %fetch_blocks.1.own, bf16[4,256,1024]{2,1,0:T(8,128)(2,1)} %collective-permute-done.2.other), custom_call_target="tpu_custom_call" | custom-call | tf_op jit(solution)/shard_map/up_rows/pallas_call | solution.py:270
  128.8 3.0 %add_products.7.x_ref = bf16[384,1024]{1,0:T(8,128)(2,1)S(1)} custom-call(s32[8]{0:T(128)S(1)} %stack.39.where, bf16[384,1024]{1,0:T(8,128)(2,1)S(1)} %constant_dynamic-update-slice_fusion.refs_0_, bf16[8192,1024]{1,0:T(8,128)(2,1)} %refs_1_.3, f32[384,1024]{1,0:T(8,128)S(1)} %add_products.6.refs_2_, f32[384,1024]{1,0:T(8,128)S(1)} %get-tuple-element.77.refs_3_), custom_call_target="tpu_custom_call" | custom-call | tf_op jit(solution)/shard_map/add_products/pallas_call | solution.py:328
  133.5 2.5 %unpack_rows.2 = bf16[512,1024]{1,0:T(8,128)(2,1)} custom-call(s32[4]{0:T(128)S(1)} %copy-done.7, s32[1]{0:T(128)} %bitcast.place, bf16[384,1024]{1,0:T(8,128)(2,1)S(1)} %add_products.7.x_ref, bf16[128,1024]{1,0:T(8,128)(2,1)S(1)} %collective-permute-done.19.spare_ref), custom_call_target="tpu_custom_call" | custom-call | tf_op jit(solution)/shard_map/unpack_rows/pallas_call | solution.py:156
  135.9 3.8 %collective-permute-done.20 = f16[384,1024]{1,0:T(8,128)(2,1)S(1)} collective-permute-done((f16[384,1024]{1,0:T(8,128)(2,1)S(1)}, f16[384,1024]{1,0:T(8,128)(2,1)S(1)}, u32[]{:S(2)}, u32[]{:S(2)}) %collective-permute-start.20) | collective-permute-done | bytes 786464 | tf_op jit(solution)/shard_map/scatter_up_4/ppermute | solution.py:35
  145.5 2.5 %unpack_rows.3 = bf16[512,1024]{1,0:T(8,128)(2,1)} custom-call(s32[4]{0:T(128)S(1)} %copy-done.7, s32[1]{0:T(128)} %bitcast.place, bf16[384,1024]{1,0:T(8,128)(2,1)S(1)} %fusion.3.x_ref, bf16[128,1024]{1,0:T(8,128)(2,1)S(1)} %collective-permute-done.22.spare_ref), custom_call_target="tpu_custom_call" | custom-call | tf_op jit(solution)/shard_map/unpack_rows/pallas_call | solution.py:156
  (79 shorter events, 43.8 us)
Async XLA Ops:
  4.7 4.1 %copy-start.4 = (bf16[512,1024]{1,0:T(8,128)(2,1)S(1)}, bf16[512,1024]{1,0:T(8,128)(2,1)}, u32[]{:S(2)}) copy-start(bf16[512,1024]{1,0:T(8,128)(2,1)} %x_ref.5) | copy-start | bytes 3145732
  4.8 2.1 %collective-permute-start = (bf16[256,1024]{1,0:T(8,128)(2,1)S(1)}, bf16[256,1024]{1,0:T(8,128)(2,1)S(1)}, u32[]{:S(2)}, u32[]{:S(2)}) collective-permute-start(bf16[256,1024]{1,0:T(8,128)(2,1)S(1)} %spare_rows.1), channel_id=1, source_target_pairs={{0,1},{1,0},{2,3},{3,2},{4,5},{5,4},{6,7},{7,6},{8,9},{9,8},{10,11... | collective-permute-start | bytes 1572872 | tf_op jit(solution)/shard_map/ppermute | solution.py:39
  13.6 8.8 %collective-permute-start.2 = (bf16[4,256,1024]{2,1,0:T(8,128)(2,1)S(1)}, bf16[4,256,1024]{2,1,0:T(8,128)(2,1)}, u32[]{:S(2)}, u32[]{:S(2)}) collective-permute-start(bf16[4,256,1024]{2,1,0:T(8,128)(2,1)S(1)} %fetch_blocks.1.own), channel_id=1, source_target_pairs={{0,1},{1,0},{2,3},{3,2},{4,5},{5,4},{6,7},{7,6},{8,9},{9,8},{10,11... | collective-permute-start | bytes 6291464 | tf_op jit(solution)/shard_map/ppermute | solution.py:39
  13.9 21.5 %collective-permute-start.1 = (bf16[384,1024]{1,0:T(8,128)(2,1)}, bf16[384,1024]{1,0:T(8,128)(2,1)S(1)}, u32[]{:S(2)}, u32[]{:S(2)}) collective-permute-start(bf16[384,1024]{1,0:T(8,128)(2,1)} %copy-done), channel_id=1, source_target_pairs={{0,4},{4,8},{8,12},{12,14},{14,10},{10,6},{6,2},{2,0},{1,5},{5,9},... | collective-permute-start | bytes 2359304 | tf_op jit(solution)/shard_map/gather_up_1/ppermute | solution.py:35
  16.8 20.6 %collective-permute-start.3 = (bf16[384,1024]{1,0:T(8,128)(2,1)}, bf16[384,1024]{1,0:T(8,128)(2,1)S(1)}, u32[]{:S(2)}, u32[]{:S(2)}) collective-permute-start(bf16[384,1024]{1,0:T(8,128)(2,1)} %copy-done), channel_id=1, source_target_pairs={{4,0},{8,4},{12,8},{14,12},{10,14},{6,10},{2,6},{0,2},{5,1},{9,5},... | collective-permute-start | bytes 2359304 | tf_op jit(solution)/shard_map/gather_down_1/ppermute | solution.py:35
  20.3 36.2 %collective-permute-start.5 = (f16[192,1024]{1,0:T(8,128)(2,1)S(1)}, f16[192,1024]{1,0:T(8,128)(2,1)S(1)}, u32[]{:S(2)}, u32[]{:S(2)}) collective-permute-start(f16[192,1024]{1,0:T(8,128)(2,1)S(1)} %get-tuple-element.91), channel_id=1, source_target_pairs={{0,4},{4,8},{8,12},{12,14},{14,10},{10,6},{6,2},{2,0},{1,5},{5,9},... | collective-permute-start | bytes 1179656 | tf_op jit(solution)/shard_map/scatter_up_1/ppermute | solution.py:35
  22.3 34.2 %collective-permute-start.6 = (f16[192,1024]{1,0:T(8,128)(2,1)S(1)}, f16[192,1024]{1,0:T(8,128)(2,1)S(1)}, u32[]{:S(2)}, u32[]{:S(2)}) collective-permute-start(f16[192,1024]{1,0:T(8,128)(2,1)S(1)} %get-tuple-element.90), channel_id=1, source_target_pairs={{4,0},{8,4},{12,8},{14,12},{10,14},{6,10},{2,6},{0,2},{5,1},{9,5},... | collective-permute-start | bytes 1179656 | tf_op jit(solution)/shard_map/scatter_down_1/ppermute | solution.py:35
  30.1 26.4 %collective-permute-start.7 = (f16[384,128]{1,0:T(8,128)(2,1)S(1)}, f16[384,128]{1,0:T(8,128)(2,1)S(1)}, u32[]{:S(2)}, u32[]{:S(2)}) collective-permute-start(f16[384,128]{1,0:T(8,128)(2,1)S(1)} %multiply_convert_fusion.3), channel_id=1, source_target_pairs={{0,2},{2,0},{4,6},{6,4},{8,10},{10,8},{12,14},{14,12},{1,3},{3,1},... | collective-permute-start | bytes 294920 | tf_op jit(solution)/shard_map/down_sums_1/ppermute | solution.py:35
  37.4 25.3 %collective-permute-start.4 = (bf16[384,1024]{1,0:T(8,128)(2,1)S(1)}, bf16[384,1024]{1,0:T(8,128)(2,1)S(1)}, u32[]{:S(2)}, u32[]{:S(2)}) collective-permute-start(bf16[384,1024]{1,0:T(8,128)(2,1)S(1)} %collective-permute-done.1.refs_2_), channel_id=1, source_target_pairs={{0,4},{4,8},{8,12},{12,14},{14,10},{10,6},{6,2},{2,0},{1,5},{5,9},... | collective-permute-start | bytes 2359304 | tf_op jit(solution)/shard_map/gather_up_2/ppermute | solution.py:35
  39.0 23.7 %collective-permute-start.8 = (bf16[384,1024]{1,0:T(8,128)(2,1)S(1)}, bf16[384,1024]{1,0:T(8,128)(2,1)S(1)}, u32[]{:S(2)}, u32[]{:S(2)}) collective-permute-start(bf16[384,1024]{1,0:T(8,128)(2,1)S(1)} %collective-permute-done.3.refs_1_), channel_id=1, source_target_pairs={{4,0},{8,4},{12,8},{14,12},{10,14},{6,10},{2,6},{0,2},{5,1},{9,5},... | collective-permute-start | bytes 2359304 | tf_op jit(solution)/shard_map/gather_down_2/ppermute | solution.py:35
  57.0 22.6 %collective-permute-start.10 = (f16[384,1024]{1,0:T(8,128)(2,1)S(1)}, f16[384,1024]{1,0:T(8,128)(2,1)S(1)}, u32[]{:S(2)}, u32[]{:S(2)}) collective-permute-start(f16[384,1024]{1,0:T(8,128)(2,1)S(1)} %fusion.16), channel_id=1, source_target_pairs={{0,4},{4,8},{8,12},{12,14},{14,10},{10,6},{6,2},{2,0},{1,5},{5,9},... | collective-permute-start | bytes 2359304 | tf_op jit(solution)/shard_map/scatter_up_2/ppermute | solution.py:35
  58.8 22.9 %collective-permute-start.11 = (f16[384,1024]{1,0:T(8,128)(2,1)S(1)}, f16[384,1024]{1,0:T(8,128)(2,1)S(1)}, u32[]{:S(2)}, u32[]{:S(2)}) collective-permute-start(f16[384,1024]{1,0:T(8,128)(2,1)S(1)} %fusion.17), channel_id=1, source_target_pairs={{4,0},{8,4},{12,8},{14,12},{10,14},{6,10},{2,6},{0,2},{5,1},{9,5},... | collective-permute-start | bytes 2359304 | tf_op jit(solution)/shard_map/scatter_down_2/ppermute | solution.py:35
  59.4 22.3 %collective-permute-start.12 = (f16[384,128]{1,0:T(8,128)(2,1)S(1)}, f16[384,128]{1,0:T(8,128)(2,1)S(1)}, u32[]{:S(2)}, u32[]{:S(2)}) collective-permute-start(f16[384,128]{1,0:T(8,128)(2,1)S(1)} %multiply_convert_fusion.2), channel_id=1, source_target_pairs={{0,4},{2,6},{4,0},{6,2},{8,12},{10,14},{12,8},{14,10},{1,5},{3,7},... | collective-permute-start | bytes 294920 | tf_op jit(solution)/shard_map/down_sums_2/ppermute | solution.py:35
  62.8 33.7 %collective-permute-start.9 = (bf16[384,1024]{1,0:T(8,128)(2,1)S(1)}, bf16[384,1024]{1,0:T(8,128)(2,1)S(1)}, u32[]{:S(2)}, u32[]{:S(2)}) collective-permute-start(bf16[384,1024]{1,0:T(8,128)(2,1)S(1)} %collective-permute-done.4.refs_1_), channel_id=1, source_target_pairs={{0,4},{4,8},{8,12},{12,14},{14,10},{10,6},{6,2},{2,0},{1,5},{5,9},... | collective-permute-start | bytes 2359304 | tf_op jit(solution)/shard_map/gather_up_3/ppermute | solution.py:35
  68.6 30.0 %collective-permute-start.13 = (bf16[384,1024]{1,0:T(8,128)(2,1)S(1)}, bf16[384,1024]{1,0:T(8,128)(2,1)S(1)}, u32[]{:S(2)}, u32[]{:S(2)}) collective-permute-start(bf16[384,1024]{1,0:T(8,128)(2,1)S(1)} %collective-permute-done.8.refs_0_), channel_id=1, source_target_pairs={{4,0},{8,4},{12,8},{14,12},{10,14},{6,10},{2,6},{0,2},{5,1},{9,5},... | collective-permute-start | bytes 2359304 | tf_op jit(solution)/shard_map/gather_down_3/ppermute | solution.py:35
  84.3 29.0 %collective-permute-start.15 = (f16[384,1024]{1,0:T(8,128)(2,1)S(1)}, f16[384,1024]{1,0:T(8,128)(2,1)S(1)}, u32[]{:S(2)}, u32[]{:S(2)}) collective-permute-start(f16[384,1024]{1,0:T(8,128)(2,1)S(1)} %get-tuple-element.85), channel_id=1, source_target_pairs={{0,4},{4,8},{8,12},{12,14},{14,10},{10,6},{6,2},{2,0},{1,5},{5,9},... | collective-permute-start | bytes 2359304 | tf_op jit(solution)/shard_map/scatter_up_3/ppermute | solution.py:35
  84.3 33.1 %collective-permute-start.16 = (f16[384,1024]{1,0:T(8,128)(2,1)S(1)}, f16[384,1024]{1,0:T(8,128)(2,1)S(1)}, u32[]{:S(2)}, u32[]{:S(2)}) collective-permute-start(f16[384,1024]{1,0:T(8,128)(2,1)S(1)} %get-tuple-element.84), channel_id=1, source_target_pairs={{4,0},{8,4},{12,8},{14,12},{10,14},{6,10},{2,6},{0,2},{5,1},{9,5},... | collective-permute-start | bytes 2359304 | tf_op jit(solution)/shard_map/scatter_down_3/ppermute | solution.py:35
  86.4 30.7 %collective-permute-start.17 = (f16[384,128]{1,0:T(8,128)(2,1)S(1)}, f16[384,128]{1,0:T(8,128)(2,1)S(1)}, u32[]{:S(2)}, u32[]{:S(2)}) collective-permute-start(f16[384,128]{1,0:T(8,128)(2,1)S(1)} %multiply_convert_fusion.1), channel_id=1, source_target_pairs={{0,8},{2,10},{4,12},{6,14},{8,0},{10,2},{12,4},{14,6},{1,9},{3,11}... | collective-permute-start | bytes 294920 | tf_op jit(solution)/shard_map/down_sums_4/ppermute | solution.py:35
  102.9 20.6 %collective-permute-start.14 = (bf16[192,1024]{1,0:T(8,128)(2,1)S(1)}, bf16[192,1024]{1,0:T(8,128)(2,1)S(1)}, u32[]{:S(2)}, u32[]{:S(2)}) collective-permute-start(bf16[192,1024]{1,0:T(8,128)(2,1)S(1)} %slice.83), channel_id=1, source_target_pairs={{0,4},{4,8},{8,12},{12,14},{14,10},{10,6},{6,2},{2,0},{1,5},{5,9},... | collective-permute-start | bytes 1179656 | tf_op jit(solution)/shard_map/gather_up_4/ppermute | solution.py:35
  102.9 23.0 %collective-permute-start.18 = (bf16[192,1024]{1,0:T(8,128)(2,1)S(1)}, bf16[192,1024]{1,0:T(8,128)(2,1)S(1)}, u32[]{:S(2)}, u32[]{:S(2)}) collective-permute-start(bf16[192,1024]{1,0:T(8,128)(2,1)S(1)} %slice.86), channel_id=1, source_target_pairs={{4,0},{8,4},{12,8},{14,12},{10,14},{6,10},{2,6},{0,2},{5,1},{9,5},... | collective-permute-start | bytes 1179656 | tf_op jit(solution)/shard_map/gather_down_4/ppermute | solution.py:35
  120.1 19.6 %collective-permute-start.20 = (f16[384,1024]{1,0:T(8,128)(2,1)S(1)}, f16[384,1024]{1,0:T(8,128)(2,1)S(1)}, u32[]{:S(2)}, u32[]{:S(2)}) collective-permute-start(f16[384,1024]{1,0:T(8,128)(2,1)S(1)} %get-tuple-element.83), channel_id=1, source_target_pairs={{0,4},{4,8},{8,12},{12,14},{14,10},{10,6},{6,2},{2,0},{1,5},{5,9},... | collective-permute-start | bytes 2359304 | tf_op jit(solution)/shard_map/scatter_up_4/ppermute | solution.py:35
  122.7 19.1 %collective-permute-start.21 = (f16[384,1024]{1,0:T(8,128)(2,1)S(1)}, f16[384,1024]{1,0:T(8,128)(2,1)S(1)}, u32[]{:S(2)}, u32[]{:S(2)}) collective-permute-start(f16[384,1024]{1,0:T(8,128)(2,1)S(1)} %get-tuple-element.82), channel_id=1, source_target_pairs={{4,0},{8,4},{12,8},{14,12},{10,14},{6,10},{2,6},{0,2},{5,1},{9,5},... | collective-permute-start | bytes 2359304 | tf_op jit(solution)/shard_map/scatter_down_4/ppermute | solution.py:35
  131.8 1.6 %collective-permute-start.19 = (bf16[128,1024]{1,0:T(8,128)(2,1)S(1)}, bf16[128,1024]{1,0:T(8,128)(2,1)S(1)}, u32[]{:S(2)}, u32[]{:S(2)}) collective-permute-start(bf16[128,1024]{1,0:T(8,128)(2,1)S(1)} %slice.100), channel_id=1, source_target_pairs={{0,1},{1,0},{2,3},{3,2},{4,5},{5,4},{6,7},{7,6},{8,9},{9,8},{10,11... | collective-permute-start | bytes 786440 | tf_op jit(solution)/shard_map/ppermute | solution.py:39
  143.9 1.6 %collective-permute-start.22 = (bf16[128,1024]{1,0:T(8,128)(2,1)S(1)}, bf16[128,1024]{1,0:T(8,128)(2,1)S(1)}, u32[]{:S(2)}, u32[]{:S(2)}) collective-permute-start(bf16[128,1024]{1,0:T(8,128)(2,1)S(1)} %slice.102), channel_id=1, source_target_pairs={{0,1},{1,0},{2,3},{3,2},{4,5},{5,4},{6,7},{7,6},{8,9},{9,8},{10,11... | collective-permute-start | bytes 786440 | tf_op jit(solution)/shard_map/ppermute | solution.py:39
  (9 other events, 15.2 us)

commit v5 on v4

--- a/solution.py
+++ b/solution.py
@@ -22,6 +22,7 @@
 
 SMALL = 16 * 1024 * 1024
 LARGE = 48 * 1024 * 1024
+FULL = 62 * 1024 * 1024
 
 
 def ring_order(size):
@@ -82,11 +83,11 @@
 
 
 def spare_kernel(counts, place, x_ref, v_ref, out):
-    rows, spare = x_ref.shape[0], out.shape[0] // 2
-    packed = rows - spare
+    spare = x_ref.shape[0]
+    packed = 2 * REQUEST_LENGTH - spare
     c_a, c_b, d_a, d_b = lengths(counts, place)
     seat = iota((spare, 1), 0) + packed - spare - d_a - d_b
-    home = home_of(packed + seat, seat >= 0, c_a)
+    home = home_of(packed + seat, seat >= 0, c_a) - packed
     out[:spare] = select_rows(home, x_ref).astype(BF16)
     out[spare:] = select_rows(home, v_ref).astype(BF16)
 
@@ -98,11 +99,11 @@
         grid_spec=pltpu.PrefetchScalarGridSpec(
             num_scalar_prefetch=2,
             grid=(1,),
-            in_specs=[whole(x.shape)] * 2,
+            in_specs=[pl.BlockSpec((spare, x.shape[1]), lambda *_: (x.shape[0] // spare - 1, 0))] * 2,
             out_specs=whole(shape),
         ),
         out_shape=jax.ShapeDtypeStruct(shape, BF16),
-        compiler_params=params(LARGE),
+        compiler_params=params(FULL),
         name="spare_rows",
     )(counts, place, x, v)
 
@@ -392,18 +393,19 @@
         tok = pack(counts, place, tokens, moved, 0)
         ahead, behind = send(tok, following, "gather_up_1"), send(tok, preceding, "gather_down_1")
         ctx = pack(counts, tie(place, tok), context, moved, 1)
-        stores = (store_aq, store_ao, store_bq, store_bo)
-        mine = fetch(stores, adapter_of, location, place, ctx)
-        theirs = other_replica(mine)
-        far = narrow(shares(tie(where, mine), size - 1, 1, ctx, output_weight)[0])
+        farthest = shares(where, size - 1, 1, ctx, output_weight)
+        far = narrow(farthest[0])
         up_sum = send(far[:half], following, "scatter_up_1")
         down_sum = send(far[half:], preceding, "scatter_down_1")
-        parts = down(counts, place, tok, tie(ctx, far), mine, theirs)
+        stores = (store_aq, store_ao, store_bq, store_bo)
+        mine = fetch(stores, adapter_of, location, place, tok)
+        theirs = other_replica(mine)
+        near = shares(tie(where, mine), size - 3, 2, ctx, output_weight)
+        parts = down(counts, place, tok, tie(ctx, near), mine, theirs)
         bits = [1 << i for i in range(size.bit_length() - 1)]
         swapped = swap(parts, bits.pop(0), size)
-        near = shares(tie(where, parts), size - 3, 2, ctx, output_weight)
-
-        q, ready = None, near
+
+        q, ready = None, parts
         for step in range(1, steps):
             got_up, got_down = lax.optimization_barrier((tie(ahead, ready), behind))
             if step < steps - 1:
@@ -446,9 +448,12 @@
         q = add_products(where, [last], [size - 1], query_weight, [q, up_q], BF16)
         q_m = other_replica(q[packed - spare :])
         queries = unpack(counts, place, rows, (q, q_m))
-        up_sum, down_sum = lax.optimization_barrier((tie(up_sum, queries), down_sum))
-        o = (rest[0] + widen(up_sum) + widen(down_sum) + up_o).astype(BF16)
-        o_m = other_replica(o[packed - spare :])
+        base = rest[0] + up_o
+        up_sum, down_sum = lax.optimization_barrier((tie(up_sum, queries, base), down_sum))
+        first = packed - spare
+        o_last = (base[first:] + widen(up_sum[first:]) + widen(down_sum[first:])).astype(BF16)
+        o_m = other_replica(o_last)
+        o = (base + widen(up_sum) + widen(down_sum)).astype(BF16)
         attended = unpack(counts, place, rows, (o, o_m))
         return queries, attended
 

time: 149 us -> 144 us (0.966)
  waiting for transfers between devices: 55 us -> 50.7 us
  Pallas kernels: 53.5 us -> 55.3 us
  local copies, waits for them, and re-layouts: 4.98 us -> 3.42 us
    ppermute x19, waiting for transfers between devices: 50.5 us -> 47.9 us  [send(): return lax.ppermute(value, 'tensor', pairs)]
    pallas_call x1, Pallas kernels: 0.99 us -> 2.9 us  [spare_rows(): pl.pallas_call(spare_kernel, grid_spec=pltpu.PrefetchScalarGridSpec(num_s...]
    ppermute x4, waiting for transfers between devices: 4.58 us -> 2.81 us  [other_replica(): return lax.ppermute(value, 'replica', [(0, 1), (1, 0)])]
    add x0 -> x1, other arithmetic: none -> 1.72 us  [local(): base = rest[0] + up_o]
    unnamed x21 -> x13, local copies, waits for them, and re-layouts: 4.47 us -> 2.93 us
  transfers between devices with their start and end apart: 23 -> 23, of which waited for: 17 -> 16; matrix products, arithmetic and copies ran while one was open for 4% -> 6% of each run, Pallas kernels for 30% -> 32%
where the time goes in v5:
time: 144 us
  Pallas kernels  55.3 us (38%)
  waiting for transfers between devices  50.7 us (35%)
  starting transfers between devices  25.3 us (18%)
  other arithmetic  8.34 us (6%)
  local copies, waits for them, and re-layouts  3.42 us (2%)
    ppermute x19, waiting for transfers between devices, send(): return lax.ppermute(value, 'tensor', pairs)  47.9 us
    ppermute x19, starting transfers between devices, send(): return lax.ppermute(value, 'tensor', pairs)  24.2 us
    pallas_call x3, Pallas kernels, shares(): pl.pallas_call(shares_kernel, grid_spec=pltpu.PrefetchScalarGridSpec(num_...  18.8 us
    pallas_call x4, Pallas kernels, add_products(): pl.pallas_call(functools.partial(add_kernel, len(pieces)), grid_spec=pltp...  16.9 us
    convert_element_type x5, other arithmetic, narrow(): return (value * SUM_SCALE).astype(F16)  5.59 us
    pallas_call x2, Pallas kernels, unpack(): pl.pallas_call(unpack_kernel, grid_spec=pltpu.PrefetchScalarGridSpec(num_...  4.95 us
    pallas_call x1, Pallas kernels, down(): pl.pallas_call(down_kernel, grid_spec=pltpu.PrefetchScalarGridSpec(num_sc...  3.56 us
    pallas_call x1, Pallas kernels, fetch(): pl.pallas_call(functools.partial(fetch_kernel, held), grid_spec=pltpu.Pre...  3.13 us
  transfers between devices with their start and end apart: 23, of which 16 were waited for; matrix products, arithmetic and copies ran while one was open for 6% of the time, Pallas kernels for 32%

profile of v5, /device:TPU:0, one launch (start us, length us, event | category | flops | bytes accessed | tf_op | source)
XLA Modules:
  0.0 144.0 jit_solution(10087010378653294263)
XLA Ops:
  0.7 2.9 %spare_rows.1 = bf16[256,1024]{1,0:T(8,128)(2,1)} custom-call(s32[4]{0:T(128)} %counts.13, s32[1]{0:T(128)} %bitcast.place, bf16[512,1024]{1,0:T(8,128)(2,1)} %x_ref.4, bf16[512,1024]{1,0:T(8,128)(2,1)} %x_ref.5), custom_call_target="tpu_custom_call" | custom-call | tf_op jit(solution)/shard_map/spare_rows/pallas_call | solution.py:97
  8.6 3.1 %fetch_blocks.1.own = bf16[4,256,1024]{2,1,0:T(8,128)(2,1)S(1)} custom-call(s32[4]{0:T(128)S(1)} %copy-done.4, s32[32]{0:T(128)S(1)} %copy-done.5, s32[1]{0:T(128)} %bitcast.place, bf16[16,64,1024]{2,1,0:T(8,128)(2,1)S(1)} %copy-done.2, bf16[16,64,1024]{2,1,0:T(8,128)(2,1)} %refs_1_.2, bf16[16,64,1024]{2,1,0:T(8,128)(2,1)} %refs_2_.3, ...), custom_call_target="tpu_custom_call" | custom-call | tf_op jit(solution)/shard_map/fetch_blocks/pallas_call | solution.py:198
  12.3 2.7 %collective-permute-start.1 = (bf16[384,1024]{1,0:T(8,128)(2,1)S(1)}, bf16[384,1024]{1,0:T(8,128)(2,1)S(1)}, u32[]{:S(2)}, u32[]{:S(2)}) collective-permute-start(bf16[384,1024]{1,0:T(8,128)(2,1)S(1)} %pack_rows.2.refs_4_.x.refs_0_), channel_id=1, source_target_pairs={{0,4},{4,8},{8,12},{12,14},{14,10},{10,6},{6,2},{2,0},{1,5},{5,9},... | collective-permute-start | bytes 2359304 | tf_op jit(solution)/shard_map/gather_up_1/ppermute | solution.py:36
  17.3 3.1 %shares.4 = f32[1,384,1024]{2,1,0:T(8,128)S(1)} custom-call(s32[8]{0:T(128)S(1)} %stack.39.where, bf16[384,1024]{1,0:T(8,128)(2,1)S(1)} %pack_rows.3.x_ref.v, bf16[1024,8192]{1,0:T(8,128)(2,1)} %w_ref.5), custom_call_target="tpu_custom_call" | custom-call | tf_op jit(solution)/shard_map/shares/pallas_call | solution.py:293
  20.6 4.1 %shares.3 = f32[2,384,1024]{2,1,0:T(8,128)S(1)} custom-call(s32[8]{0:T(128)S(1)} %stack.39.where, bf16[384,1024]{1,0:T(8,128)(2,1)S(1)} %pack_rows.3.x_ref.v, bf16[1024,8192]{1,0:T(8,128)(2,1)} %w_ref.5), custom_call_target="tpu_custom_call" | custom-call | tf_op jit(solution)/shard_map/shares/pallas_call | solution.py:293
  27.0 3.6 %down_rows.1 = f32[384,128]{1,0:T(8,128)S(1)} custom-call(s32[4]{0:T(128)S(1)} %copy-done.3, s32[1]{0:T(128)} %bitcast.place, bf16[384,1024]{1,0:T(8,128)(2,1)S(1)} %pack_rows.2.refs_4_.x.refs_0_, bf16[384,1024]{1,0:T(8,128)(2,1)S(1)} %pack_rows.3.x_ref.v, bf16[4,256,1024]{2,1,0:T(8,128)(2,1)S(1)} %fetch_blocks.1.own, ...), custom_call_target="tpu_custom_call" | custom-call | tf_op jit(solution)/shard_map/down_rows/pallas_call | solution.py:233
  37.4 11.6 %shares.5 = f32[5,384,1024]{2,1,0:T(8,128)} custom-call(s32[8]{0:T(128)S(1)} %stack.39.where, bf16[384,1024]{1,0:T(8,128)(2,1)S(1)} %pack_rows.3.x_ref.v, bf16[1024,8192]{1,0:T(8,128)(2,1)} %w_ref.5), custom_call_target="tpu_custom_call" | custom-call | tf_op jit(solution)/shard_map/shares/pallas_call | solution.py:293
  49.0 5.4 %add_products.4.refs_4_ = f32[384,1024]{1,0:T(8,128)S(1)} custom-call(s32[8]{0:T(128)S(1)} %stack.39.where, bf16[384,1024]{1,0:T(8,128)(2,1)S(1)} %pack_rows.2.refs_4_.x.refs_0_, bf16[384,1024]{1,0:T(8,128)(2,1)S(1)} %collective-permute-done.3.refs_1_, bf16[384,1024]{1,0:T(8,128)(2,1)S(1)} %collective-permute-done.1.refs_2_, bf16[8192,1024]{1,0:T(8,128)(2,1)} %refs_1_.3, ...), custom_call_target="tpu_custom_call" | custom-call | tf_op jit(solution)/shard_map/add_products/pallas_call | solution.py:329
  62.3 4.3 %add_products.5.refs_4_ = f32[384,1024]{1,0:T(8,128)S(1)} custom-call(s32[8]{0:T(128)S(1)} %stack.39.where, bf16[384,1024]{1,0:T(8,128)(2,1)S(1)} %collective-permute-done.8.refs_0_, bf16[384,1024]{1,0:T(8,128)(2,1)S(1)} %collective-permute-done.4.refs_1_, bf16[8192,1024]{1,0:T(8,128)(2,1)} %refs_1_.3, bf16[8192,1024]{1,0:T(8,128)(2,1)} %refs_1_.3, ...), custom_call_target="tpu_custom_call" | custom-call | tf_op jit(solution)/shard_map/add_products/pallas_call | solution.py:329
  67.1 10.5 %collective-permute-done.10 = f16[384,1024]{1,0:T(8,128)(2,1)S(1)} collective-permute-done((f16[384,1024]{1,0:T(8,128)(2,1)S(1)}, f16[384,1024]{1,0:T(8,128)(2,1)S(1)}, u32[]{:S(2)}, u32[]{:S(2)}) %collective-permute-start.10) | collective-permute-done | bytes 786464 | tf_op jit(solution)/shard_map/scatter_up_2/ppermute | solution.py:36
  79.6 2.6 %fusion.9 = (f16[384,1024]{1,0:T(8,128)(2,1)S(1)}, f16[384,1024]{1,0:T(8,128)(2,1)S(1)}) fusion(f32[5,384,1024]{2,1,0:T(8,128)} %shares.5, f16[384,1024]{1,0:T(8,128)(2,1)S(1)} %collective-permute-done.11, f16[384,1024]{1,0:T(8,128)(2,1)S(1)} %collective-permute-done.10), kind=kLoop, calls=%fused_computation.13 | loop fusion | flops 3932160 | bytes 6291456 | tf_op jit(solution)/shard_map/convert_element_type | solution.py:346
  84.3 2.7 %collective-permute-start.17 = (f16[384,128]{1,0:T(8,128)(2,1)S(1)}, f16[384,128]{1,0:T(8,128)(2,1)S(1)}, u32[]{:S(2)}, u32[]{:S(2)}) collective-permute-start(f16[384,128]{1,0:T(8,128)(2,1)S(1)} %multiply_convert_fusion.1), channel_id=1, source_target_pairs={{0,8},{2,10},{4,12},{6,14},{8,0},{10,2},{12,4},{14,6},{1,9},{3,11}... | collective-permute-start | bytes 294920 | tf_op jit(solution)/shard_map/down_sums_4/ppermute | solution.py:36
  87.0 7.4 %collective-permute-done.9.refs_1_ = bf16[384,1024]{1,0:T(8,128)(2,1)S(1)} collective-permute-done((bf16[384,1024]{1,0:T(8,128)(2,1)S(1)}, bf16[384,1024]{1,0:T(8,128)(2,1)S(1)}, u32[]{:S(2)}, u32[]{:S(2)}) %collective-permute-start.9) | collective-permute-done | bytes 786464 | tf_op jit(solution)/shard_map/gather_up_3/ppermute | solution.py:36
  96.5 4.3 %add_products.6.refs_2_ = f32[384,1024]{1,0:T(8,128)S(1)} custom-call(s32[8]{0:T(128)S(1)} %stack.39.where, bf16[384,1024]{1,0:T(8,128)(2,1)S(1)} %collective-permute-done.13.refs_0_, bf16[384,1024]{1,0:T(8,128)(2,1)S(1)} %collective-permute-done.9.refs_1_, bf16[8192,1024]{1,0:T(8,128)(2,1)} %refs_1_.3, bf16[8192,1024]{1,0:T(8,128)(2,1)} %refs_1_.3, ...), custom_call_target="tpu_custom_call" | custom-call | tf_op jit(solution)/shard_map/add_products/pallas_call | solution.py:329
  102.9 8.3 %collective-permute-done.15 = f16[384,1024]{1,0:T(8,128)(2,1)S(1)} collective-permute-done((f16[384,1024]{1,0:T(8,128)(2,1)S(1)}, f16[384,1024]{1,0:T(8,128)(2,1)S(1)}, u32[]{:S(2)}, u32[]{:S(2)}) %collective-permute-start.15) | collective-permute-done | bytes 786464 | tf_op jit(solution)/shard_map/scatter_up_3/ppermute | solution.py:36
  111.2 3.9 %collective-permute-done.17 = f16[384,128]{1,0:T(8,128)(2,1)S(1)} collective-permute-done((f16[384,128]{1,0:T(8,128)(2,1)S(1)}, f16[384,128]{1,0:T(8,128)(2,1)S(1)}, u32[]{:S(2)}, u32[]{:S(2)}) %collective-permute-start.17) | collective-permute-done | bytes 98336 | tf_op jit(solution)/shard_map/down_sums_4/ppermute | solution.py:36
  115.4 2.6 %fusion.3 = (f16[384,1024]{1,0:T(8,128)(2,1)S(1)}, f16[384,1024]{1,0:T(8,128)(2,1)S(1)}) fusion(f32[5,384,1024]{2,1,0:T(8,128)} %shares.5, f16[384,1024]{1,0:T(8,128)(2,1)S(1)} %collective-permute-done.16, f16[384,1024]{1,0:T(8,128)(2,1)S(1)} %collective-permute-done.15), kind=kLoop, calls=%fused_computation.5 | loop fusion | flops 3932160 | bytes 6291456 | tf_op jit(solution)/shard_map/convert_element_type | solution.py:346
  118.0 2.7 %collective-permute-start.20 = (f16[384,1024]{1,0:T(8,128)(2,1)S(1)}, f16[384,1024]{1,0:T(8,128)(2,1)S(1)}, u32[]{:S(2)}, u32[]{:S(2)}) collective-permute-start(f16[384,1024]{1,0:T(8,128)(2,1)S(1)} %get-tuple-element.83), channel_id=1, source_target_pairs={{0,4},{4,8},{8,12},{12,14},{14,10},{10,6},{6,2},{2,0},{1,5},{5,9},... | collective-permute-start | bytes 2359304 | tf_op jit(solution)/shard_map/scatter_up_4/ppermute | solution.py:36
  121.4 2.5 %collective-permute-done.18 = bf16[192,1024]{1,0:T(8,128)(2,1)S(1)} collective-permute-done((bf16[192,1024]{1,0:T(8,128)(2,1)S(1)}, bf16[192,1024]{1,0:T(8,128)(2,1)S(1)}, u32[]{:S(2)}, u32[]{:S(2)}) %collective-permute-start.18) | collective-permute-done | bytes 393248 | tf_op jit(solution)/shard_map/gather_down_4/ppermute | solution.py:36
  123.9 2.8 %up_rows.1 = (f32[384,1024]{1,0:T(8,128)S(1)}, f32[384,1024]{1,0:T(8,128)S(1)}) custom-call(s32[4]{0:T(128)S(1)} %copy-done.3, s32[1]{0:T(128)} %bitcast.place, f32[384,128]{1,0:T(8,128)S(1)} %add_multiply_fusion.low, bf16[4,256,1024]{2,1,0:T(8,128)(2,1)S(1)} %fetch_blocks.1.own, bf16[4,256,1024]{2,1,0:T(8,128)(2,1)} %collective-permute-done.2.other), custom_call_target="tpu_custom_call" | custom-call | tf_op jit(solution)/shard_map/up_rows/pallas_call | solution.py:271
  126.7 3.0 %add_products.7.x_ref = bf16[384,1024]{1,0:T(8,128)(2,1)S(1)} custom-call(s32[8]{0:T(128)S(1)} %stack.39.where, bf16[384,1024]{1,0:T(8,128)(2,1)S(1)} %constant_dynamic-update-slice_fusion.refs_0_, bf16[8192,1024]{1,0:T(8,128)(2,1)} %refs_1_.3, f32[384,1024]{1,0:T(8,128)S(1)} %add_products.6.refs_2_, f32[384,1024]{1,0:T(8,128)S(1)} %get-tuple-element.77.refs_3_), custom_call_target="tpu_custom_call" | custom-call | tf_op jit(solution)/shard_map/add_products/pallas_call | solution.py:329
  131.6 2.5 %unpack_rows.2 = bf16[512,1024]{1,0:T(8,128)(2,1)} custom-call(s32[4]{0:T(128)S(1)} %copy-done.3, s32[1]{0:T(128)} %bitcast.place, bf16[384,1024]{1,0:T(8,128)(2,1)S(1)} %add_products.7.x_ref, bf16[128,1024]{1,0:T(8,128)(2,1)S(1)} %collective-permute-done.19.spare_ref), custom_call_target="tpu_custom_call" | custom-call | tf_op jit(solution)/shard_map/unpack_rows/pallas_call | solution.py:157
  134.1 3.6 %collective-permute-done.20 = f16[384,1024]{1,0:T(8,128)(2,1)S(1)} collective-permute-done((f16[384,1024]{1,0:T(8,128)(2,1)S(1)}, f16[384,1024]{1,0:T(8,128)(2,1)S(1)}, u32[]{:S(2)}, u32[]{:S(2)}) %collective-permute-start.20) | collective-permute-done | bytes 786464 | tf_op jit(solution)/shard_map/scatter_up_4/ppermute | solution.py:36
  141.6 2.5 %unpack_rows.3 = bf16[512,1024]{1,0:T(8,128)(2,1)} custom-call(s32[4]{0:T(128)S(1)} %copy-done.3, s32[1]{0:T(128)} %bitcast.place, bf16[384,1024]{1,0:T(8,128)(2,1)S(1)} %add_convert_fusion.x_ref, bf16[128,1024]{1,0:T(8,128)(2,1)S(1)} %collective-permute-done.22.spare_ref), custom_call_target="tpu_custom_call" | custom-call | tf_op jit(solution)/shard_map/unpack_rows/pallas_call | solution.py:157
  (72 shorter events, 40.6 us)
Async XLA Ops:
  0.6 7.5 %copy-start.4 = (s32[4]{0:T(128)S(1)}, s32[4]{0:T(128)}, u32[]{:S(2)}) copy-start(s32[4]{0:T(128)} %adapter_of.1) | copy-start | bytes 52
  3.6 2.2 %collective-permute-start = (bf16[256,1024]{1,0:T(8,128)(2,1)}, bf16[256,1024]{1,0:T(8,128)(2,1)S(1)}, u32[]{:S(2)}, u32[]{:S(2)}) collective-permute-start(bf16[256,1024]{1,0:T(8,128)(2,1)} %spare_rows.1), channel_id=1, source_target_pairs={{0,1},{1,0},{2,3},{3,2},{4,5},{5,4},{6,7},{7,6},{8,9},{9,8},{10,11... | collective-permute-start | bytes 1572872 | tf_op jit(solution)/shard_map/ppermute | solution.py:40
  11.7 15.3 %collective-permute-start.2 = (bf16[4,256,1024]{2,1,0:T(8,128)(2,1)S(1)}, bf16[4,256,1024]{2,1,0:T(8,128)(2,1)}, u32[]{:S(2)}, u32[]{:S(2)}) collective-permute-start(bf16[4,256,1024]{2,1,0:T(8,128)(2,1)S(1)} %fetch_blocks.1.own), channel_id=1, source_target_pairs={{0,1},{1,0},{2,3},{3,2},{4,5},{5,4},{6,7},{7,6},{8,9},{9,8},{10,11... | collective-permute-start | bytes 6291464 | tf_op jit(solution)/shard_map/ppermute | solution.py:40
  12.3 21.0 %collective-permute-start.1 = (bf16[384,1024]{1,0:T(8,128)(2,1)S(1)}, bf16[384,1024]{1,0:T(8,128)(2,1)S(1)}, u32[]{:S(2)}, u32[]{:S(2)}) collective-permute-start(bf16[384,1024]{1,0:T(8,128)(2,1)S(1)} %pack_rows.2.refs_4_.x.refs_0_), channel_id=1, source_target_pairs={{0,4},{4,8},{8,12},{12,14},{14,10},{10,6},{6,2},{2,0},{1,5},{5,9},... | collective-permute-start | bytes 2359304 | tf_op jit(solution)/shard_map/gather_up_1/ppermute | solution.py:36
  15.0 20.4 %collective-permute-start.3 = (bf16[384,1024]{1,0:T(8,128)(2,1)S(1)}, bf16[384,1024]{1,0:T(8,128)(2,1)S(1)}, u32[]{:S(2)}, u32[]{:S(2)}) collective-permute-start(bf16[384,1024]{1,0:T(8,128)(2,1)S(1)} %pack_rows.2.refs_4_.x.refs_0_), channel_id=1, source_target_pairs={{4,0},{8,4},{12,8},{14,12},{10,14},{6,10},{2,6},{0,2},{5,1},{9,5},... | collective-permute-start | bytes 2359304 | tf_op jit(solution)/shard_map/gather_down_1/ppermute | solution.py:36
  24.9 29.5 %collective-permute-start.5 = (f16[192,1024]{1,0:T(8,128)(2,1)S(1)}, f16[192,1024]{1,0:T(8,128)(2,1)S(1)}, u32[]{:S(2)}, u32[]{:S(2)}) collective-permute-start(f16[192,1024]{1,0:T(8,128)(2,1)S(1)} %get-tuple-element.91), channel_id=1, source_target_pairs={{0,4},{4,8},{8,12},{12,14},{14,10},{10,6},{6,2},{2,0},{1,5},{5,9},... | collective-permute-start | bytes 1179656 | tf_op jit(solution)/shard_map/scatter_up_1/ppermute | solution.py:36
  27.0 27.4 %collective-permute-start.6 = (f16[192,1024]{1,0:T(8,128)(2,1)S(1)}, f16[192,1024]{1,0:T(8,128)(2,1)S(1)}, u32[]{:S(2)}, u32[]{:S(2)}) collective-permute-start(f16[192,1024]{1,0:T(8,128)(2,1)S(1)} %get-tuple-element.90), channel_id=1, source_target_pairs={{4,0},{8,4},{12,8},{14,12},{10,14},{6,10},{2,6},{0,2},{5,1},{9,5},... | collective-permute-start | bytes 1179656 | tf_op jit(solution)/shard_map/scatter_down_1/ppermute | solution.py:36
  30.6 23.8 %collective-permute-start.7 = (f16[384,128]{1,0:T(8,128)(2,1)S(1)}, f16[384,128]{1,0:T(8,128)(2,1)S(1)}, u32[]{:S(2)}, u32[]{:S(2)}) collective-permute-start(f16[384,128]{1,0:T(8,128)(2,1)S(1)} %multiply_convert_fusion.3), channel_id=1, source_target_pairs={{0,2},{2,0},{4,6},{6,4},{8,10},{10,8},{12,14},{14,12},{1,3},{3,1},... | collective-permute-start | bytes 294920 | tf_op jit(solution)/shard_map/down_sums_1/ppermute | solution.py:36
  35.4 25.3 %collective-permute-start.4 = (bf16[384,1024]{1,0:T(8,128)(2,1)S(1)}, bf16[384,1024]{1,0:T(8,128)(2,1)S(1)}, u32[]{:S(2)}, u32[]{:S(2)}) collective-permute-start(bf16[384,1024]{1,0:T(8,128)(2,1)S(1)} %collective-permute-done.1.refs_2_), channel_id=1, source_target_pairs={{0,4},{4,8},{8,12},{12,14},{14,10},{10,6},{6,2},{2,0},{1,5},{5,9},... | collective-permute-start | bytes 2359304 | tf_op jit(solution)/shard_map/gather_up_2/ppermute | solution.py:36
  37.0 23.7 %collective-permute-start.8 = (bf16[384,1024]{1,0:T(8,128)(2,1)S(1)}, bf16[384,1024]{1,0:T(8,128)(2,1)S(1)}, u32[]{:S(2)}, u32[]{:S(2)}) collective-permute-start(bf16[384,1024]{1,0:T(8,128)(2,1)S(1)} %collective-permute-done.3.refs_1_), channel_id=1, source_target_pairs={{4,0},{8,4},{12,8},{14,12},{10,14},{6,10},{2,6},{0,2},{5,1},{9,5},... | collective-permute-start | bytes 2359304 | tf_op jit(solution)/shard_map/gather_down_2/ppermute | solution.py:36
  54.8 22.7 %collective-permute-start.10 = (f16[384,1024]{1,0:T(8,128)(2,1)S(1)}, f16[384,1024]{1,0:T(8,128)(2,1)S(1)}, u32[]{:S(2)}, u32[]{:S(2)}) collective-permute-start(f16[384,1024]{1,0:T(8,128)(2,1)S(1)} %fusion.13), channel_id=1, source_target_pairs={{0,4},{4,8},{8,12},{12,14},{14,10},{10,6},{6,2},{2,0},{1,5},{5,9},... | collective-permute-start | bytes 2359304 | tf_op jit(solution)/shard_map/scatter_up_2/ppermute | solution.py:36
  56.6 23.0 %collective-permute-start.11 = (f16[384,1024]{1,0:T(8,128)(2,1)S(1)}, f16[384,1024]{1,0:T(8,128)(2,1)S(1)}, u32[]{:S(2)}, u32[]{:S(2)}) collective-permute-start(f16[384,1024]{1,0:T(8,128)(2,1)S(1)} %fusion.14), channel_id=1, source_target_pairs={{4,0},{8,4},{12,8},{14,12},{10,14},{6,10},{2,6},{0,2},{5,1},{9,5},... | collective-permute-start | bytes 2359304 | tf_op jit(solution)/shard_map/scatter_down_2/ppermute | solution.py:36
  57.2 22.4 %collective-permute-start.12 = (f16[384,128]{1,0:T(8,128)(2,1)S(1)}, f16[384,128]{1,0:T(8,128)(2,1)S(1)}, u32[]{:S(2)}, u32[]{:S(2)}) collective-permute-start(f16[384,128]{1,0:T(8,128)(2,1)S(1)} %multiply_convert_fusion.2), channel_id=1, source_target_pairs={{0,4},{2,6},{4,0},{6,2},{8,12},{10,14},{12,8},{14,10},{1,5},{3,7},... | collective-permute-start | bytes 294920 | tf_op jit(solution)/shard_map/down_sums_2/ppermute | solution.py:36
  60.7 33.7 %collective-permute-start.9 = (bf16[384,1024]{1,0:T(8,128)(2,1)S(1)}, bf16[384,1024]{1,0:T(8,128)(2,1)S(1)}, u32[]{:S(2)}, u32[]{:S(2)}) collective-permute-start(bf16[384,1024]{1,0:T(8,128)(2,1)S(1)} %collective-permute-done.4.refs_1_), channel_id=1, source_target_pairs={{0,4},{4,8},{8,12},{12,14},{14,10},{10,6},{6,2},{2,0},{1,5},{5,9},... | collective-permute-start | bytes 2359304 | tf_op jit(solution)/shard_map/gather_up_3/ppermute | solution.py:36
  66.5 30.0 %collective-permute-start.13 = (bf16[384,1024]{1,0:T(8,128)(2,1)S(1)}, bf16[384,1024]{1,0:T(8,128)(2,1)S(1)}, u32[]{:S(2)}, u32[]{:S(2)}) collective-permute-start(bf16[384,1024]{1,0:T(8,128)(2,1)S(1)} %collective-permute-done.8.refs_0_), channel_id=1, source_target_pairs={{4,0},{8,4},{12,8},{14,12},{10,14},{6,10},{2,6},{0,2},{5,1},{9,5},... | collective-permute-start | bytes 2359304 | tf_op jit(solution)/shard_map/gather_down_3/ppermute | solution.py:36
  82.2 29.1 %collective-permute-start.15 = (f16[384,1024]{1,0:T(8,128)(2,1)S(1)}, f16[384,1024]{1,0:T(8,128)(2,1)S(1)}, u32[]{:S(2)}, u32[]{:S(2)}) collective-permute-start(f16[384,1024]{1,0:T(8,128)(2,1)S(1)} %get-tuple-element.85), channel_id=1, source_target_pairs={{0,4},{4,8},{8,12},{12,14},{14,10},{10,6},{6,2},{2,0},{1,5},{5,9},... | collective-permute-start | bytes 2359304 | tf_op jit(solution)/shard_map/scatter_up_3/ppermute | solution.py:36
  82.3 33.2 %collective-permute-start.16 = (f16[384,1024]{1,0:T(8,128)(2,1)S(1)}, f16[384,1024]{1,0:T(8,128)(2,1)S(1)}, u32[]{:S(2)}, u32[]{:S(2)}) collective-permute-start(f16[384,1024]{1,0:T(8,128)(2,1)S(1)} %get-tuple-element.84), channel_id=1, source_target_pairs={{4,0},{8,4},{12,8},{14,12},{10,14},{6,10},{2,6},{0,2},{5,1},{9,5},... | collective-permute-start | bytes 2359304 | tf_op jit(solution)/shard_map/scatter_down_3/ppermute | solution.py:36
  84.3 30.8 %collective-permute-start.17 = (f16[384,128]{1,0:T(8,128)(2,1)S(1)}, f16[384,128]{1,0:T(8,128)(2,1)S(1)}, u32[]{:S(2)}, u32[]{:S(2)}) collective-permute-start(f16[384,128]{1,0:T(8,128)(2,1)S(1)} %multiply_convert_fusion.1), channel_id=1, source_target_pairs={{0,8},{2,10},{4,12},{6,14},{8,0},{10,2},{12,4},{14,6},{1,9},{3,11}... | collective-permute-start | bytes 294920 | tf_op jit(solution)/shard_map/down_sums_4/ppermute | solution.py:36
  100.8 20.6 %collective-permute-start.14 = (bf16[192,1024]{1,0:T(8,128)(2,1)S(1)}, bf16[192,1024]{1,0:T(8,128)(2,1)S(1)}, u32[]{:S(2)}, u32[]{:S(2)}) collective-permute-start(bf16[192,1024]{1,0:T(8,128)(2,1)S(1)} %slice.89), channel_id=1, source_target_pairs={{0,4},{4,8},{8,12},{12,14},{14,10},{10,6},{6,2},{2,0},{1,5},{5,9},... | collective-permute-start | bytes 1179656 | tf_op jit(solution)/shard_map/gather_up_4/ppermute | solution.py:36
  100.9 23.0 %collective-permute-start.18 = (bf16[192,1024]{1,0:T(8,128)(2,1)S(1)}, bf16[192,1024]{1,0:T(8,128)(2,1)S(1)}, u32[]{:S(2)}, u32[]{:S(2)}) collective-permute-start(bf16[192,1024]{1,0:T(8,128)(2,1)S(1)} %slice.92), channel_id=1, source_target_pairs={{4,0},{8,4},{12,8},{14,12},{10,14},{6,10},{2,6},{0,2},{5,1},{9,5},... | collective-permute-start | bytes 1179656 | tf_op jit(solution)/shard_map/gather_down_4/ppermute | solution.py:36
  118.0 19.6 %collective-permute-start.20 = (f16[384,1024]{1,0:T(8,128)(2,1)S(1)}, f16[384,1024]{1,0:T(8,128)(2,1)S(1)}, u32[]{:S(2)}, u32[]{:S(2)}) collective-permute-start(f16[384,1024]{1,0:T(8,128)(2,1)S(1)} %get-tuple-element.83), channel_id=1, source_target_pairs={{0,4},{4,8},{8,12},{12,14},{14,10},{10,6},{6,2},{2,0},{1,5},{5,9},... | collective-permute-start | bytes 2359304 | tf_op jit(solution)/shard_map/scatter_up_4/ppermute | solution.py:36
  120.7 19.1 %collective-permute-start.21 = (f16[384,1024]{1,0:T(8,128)(2,1)S(1)}, f16[384,1024]{1,0:T(8,128)(2,1)S(1)}, u32[]{:S(2)}, u32[]{:S(2)}) collective-permute-start(f16[384,1024]{1,0:T(8,128)(2,1)S(1)} %get-tuple-element.82), channel_id=1, source_target_pairs={{4,0},{8,4},{12,8},{14,12},{10,14},{6,10},{2,6},{0,2},{5,1},{9,5},... | collective-permute-start | bytes 2359304 | tf_op jit(solution)/shard_map/scatter_down_4/ppermute | solution.py:36
  129.8 1.8 %collective-permute-start.19 = (bf16[128,1024]{1,0:T(8,128)(2,1)S(1)}, bf16[128,1024]{1,0:T(8,128)(2,1)S(1)}, u32[]{:S(2)}, u32[]{:S(2)}) collective-permute-start(bf16[128,1024]{1,0:T(8,128)(2,1)S(1)} %slice.108), channel_id=1, source_target_pairs={{0,1},{1,0},{2,3},{3,2},{4,5},{5,4},{6,7},{7,6},{8,9},{9,8},{10,11... | collective-permute-start | bytes 786440 | tf_op jit(solution)/shard_map/ppermute | solution.py:40
  140.0 1.6 %collective-permute-start.22 = (bf16[128,1024]{1,0:T(8,128)(2,1)S(1)}, bf16[128,1024]{1,0:T(8,128)(2,1)S(1)}, u32[]{:S(2)}, u32[]{:S(2)}) collective-permute-start(bf16[128,1024]{1,0:T(8,128)(2,1)S(1)} %fusion.18), channel_id=1, source_target_pairs={{0,1},{1,0},{2,3},{3,2},{4,5},{5,4},{6,7},{7,6},{8,9},{9,8},{10,11... | collective-permute-start | bytes 786440 | tf_op jit(solution)/shard_map/ppermute | solution.py:40
  (5 other events, 16.7 us)

commit v6 on v5

--- a/solution.py
+++ b/solution.py
@@ -179,12 +179,13 @@
 
 
 def fetch_kernel(held, adapter_of, location, place, *refs):
-    stores, out = refs[:4], refs[-1]
+    count = (len(refs) - 1) // 2
+    stores, outs = refs[:count], refs[count + 1 :]
     slot = location[adapter_of[pl.program_id(0)]] - place[0] * held
     mine = (slot >= 0) & (slot < held)
-    for k, table in enumerate(stores):
+    for table, out in zip(stores, outs):
         block = table[0]
-        out[k] = jnp.where(mine, block, jnp.zeros_like(block))
+        out[...] = jnp.where(mine, block, jnp.zeros_like(block))
 
 
 def fetch(stores, adapter_of, location, place, after):
@@ -200,63 +201,64 @@
         grid_spec=pltpu.PrefetchScalarGridSpec(
             num_scalar_prefetch=3,
             grid=(requests,),
-            in_specs=[pl.BlockSpec((1, rank, width), at)] * 4 + [pl.BlockSpec(memory_space=pl.ANY)],
-            out_specs=pl.BlockSpec((4, rank, width), lambda i, *_: (0, i, 0)),
-        ),
-        out_shape=jax.ShapeDtypeStruct((4, requests * rank, width), BF16),
+            in_specs=[pl.BlockSpec((1, rank, width), at)] * len(stores)
+            + [pl.BlockSpec(memory_space=pl.ANY)],
+            out_specs=[pl.BlockSpec((rank, width), lambda i, *_: (i, 0))] * len(stores),
+        ),
+        out_shape=[jax.ShapeDtypeStruct((requests * rank, width), BF16)] * len(stores),
         compiler_params=params(LARGE),
         name="fetch_blocks",
     )(adapter_of, location, place, *stores, after)
 
 
-def down_kernel(counts, place, x, v, own, other, out, blocks):
+def down_kernel(counts, place, x, v, own_q, own_o, other_q, other_o, out, blocks):
     rank = out.shape[1] // 2
     packed, width = x.shape
-    requests = own.shape[1] // rank
+    requests = own_q.shape[0] // rank
     blocks[...] = jnp.zeros_like(blocks)
     who = request_of(counts, place, iota((packed, 1), 0), packed)
     total = jnp.zeros(out.shape, F32)
     for i in range(requests):
         rows = pl.ds(i * rank, rank)
-        blocks[:rank, :width] = own[0, rows] + other[0, rows]
-        blocks[rank:, width:] = own[1, rows] + other[1, rows]
+        blocks[:rank, :width] = own_q[rows] + other_q[rows]
+        blocks[rank:, width:] = own_o[rows] + other_o[rows]
         got = dot_t(x[...], blocks[:, :width]) + dot_t(v[...], blocks[:, width:])
         total = total + jnp.where(who == i, got, 0.0)
     out[...] = total
 
 
 def down(counts, place, x, v, own, other):
-    requests_rank, width = own.shape[1:]
+    requests_rank, width = own[0].shape
     rank = requests_rank // 4
     packed = x.shape[0]
-    half = (2, requests_rank, width)
+    half = (requests_rank, width)
     return pl.pallas_call(
         down_kernel,
         grid_spec=pltpu.PrefetchScalarGridSpec(
             num_scalar_prefetch=2,
             grid=(1,),
-            in_specs=[whole(v.shape) for v in (x, v)] + [whole(half)] * 2,
+            in_specs=[whole(v.shape) for v in (x, v)] + [whole(half)] * 4,
             out_specs=whole((packed, 2 * rank)),
             scratch_shapes=[pltpu.VMEM((2 * rank, 2 * width), BF16)],
         ),
         out_shape=jax.ShapeDtypeStruct((packed, 2 * rank), F32),
         compiler_params=params(),
         name="down_rows",
-    )(counts, place, x, v, own, other)
-
-
-def up_kernel(counts, place, low, own, other, q_ref, o_ref, blocks):
+    )(counts, place, x, v, *own, *other)
+
+
+def up_kernel(counts, place, low, own_q, own_o, other_q, other_o, q_ref, o_ref, blocks):
     packed, both = low.shape
     rank = both // 2
     width = q_ref.shape[1]
-    requests = own.shape[1] // rank
+    requests = own_q.shape[0] // rank
     blocks[...] = jnp.zeros_like(blocks)
     who = request_of(counts, place, iota((packed, 1), 0), packed)
     rows_low = low[...].astype(BF16).astype(F32)
     for i in range(requests):
         rows = pl.ds(i * rank, rank)
-        blocks[pl.ds(2 * i * rank, rank), :width] = own[0, rows] + other[0, rows]
-        blocks[pl.ds((2 * i + 1) * rank, rank), width:] = own[1, rows] + other[1, rows]
+        blocks[pl.ds(2 * i * rank, rank), :width] = own_q[rows] + other_q[rows]
+        blocks[pl.ds((2 * i + 1) * rank, rank), width:] = own_o[rows] + other_o[rows]
     wide = jnp.concatenate(
         [jnp.where(who == i, rows_low, 0.0).astype(BF16) for i in range(requests)], axis=1
     )
@@ -266,22 +268,22 @@
 
 def up(counts, place, low, own, other):
     packed, both = low.shape
-    requests_rank, width = own.shape[1:]
-    half = (2, requests_rank, width)
+    requests_rank, width = own[0].shape
+    half = (requests_rank, width)
     return pl.pallas_call(
         up_kernel,
         grid_spec=pltpu.PrefetchScalarGridSpec(
             num_scalar_prefetch=2,
             grid=(1,),
             in_specs=[whole(low.shape)]
-            + [pl.BlockSpec(half, lambda *_: (1, 0, 0))] * 2,
+            + [whole(half)] * 4,
             out_specs=[whole((packed, width))] * 2,
             scratch_shapes=[pltpu.VMEM((2 * requests_rank, 2 * width), BF16)],
         ),
         out_shape=[jax.ShapeDtypeStruct((packed, width), F32)] * 2,
         compiler_params=params(),
         name="up_rows",
-    )(counts, place, low, own, other)
+    )(counts, place, low, *own, *other)
 
 
 def shares_kernel(where, x_ref, w_ref, out):
@@ -397,9 +399,8 @@
         far = narrow(farthest[0])
         up_sum = send(far[:half], following, "scatter_up_1")
         down_sum = send(far[half:], preceding, "scatter_down_1")
-        stores = (store_aq, store_ao, store_bq, store_bo)
-        mine = fetch(stores, adapter_of, location, place, tok)
-        theirs = other_replica(mine)
+        mine = fetch((store_aq, store_ao), adapter_of, location, place, tok)
+        theirs = [other_replica(blocks) for blocks in mine]
         near = shares(tie(where, mine), size - 3, 2, ctx, output_weight)
         parts = down(counts, place, tok, tie(ctx, near), mine, theirs)
         bits = [1 << i for i in range(size.bit_length() - 1)]
@@ -412,14 +413,18 @@
                 ahead = send(got_up, following, f"gather_up_{step + 1}")
                 behind = send(got_down, preceding, f"gather_down_{step + 1}")
             else:
-                ahead = send(got_up[:half], following, f"gather_up_{step + 1}")
-                behind = send(got_down[half:], preceding, f"gather_down_{step + 1}")
+                up_half, down_half = lax.optimization_barrier((got_up[:half], got_down[half:]))
+                ahead = send(up_half, following, f"gather_up_{step + 1}")
+                behind = send(down_half, preceding, f"gather_down_{step + 1}")
+                rest = tie(rest, up_half, down_half)
             if step == 1:
                 rest = shares(where, 0, size - 3, tie(ctx, got_up, got_down), output_weight)
                 pieces, at_pieces, sofar = [tok, got_down, got_up], [0, 1, 2], []
             else:
                 pieces, at_pieces, sofar = [got_down, got_up], [2 * step - 1, 2 * step], [q]
             q = add_products(tie(where, rest), pieces, at_pieces, query_weight, sofar)
+            if step == 2:
+                mine = fetch((store_bq, store_bo), adapter_of, location, place, q)
             up_sum, down_sum, swapped = lax.optimization_barrier((tie(up_sum, q), down_sum, swapped))
             if swapped is not None:
                 parts = meet(*swapped)
@@ -438,6 +443,7 @@
             up_sum = send(up_out, following, f"scatter_up_{step + 1}")
             down_sum = send(down_out, preceding, f"scatter_down_{step + 1}")
             ready = (up_out, down_out)
+        theirs = [other_replica(tie(blocks, up_out, down_out)) for blocks in mine]
         got_up, got_down, swapped = lax.optimization_barrier((tie(ahead, ready), behind, swapped))
         if swapped is not None:
             parts = meet(*swapped)

time: 144 us -> 140 us (0.972)
  waiting for transfers between devices: 50.7 us -> 46 us
  starting transfers between devices: 25.3 us -> 28.7 us
  Pallas kernels: 55.3 us -> 53.2 us
    ppermute x19, waiting for transfers between devices: 47.9 us -> 43.2 us  [send(): return lax.ppermute(value, 'tensor', pairs)]
    ppermute x19, starting transfers between devices: 24.2 us -> 27 us  [send(): return lax.ppermute(value, 'tensor', pairs)]
    unnamed x13 -> x17, local copies, waits for them, and re-layouts: 2.93 us -> 1.65 us
    pallas_call x1 -> x2, Pallas kernels: 3.13 us -> 3.36 us  [fetch(): pl.pallas_call(functools.partial(fetch_kernel, held), grid_spec=pltpu.Pre...]
  transfers between devices with their start and end apart: 23 -> 26, of which waited for: 16 -> 12; matrix products, arithmetic and copies ran while one was open for 6% -> 6% of each run, Pallas kernels for 32% -> 33%
where the time goes in v6:
time: 140 us
  Pallas kernels  53.2 us (38%)
  waiting for transfers between devices  46 us (33%)
  starting transfers between devices  28.7 us (20%)
  other arithmetic  8.58 us (6%)
  local copies, waits for them, and re-layouts  2.13 us (2%)
    ppermute x19, waiting for transfers between devices, send(): return lax.ppermute(value, 'tensor', pairs)  43.2 us
    ppermute x19, starting transfers between devices, send(): return lax.ppermute(value, 'tensor', pairs)  27 us
    pallas_call x3, Pallas kernels, shares(): pl.pallas_call(shares_kernel, grid_spec=pltpu.PrefetchScalarGridSpec(num_...  18.9 us
    pallas_call x4, Pallas kernels, add_products(): pl.pallas_call(functools.partial(add_kernel, len(pieces)), grid_spec=pltp...  16.9 us
    convert_element_type x5, other arithmetic, narrow(): return (value * SUM_SCALE).astype(F16)  5.64 us
    pallas_call x2, Pallas kernels, unpack(): pl.pallas_call(unpack_kernel, grid_spec=pltpu.PrefetchScalarGridSpec(num_...  4.94 us
    pallas_call x2, Pallas kernels, fetch(): pl.pallas_call(functools.partial(fetch_kernel, held), grid_spec=pltpu.Pre...  3.36 us
    pallas_call x1, Pallas kernels, spare_rows(): pl.pallas_call(spare_kernel, grid_spec=pltpu.PrefetchScalarGridSpec(num_s...  2.91 us
  transfers between devices with their start and end apart: 26, of which 12 were waited for; matrix products, arithmetic and copies ran while one was open for 6% of the time, Pallas kernels for 33%

profile of v6, /device:TPU:0, one launch (start us, length us, event | category | flops | bytes accessed | tf_op | source)
XLA Modules:
  0.0 139.6 jit_solution(3200962044169913067)
XLA Ops:
  0.7 2.9 %spare_rows.1 = bf16[256,1024]{1,0:T(8,128)(2,1)} custom-call(s32[4]{0:T(128)} %counts.13, s32[1]{0:T(128)} %bitcast.place, bf16[512,1024]{1,0:T(8,128)(2,1)} %x_ref.4, bf16[512,1024]{1,0:T(8,128)(2,1)} %x_ref.5), custom_call_target="tpu_custom_call" | custom-call | tf_op jit(solution)/shard_map/spare_rows/pallas_call | solution.py:97
  6.9 3.0 %collective-permute-start.1 = (bf16[384,1024]{1,0:T(8,128)(2,1)S(1)}, bf16[384,1024]{1,0:T(8,128)(2,1)S(1)}, u32[]{:S(2)}, u32[]{:S(2)}) collective-permute-start(bf16[384,1024]{1,0:T(8,128)(2,1)S(1)} %pack_rows.2.refs_2_.x.refs_0_), channel_id=1, source_target_pairs={{0,4},{4,8},{8,12},{12,14},{14,10},{10,6},{6,2},{2,0},{1,5},{5,9},... | collective-permute-start | bytes 2359304 | tf_op jit(solution)/shard_map/gather_up_1/ppermute | solution.py:36
  14.0 3.1 %shares.4 = f32[1,384,1024]{2,1,0:T(8,128)S(1)} custom-call(s32[8]{0:T(128)S(1)} %stack.39.where, bf16[384,1024]{1,0:T(8,128)(2,1)S(1)} %pack_rows.3.x_ref.v, bf16[1024,8192]{1,0:T(8,128)(2,1)} %w_ref.5), custom_call_target="tpu_custom_call" | custom-call | tf_op jit(solution)/shard_map/shares/pallas_call | solution.py:295
  17.3 4.1 %shares.3 = f32[2,384,1024]{2,1,0:T(8,128)S(1)} custom-call(s32[8]{0:T(128)S(1)} %stack.39.where, bf16[384,1024]{1,0:T(8,128)(2,1)S(1)} %pack_rows.3.x_ref.v, bf16[1024,8192]{1,0:T(8,128)(2,1)} %w_ref.5), custom_call_target="tpu_custom_call" | custom-call | tf_op jit(solution)/shard_map/shares/pallas_call | solution.py:295
  23.7 2.3 %down_rows.1 = f32[384,128]{1,0:T(8,128)S(1)} custom-call(s32[4]{0:T(128)S(1)} %copy-done.5, s32[1]{0:T(128)} %bitcast.place, bf16[384,1024]{1,0:T(8,128)(2,1)S(1)} %pack_rows.2.refs_2_.x.refs_0_, bf16[384,1024]{1,0:T(8,128)(2,1)S(1)} %pack_rows.3.x_ref.v, bf16[256,1024]{1,0:T(8,128)(2,1)S(1)} %get-tuple-element.53.own_q, ...), custom_call_target="tpu_custom_call" | custom-call | tf_op jit(solution)/shard_map/down_rows/pallas_call | solution.py:235
  32.4 11.6 %shares.5 = f32[5,384,1024]{2,1,0:T(8,128)} custom-call(s32[8]{0:T(128)S(1)} %stack.39.where, bf16[384,1024]{1,0:T(8,128)(2,1)S(1)} %pack_rows.3.x_ref.v, bf16[1024,8192]{1,0:T(8,128)(2,1)} %w_ref.5), custom_call_target="tpu_custom_call" | custom-call | tf_op jit(solution)/shard_map/shares/pallas_call | solution.py:295
  44.0 5.4 %add_products.4.refs_4_ = f32[384,1024]{1,0:T(8,128)S(1)} custom-call(s32[8]{0:T(128)S(1)} %stack.39.where, bf16[384,1024]{1,0:T(8,128)(2,1)S(1)} %pack_rows.2.refs_2_.x.refs_0_, bf16[384,1024]{1,0:T(8,128)(2,1)S(1)} %collective-permute-done.4.refs_1_, bf16[384,1024]{1,0:T(8,128)(2,1)S(1)} %collective-permute-done.1.refs_2_, bf16[8192,1024]{1,0:T(8,128)(2,1)} %refs_1_.5, ...), custom_call_target="tpu_custom_call" | custom-call | tf_op jit(solution)/shard_map/add_products/pallas_call | solution.py:331
  57.2 4.3 %add_products.5.refs_4_.refs_2_ = f32[384,1024]{1,0:T(8,128)S(1)} custom-call(s32[8]{0:T(128)S(1)} %stack.39.where, bf16[384,1024]{1,0:T(8,128)(2,1)S(1)} %collective-permute-done.9.refs_0_, bf16[384,1024]{1,0:T(8,128)(2,1)S(1)} %collective-permute-done.5.refs_1_, bf16[8192,1024]{1,0:T(8,128)(2,1)} %refs_1_.5, bf16[8192,1024]{1,0:T(8,128)(2,1)} %refs_1_.5, ...), custom_call_target="tpu_custom_call" | custom-call | tf_op jit(solution)/shard_map/add_products/pallas_call | solution.py:331
  62.0 10.4 %collective-permute-done.11 = f16[384,1024]{1,0:T(8,128)(2,1)S(1)} collective-permute-done((f16[384,1024]{1,0:T(8,128)(2,1)S(1)}, f16[384,1024]{1,0:T(8,128)(2,1)S(1)}, u32[]{:S(2)}, u32[]{:S(2)}) %collective-permute-start.11) | collective-permute-done | bytes 786464 | tf_op jit(solution)/shard_map/scatter_up_2/ppermute | solution.py:36
  74.6 2.6 %fusion.8 = (f16[384,1024]{1,0:T(8,128)(2,1)S(1)}, f16[384,1024]{1,0:T(8,128)(2,1)S(1)}) fusion(f32[5,384,1024]{2,1,0:T(8,128)} %shares.5, f16[384,1024]{1,0:T(8,128)(2,1)S(1)} %collective-permute-done.12, f16[384,1024]{1,0:T(8,128)(2,1)S(1)} %collective-permute-done.11), kind=kLoop, calls=%fused_computation.11 | loop fusion | flops 3932160 | bytes 6291456 | tf_op jit(solution)/shard_map/convert_element_type | solution.py:348
  79.3 2.6 %collective-permute-start.18 = (f16[384,128]{1,0:T(8,128)(2,1)S(1)}, f16[384,128]{1,0:T(8,128)(2,1)S(1)}, u32[]{:S(2)}, u32[]{:S(2)}) collective-permute-start(f16[384,128]{1,0:T(8,128)(2,1)S(1)} %multiply_convert_fusion.1), channel_id=1, source_target_pairs={{0,8},{2,10},{4,12},{6,14},{8,0},{10,2},{12,4},{14,6},{1,9},{3,11}... | collective-permute-start | bytes 294920 | tf_op jit(solution)/shard_map/down_sums_4/ppermute | solution.py:36
  82.0 7.3 %collective-permute-done.10.refs_1_ = bf16[384,1024]{1,0:T(8,128)(2,1)S(1)} collective-permute-done((bf16[384,1024]{1,0:T(8,128)(2,1)S(1)}, bf16[384,1024]{1,0:T(8,128)(2,1)S(1)}, u32[]{:S(2)}, u32[]{:S(2)}) %collective-permute-start.10) | collective-permute-done | bytes 786464 | tf_op jit(solution)/shard_map/gather_up_3/ppermute | solution.py:36
  91.6 2.6 %fetch_blocks.3 = (bf16[256,1024]{1,0:T(8,128)(2,1)S(1)}, bf16[256,1024]{1,0:T(8,128)(2,1)S(1)}) custom-call(s32[4]{0:T(128)S(1)} %copy-done.6, s32[32]{0:T(128)S(1)} %copy-done.7, s32[1]{0:T(128)} %bitcast.place, bf16[16,64,1024]{2,1,0:T(8,128)(2,1)S(1)} %copy-done.2, bf16[16,64,1024]{2,1,0:T(8,128)(2,1)} %refs_1_.4, ...), custom_call_target="tpu_custom_call" | custom-call | tf_op jit(solution)/shard_map/fetch_blocks/pallas_call | solution.py:199
  96.2 4.3 %add_products.6.refs_2_ = f32[384,1024]{1,0:T(8,128)S(1)} custom-call(s32[8]{0:T(128)S(1)} %stack.39.where, bf16[384,1024]{1,0:T(8,128)(2,1)S(1)} %collective-permute-done.14.refs_0_, bf16[384,1024]{1,0:T(8,128)(2,1)S(1)} %collective-permute-done.10.refs_1_, bf16[8192,1024]{1,0:T(8,128)(2,1)} %refs_1_.5, bf16[8192,1024]{1,0:T(8,128)(2,1)} %refs_1_.5, ...), custom_call_target="tpu_custom_call" | custom-call | tf_op jit(solution)/shard_map/add_products/pallas_call | solution.py:331
  100.5 5.7 %collective-permute-done.16 = f16[384,1024]{1,0:T(8,128)(2,1)S(1)} collective-permute-done((f16[384,1024]{1,0:T(8,128)(2,1)S(1)}, f16[384,1024]{1,0:T(8,128)(2,1)S(1)}, u32[]{:S(2)}, u32[]{:S(2)}) %collective-permute-start.16) | collective-permute-done | bytes 786464 | tf_op jit(solution)/shard_map/scatter_up_3/ppermute | solution.py:36
  106.1 4.3 %collective-permute-done.18 = f16[384,128]{1,0:T(8,128)(2,1)S(1)} collective-permute-done((f16[384,128]{1,0:T(8,128)(2,1)S(1)}, f16[384,128]{1,0:T(8,128)(2,1)S(1)}, u32[]{:S(2)}, u32[]{:S(2)}) %collective-permute-start.18) | collective-permute-done | bytes 98336 | tf_op jit(solution)/shard_map/down_sums_4/ppermute | solution.py:36
  110.4 2.6 %fusion.2 = (f16[384,1024]{1,0:T(8,128)(2,1)S(1)}, f16[384,1024]{1,0:T(8,128)(2,1)S(1)}) fusion(f32[5,384,1024]{2,1,0:T(8,128)} %shares.5, f16[384,1024]{1,0:T(8,128)(2,1)S(1)} %collective-permute-done.17, f16[384,1024]{1,0:T(8,128)(2,1)S(1)} %collective-permute-done.16), kind=kLoop, calls=%fused_computation.3 | loop fusion | flops 3932160 | bytes 6291456 | tf_op jit(solution)/shard_map/convert_element_type | solution.py:348
  113.6 2.5 %collective-permute-start.23 = (f16[384,1024]{1,0:T(8,128)(2,1)S(1)}, f16[384,1024]{1,0:T(8,128)(2,1)S(1)}, u32[]{:S(2)}, u32[]{:S(2)}) collective-permute-start(f16[384,1024]{1,0:T(8,128)(2,1)S(1)} %get-tuple-element.103), channel_id=1, source_target_pairs={{0,4},{4,8},{8,12},{12,14},{14,10},{10,6},{6,2},{2,0},{1,5},{5,9},... | collective-permute-start | bytes 2359304 | tf_op jit(solution)/shard_map/scatter_up_4/ppermute | solution.py:36
  116.2 2.6 %collective-permute-start.24 = (f16[384,1024]{1,0:T(8,128)(2,1)S(1)}, f16[384,1024]{1,0:T(8,128)(2,1)S(1)}, u32[]{:S(2)}, u32[]{:S(2)}) collective-permute-start(f16[384,1024]{1,0:T(8,128)(2,1)S(1)} %get-tuple-element.102), channel_id=1, source_target_pairs={{4,0},{8,4},{12,8},{14,12},{10,14},{6,10},{2,6},{0,2},{5,1},{9,5},... | collective-permute-start | bytes 2359304 | tf_op jit(solution)/shard_map/scatter_down_4/ppermute | solution.py:36
  120.4 3.0 %add_products.7.x_ref = bf16[384,1024]{1,0:T(8,128)(2,1)S(1)} custom-call(s32[8]{0:T(128)S(1)} %stack.39.where, bf16[384,1024]{1,0:T(8,128)(2,1)S(1)} %constant_dynamic-update-slice_fusion.refs_0_, bf16[8192,1024]{1,0:T(8,128)(2,1)} %refs_1_.5, f32[384,1024]{1,0:T(8,128)S(1)} %add_products.6.refs_2_, f32[384,1024]{1,0:T(8,128)S(1)} %get-tuple-element.97.refs_3_), custom_call_target="tpu_custom_call" | custom-call | tf_op jit(solution)/shard_map/add_products/pallas_call | solution.py:331
  125.4 2.5 %unpack_rows.2 = bf16[512,1024]{1,0:T(8,128)(2,1)} custom-call(s32[4]{0:T(128)S(1)} %copy-done.5, s32[1]{0:T(128)} %bitcast.place, bf16[384,1024]{1,0:T(8,128)(2,1)S(1)} %add_products.7.x_ref, bf16[128,1024]{1,0:T(8,128)(2,1)S(1)} %collective-permute-done.22.spare_ref), custom_call_target="tpu_custom_call" | custom-call | tf_op jit(solution)/shard_map/unpack_rows/pallas_call | solution.py:157
  127.9 5.3 %collective-permute-done.23 = f16[384,1024]{1,0:T(8,128)(2,1)S(1)} collective-permute-done((f16[384,1024]{1,0:T(8,128)(2,1)S(1)}, f16[384,1024]{1,0:T(8,128)(2,1)S(1)}, u32[]{:S(2)}, u32[]{:S(2)}) %collective-permute-start.23) | collective-permute-done | bytes 786464 | tf_op jit(solution)/shard_map/scatter_up_4/ppermute | solution.py:36
  133.2 2.2 %collective-permute-done.24 = f16[384,1024]{1,0:T(8,128)(2,1)S(1)} collective-permute-done((f16[384,1024]{1,0:T(8,128)(2,1)S(1)}, f16[384,1024]{1,0:T(8,128)(2,1)S(1)}, u32[]{:S(2)}, u32[]{:S(2)}) %collective-permute-start.24) | collective-permute-done | bytes 786464 | tf_op jit(solution)/shard_map/scatter_down_4/ppermute | solution.py:36
  137.1 2.5 %unpack_rows.3 = bf16[512,1024]{1,0:T(8,128)(2,1)} custom-call(s32[4]{0:T(128)S(1)} %copy-done.5, s32[1]{0:T(128)} %bitcast.place, bf16[384,1024]{1,0:T(8,128)(2,1)S(1)} %add_convert_fusion.x_ref, bf16[128,1024]{1,0:T(8,128)(2,1)S(1)} %collective-permute-done.25.spare_ref), custom_call_target="tpu_custom_call" | custom-call | tf_op jit(solution)/shard_map/unpack_rows/pallas_call | solution.py:157
  (83 shorter events, 38.8 us)
Async XLA Ops:
  3.6 2.2 %collective-permute-start = (bf16[256,1024]{1,0:T(8,128)(2,1)}, bf16[256,1024]{1,0:T(8,128)(2,1)S(1)}, u32[]{:S(2)}, u32[]{:S(2)}) collective-permute-start(bf16[256,1024]{1,0:T(8,128)(2,1)} %spare_rows.1), channel_id=1, source_target_pairs={{0,1},{1,0},{2,3},{3,2},{4,5},{5,4},{6,7},{7,6},{8,9},{9,8},{10,11... | collective-permute-start | bytes 1572872 | tf_op jit(solution)/shard_map/ppermute | solution.py:40
  6.9 21.3 %collective-permute-start.1 = (bf16[384,1024]{1,0:T(8,128)(2,1)S(1)}, bf16[384,1024]{1,0:T(8,128)(2,1)S(1)}, u32[]{:S(2)}, u32[]{:S(2)}) collective-permute-start(bf16[384,1024]{1,0:T(8,128)(2,1)S(1)} %pack_rows.2.refs_2_.x.refs_0_), channel_id=1, source_target_pairs={{0,4},{4,8},{8,12},{12,14},{14,10},{10,6},{6,2},{2,0},{1,5},{5,9},... | collective-permute-start | bytes 2359304 | tf_op jit(solution)/shard_map/gather_up_1/ppermute | solution.py:36
  9.9 20.4 %collective-permute-start.4 = (bf16[384,1024]{1,0:T(8,128)(2,1)S(1)}, bf16[384,1024]{1,0:T(8,128)(2,1)S(1)}, u32[]{:S(2)}, u32[]{:S(2)}) collective-permute-start(bf16[384,1024]{1,0:T(8,128)(2,1)S(1)} %pack_rows.2.refs_2_.x.refs_0_), channel_id=1, source_target_pairs={{4,0},{8,4},{12,8},{14,12},{10,14},{6,10},{2,6},{0,2},{5,1},{9,5},... | collective-permute-start | bytes 2359304 | tf_op jit(solution)/shard_map/gather_down_1/ppermute | solution.py:36
  12.3 11.3 %collective-permute-start.2 = (bf16[256,1024]{1,0:T(8,128)(2,1)S(1)}, bf16[256,1024]{1,0:T(8,128)(2,1)S(1)}, u32[]{:S(2)}, u32[]{:S(2)}) collective-permute-start(bf16[256,1024]{1,0:T(8,128)(2,1)S(1)} %get-tuple-element.53.own_q), channel_id=1, source_target_pairs={{0,1},{1,0},{2,3},{3,2},{4,5},{5,4},{6,7},{7,6},{8,9},{9,8},{10,11... | collective-permute-start | bytes 1572872 | tf_op jit(solution)/shard_map/ppermute | solution.py:40
  12.4 11.3 %collective-permute-start.3 = (bf16[256,1024]{1,0:T(8,128)(2,1)S(1)}, bf16[256,1024]{1,0:T(8,128)(2,1)S(1)}, u32[]{:S(2)}, u32[]{:S(2)}) collective-permute-start(bf16[256,1024]{1,0:T(8,128)(2,1)S(1)} %get-tuple-element.54.own_o), channel_id=1, source_target_pairs={{0,1},{1,0},{2,3},{3,2},{4,5},{5,4},{6,7},{7,6},{8,9},{9,8},{10,11... | collective-permute-start | bytes 1572872 | tf_op jit(solution)/shard_map/ppermute | solution.py:40
  21.6 27.8 %collective-permute-start.6 = (f16[192,1024]{1,0:T(8,128)(2,1)S(1)}, f16[192,1024]{1,0:T(8,128)(2,1)S(1)}, u32[]{:S(2)}, u32[]{:S(2)}) collective-permute-start(f16[192,1024]{1,0:T(8,128)(2,1)S(1)} %get-tuple-element.111), channel_id=1, source_target_pairs={{0,4},{4,8},{8,12},{12,14},{14,10},{10,6},{6,2},{2,0},{1,5},{5,9},... | collective-permute-start | bytes 1179656 | tf_op jit(solution)/shard_map/scatter_up_1/ppermute | solution.py:36
  23.7 25.7 %collective-permute-start.7 = (f16[192,1024]{1,0:T(8,128)(2,1)S(1)}, f16[192,1024]{1,0:T(8,128)(2,1)S(1)}, u32[]{:S(2)}, u32[]{:S(2)}) collective-permute-start(f16[192,1024]{1,0:T(8,128)(2,1)S(1)} %get-tuple-element.110), channel_id=1, source_target_pairs={{4,0},{8,4},{12,8},{14,12},{10,14},{6,10},{2,6},{0,2},{5,1},{9,5},... | collective-permute-start | bytes 1179656 | tf_op jit(solution)/shard_map/scatter_down_1/ppermute | solution.py:36
  26.1 23.3 %collective-permute-start.8 = (f16[384,128]{1,0:T(8,128)(2,1)S(1)}, f16[384,128]{1,0:T(8,128)(2,1)S(1)}, u32[]{:S(2)}, u32[]{:S(2)}) collective-permute-start(f16[384,128]{1,0:T(8,128)(2,1)S(1)} %multiply_convert_fusion.3), channel_id=1, source_target_pairs={{0,2},{2,0},{4,6},{6,4},{8,10},{10,8},{12,14},{14,12},{1,3},{3,1},... | collective-permute-start | bytes 294920 | tf_op jit(solution)/shard_map/down_sums_1/ppermute | solution.py:36
  30.3 25.2 %collective-permute-start.5 = (bf16[384,1024]{1,0:T(8,128)(2,1)S(1)}, bf16[384,1024]{1,0:T(8,128)(2,1)S(1)}, u32[]{:S(2)}, u32[]{:S(2)}) collective-permute-start(bf16[384,1024]{1,0:T(8,128)(2,1)S(1)} %collective-permute-done.1.refs_2_), channel_id=1, source_target_pairs={{0,4},{4,8},{8,12},{12,14},{14,10},{10,6},{6,2},{2,0},{1,5},{5,9},... | collective-permute-start | bytes 2359304 | tf_op jit(solution)/shard_map/gather_up_2/ppermute | solution.py:36
  31.9 23.7 %collective-permute-start.9 = (bf16[384,1024]{1,0:T(8,128)(2,1)S(1)}, bf16[384,1024]{1,0:T(8,128)(2,1)S(1)}, u32[]{:S(2)}, u32[]{:S(2)}) collective-permute-start(bf16[384,1024]{1,0:T(8,128)(2,1)S(1)} %collective-permute-done.4.refs_1_), channel_id=1, source_target_pairs={{4,0},{8,4},{12,8},{14,12},{10,14},{6,10},{2,6},{0,2},{5,1},{9,5},... | collective-permute-start | bytes 2359304 | tf_op jit(solution)/shard_map/gather_down_2/ppermute | solution.py:36
  49.9 22.5 %collective-permute-start.11 = (f16[384,1024]{1,0:T(8,128)(2,1)S(1)}, f16[384,1024]{1,0:T(8,128)(2,1)S(1)}, u32[]{:S(2)}, u32[]{:S(2)}) collective-permute-start(f16[384,1024]{1,0:T(8,128)(2,1)S(1)} %fusion.12), channel_id=1, source_target_pairs={{0,4},{4,8},{8,12},{12,14},{14,10},{10,6},{6,2},{2,0},{1,5},{5,9},... | collective-permute-start | bytes 2359304 | tf_op jit(solution)/shard_map/scatter_up_2/ppermute | solution.py:36
  51.7 22.9 %collective-permute-start.12 = (f16[384,1024]{1,0:T(8,128)(2,1)S(1)}, f16[384,1024]{1,0:T(8,128)(2,1)S(1)}, u32[]{:S(2)}, u32[]{:S(2)}) collective-permute-start(f16[384,1024]{1,0:T(8,128)(2,1)S(1)} %fusion.13), channel_id=1, source_target_pairs={{4,0},{8,4},{12,8},{14,12},{10,14},{6,10},{2,6},{0,2},{5,1},{9,5},... | collective-permute-start | bytes 2359304 | tf_op jit(solution)/shard_map/scatter_down_2/ppermute | solution.py:36
  52.3 22.3 %collective-permute-start.13 = (f16[384,128]{1,0:T(8,128)(2,1)S(1)}, f16[384,128]{1,0:T(8,128)(2,1)S(1)}, u32[]{:S(2)}, u32[]{:S(2)}) collective-permute-start(f16[384,128]{1,0:T(8,128)(2,1)S(1)} %multiply_convert_fusion.2), channel_id=1, source_target_pairs={{0,4},{2,6},{4,0},{6,2},{8,12},{10,14},{12,8},{14,10},{1,5},{3,7},... | collective-permute-start | bytes 294920 | tf_op jit(solution)/shard_map/down_sums_2/ppermute | solution.py:36
  55.6 33.7 %collective-permute-start.10 = (bf16[384,1024]{1,0:T(8,128)(2,1)S(1)}, bf16[384,1024]{1,0:T(8,128)(2,1)S(1)}, u32[]{:S(2)}, u32[]{:S(2)}) collective-permute-start(bf16[384,1024]{1,0:T(8,128)(2,1)S(1)} %collective-permute-done.5.refs_1_), channel_id=1, source_target_pairs={{0,4},{4,8},{8,12},{12,14},{14,10},{10,6},{6,2},{2,0},{1,5},{5,9},... | collective-permute-start | bytes 2359304 | tf_op jit(solution)/shard_map/gather_up_3/ppermute | solution.py:36
  61.5 29.9 %collective-permute-start.14 = (bf16[384,1024]{1,0:T(8,128)(2,1)S(1)}, bf16[384,1024]{1,0:T(8,128)(2,1)S(1)}, u32[]{:S(2)}, u32[]{:S(2)}) collective-permute-start(bf16[384,1024]{1,0:T(8,128)(2,1)S(1)} %collective-permute-done.9.refs_0_), channel_id=1, source_target_pairs={{4,0},{8,4},{12,8},{14,12},{10,14},{6,10},{2,6},{0,2},{5,1},{9,5},... | collective-permute-start | bytes 2359304 | tf_op jit(solution)/shard_map/gather_down_3/ppermute | solution.py:36
  77.2 28.9 %collective-permute-start.16 = (f16[384,1024]{1,0:T(8,128)(2,1)S(1)}, f16[384,1024]{1,0:T(8,128)(2,1)S(1)}, u32[]{:S(2)}, u32[]{:S(2)}) collective-permute-start(f16[384,1024]{1,0:T(8,128)(2,1)S(1)} %get-tuple-element.105), channel_id=1, source_target_pairs={{0,4},{4,8},{8,12},{12,14},{14,10},{10,6},{6,2},{2,0},{1,5},{5,9},... | collective-permute-start | bytes 2359304 | tf_op jit(solution)/shard_map/scatter_up_3/ppermute | solution.py:36
  77.3 33.2 %collective-permute-start.17 = (f16[384,1024]{1,0:T(8,128)(2,1)S(1)}, f16[384,1024]{1,0:T(8,128)(2,1)S(1)}, u32[]{:S(2)}, u32[]{:S(2)}) collective-permute-start(f16[384,1024]{1,0:T(8,128)(2,1)S(1)} %get-tuple-element.104), channel_id=1, source_target_pairs={{4,0},{8,4},{12,8},{14,12},{10,14},{6,10},{2,6},{0,2},{5,1},{9,5},... | collective-permute-start | bytes 2359304 | tf_op jit(solution)/shard_map/scatter_down_3/ppermute | solution.py:36
  79.3 31.1 %collective-permute-start.18 = (f16[384,128]{1,0:T(8,128)(2,1)S(1)}, f16[384,128]{1,0:T(8,128)(2,1)S(1)}, u32[]{:S(2)}, u32[]{:S(2)}) collective-permute-start(f16[384,128]{1,0:T(8,128)(2,1)S(1)} %multiply_convert_fusion.1), channel_id=1, source_target_pairs={{0,8},{2,10},{4,12},{6,14},{8,0},{10,2},{12,4},{14,6},{1,9},{3,11}... | collective-permute-start | bytes 294920 | tf_op jit(solution)/shard_map/down_sums_4/ppermute | solution.py:36
  91.5 24.7 %collective-permute-start.15 = (bf16[192,1024]{1,0:T(8,128)(2,1)S(1)}, bf16[192,1024]{1,0:T(8,128)(2,1)S(1)}, u32[]{:S(2)}, u32[]{:S(2)}) collective-permute-start(bf16[192,1024]{1,0:T(8,128)(2,1)S(1)} %slice.89), channel_id=1, source_target_pairs={{0,4},{4,8},{8,12},{12,14},{14,10},{10,6},{6,2},{2,0},{1,5},{5,9},... | collective-permute-start | bytes 1179656 | tf_op jit(solution)/shard_map/gather_up_4/ppermute | solution.py:36
  94.2 24.6 %collective-permute-start.19 = (bf16[192,1024]{1,0:T(8,128)(2,1)S(1)}, bf16[192,1024]{1,0:T(8,128)(2,1)S(1)}, u32[]{:S(2)}, u32[]{:S(2)}) collective-permute-start(bf16[192,1024]{1,0:T(8,128)(2,1)S(1)} %slice.90), channel_id=1, source_target_pairs={{4,0},{8,4},{12,8},{14,12},{10,14},{6,10},{2,6},{0,2},{5,1},{9,5},... | collective-permute-start | bytes 1179656 | tf_op jit(solution)/shard_map/gather_down_4/ppermute | solution.py:36
  113.0 5.8 %collective-permute-start.21 = (bf16[256,1024]{1,0:T(8,128)(2,1)S(1)}, bf16[256,1024]{1,0:T(8,128)(2,1)S(1)}, u32[]{:S(2)}, u32[]{:S(2)}) collective-permute-start(bf16[256,1024]{1,0:T(8,128)(2,1)S(1)} %get-tuple-element.96.own_o), channel_id=1, source_target_pairs={{0,1},{1,0},{2,3},{3,2},{4,5},{5,4},{6,7},{7,6},{8,9},{9,8},{10,11... | collective-permute-start | bytes 1572872 | tf_op jit(solution)/shard_map/ppermute | solution.py:40
  113.1 5.7 %collective-permute-start.20 = (bf16[256,1024]{1,0:T(8,128)(2,1)S(1)}, bf16[256,1024]{1,0:T(8,128)(2,1)S(1)}, u32[]{:S(2)}, u32[]{:S(2)}) collective-permute-start(bf16[256,1024]{1,0:T(8,128)(2,1)S(1)} %get-tuple-element.95.own_q), channel_id=1, source_target_pairs={{0,1},{1,0},{2,3},{3,2},{4,5},{5,4},{6,7},{7,6},{8,9},{9,8},{10,11... | collective-permute-start | bytes 1572872 | tf_op jit(solution)/shard_map/ppermute | solution.py:40
  113.6 19.6 %collective-permute-start.23 = (f16[384,1024]{1,0:T(8,128)(2,1)S(1)}, f16[384,1024]{1,0:T(8,128)(2,1)S(1)}, u32[]{:S(2)}, u32[]{:S(2)}) collective-permute-start(f16[384,1024]{1,0:T(8,128)(2,1)S(1)} %get-tuple-element.103), channel_id=1, source_target_pairs={{0,4},{4,8},{8,12},{12,14},{14,10},{10,6},{6,2},{2,0},{1,5},{5,9},... | collective-permute-start | bytes 2359304 | tf_op jit(solution)/shard_map/scatter_up_4/ppermute | solution.py:36
  116.2 19.2 %collective-permute-start.24 = (f16[384,1024]{1,0:T(8,128)(2,1)S(1)}, f16[384,1024]{1,0:T(8,128)(2,1)S(1)}, u32[]{:S(2)}, u32[]{:S(2)}) collective-permute-start(f16[384,1024]{1,0:T(8,128)(2,1)S(1)} %get-tuple-element.102), channel_id=1, source_target_pairs={{4,0},{8,4},{12,8},{14,12},{10,14},{6,10},{2,6},{0,2},{5,1},{9,5},... | collective-permute-start | bytes 2359304 | tf_op jit(solution)/shard_map/scatter_down_4/ppermute | solution.py:36
  (10 other events, 54.3 us)

commit v7 on v6

--- a/solution.py
+++ b/solution.py
@@ -21,7 +21,7 @@
 I32 = jnp.int32
 
 SMALL = 16 * 1024 * 1024
-LARGE = 48 * 1024 * 1024
+LARGE = 40 * 1024 * 1024
 FULL = 62 * 1024 * 1024
 
 
@@ -82,58 +82,57 @@
     return jnp.where(live, home, -1)
 
 
-def spare_kernel(counts, place, x_ref, v_ref, out):
-    spare = x_ref.shape[0]
-    packed = 2 * REQUEST_LENGTH - spare
-    c_a, c_b, d_a, d_b = lengths(counts, place)
-    seat = iota((spare, 1), 0) + packed - spare - d_a - d_b
-    home = home_of(packed + seat, seat >= 0, c_a) - packed
-    out[:spare] = select_rows(home, x_ref).astype(BF16)
-    out[spare:] = select_rows(home, v_ref).astype(BF16)
-
-
-def spare_rows(counts, place, x, v, spare):
-    shape = (2 * spare, x.shape[1])
-    return pl.pallas_call(
-        spare_kernel,
+def pack_kernel(counts, place, x_ref, out):
+    c_a, c_b, _, _ = lengths(counts, place)
+    slot = iota((out.shape[0], 1), 0)
+    out[...] = select_rows(home_of(slot, slot < c_a + c_b, c_a), x_ref).astype(BF16)
+
+
+def pack(counts, place, x):
+    rows, width = x.shape
+    shape = (rows * 3 // 4, width)
+    return pl.pallas_call(
+        pack_kernel,
         grid_spec=pltpu.PrefetchScalarGridSpec(
             num_scalar_prefetch=2,
             grid=(1,),
-            in_specs=[pl.BlockSpec((spare, x.shape[1]), lambda *_: (x.shape[0] // spare - 1, 0))] * 2,
-            out_specs=whole(shape),
-        ),
-        out_shape=jax.ShapeDtypeStruct(shape, BF16),
-        compiler_params=params(FULL),
-        name="spare_rows",
-    )(counts, place, x, v)
-
-
-def pack_kernel(counts, place, x_ref, moved_ref, out):
-    packed, spare = out.shape[0], moved_ref.shape[0]
-    first = packed - spare
-    c_a, c_b, _, _ = lengths(counts, place)
-    slot = iota((packed, 1), 0)
-    here = select_rows(home_of(slot, slot < c_a + c_b, c_a), x_ref)
-    out[:first] = here[:first].astype(BF16)
-    out[first:] = (here[first:] + moved_ref[...].astype(F32)).astype(BF16)
-
-
-def pack(counts, place, x, moved, which):
-    rows, width = x.shape
-    spare = moved.shape[0] // 2
-    shape = (rows - spare, width)
-    return pl.pallas_call(
-        pack_kernel,
-        grid_spec=pltpu.PrefetchScalarGridSpec(
-            num_scalar_prefetch=2,
-            grid=(1,),
-            in_specs=[whole(x.shape), pl.BlockSpec((spare, width), lambda *_: (which, 0))],
+            in_specs=[whole(x.shape)],
             out_specs=whole(shape),
         ),
         out_shape=jax.ShapeDtypeStruct(shape, BF16),
         compiler_params=params(LARGE),
         name="pack_rows",
-    )(counts, place, x, moved)
+    )(counts, place, x)
+
+
+def fill_kernel(packed, counts, place, x_ref, theirs_ref, out):
+    spare = out.shape[0]
+    c_a, c_b, d_a, _ = lengths(counts, place)
+    n_mine = c_a + c_b
+    slot = iota((spare, 1), 0) + packed - spare
+    home = packed + slot - n_mine - d_a + REQUEST_LENGTH - (2 * REQUEST_LENGTH - spare)
+    there = select_rows(jnp.where(slot < n_mine, -1, home), theirs_ref)
+    out[...] = (x_ref[...].astype(F32) + there).astype(BF16)
+
+
+def fill(counts, place, x, theirs):
+    packed, width = x.shape
+    rows = theirs.shape[0]
+    spare = rows - packed
+    last = pl.BlockSpec((spare, width), lambda *_: (packed // spare - 1, 0))
+    return pl.pallas_call(
+        functools.partial(fill_kernel, packed),
+        grid_spec=pltpu.PrefetchScalarGridSpec(
+            num_scalar_prefetch=2,
+            grid=(1,),
+            in_specs=[last, pl.BlockSpec((spare, width), lambda *_: (rows // spare - 1, 0))],
+            out_specs=last,
+        ),
+        out_shape=jax.ShapeDtypeStruct(x.shape, BF16),
+        input_output_aliases={2: 0},
+        compiler_params=params(LARGE),
+        name="fill_rows",
+    )(counts, place, x, theirs)
 
 
 def unpack_kernel(counts, place, x_ref, spare_ref, out):
@@ -390,11 +389,9 @@
             [look_up(at, [order[(p + d) % size] for p in place_of]) for d in offsets]
         )
 
-        handed = spare_rows(counts, place, tokens, context, spare)
-        moved = other_replica(handed)
-        tok = pack(counts, place, tokens, moved, 0)
+        tok = fill(counts, place, pack(counts, place, tokens), other_replica(tokens))
         ahead, behind = send(tok, following, "gather_up_1"), send(tok, preceding, "gather_down_1")
-        ctx = pack(counts, tie(place, tok), context, moved, 1)
+        ctx = fill(counts, tie(place, tok), pack(counts, tie(place, tok), context), other_replica(context))
         farthest = shares(where, size - 1, 1, ctx, output_weight)
         far = narrow(farthest[0])
         up_sum = send(far[:half], following, "scatter_up_1")

time: 140 us -> 138 us (0.986)
  waiting for transfers between devices: 46 us -> 54 us
  Pallas kernels: 53.2 us -> 46.7 us
  other arithmetic: 8.58 us -> 3.15 us
  local copies, waits for them, and re-layouts: 2.13 us -> 3.6 us
    ppermute x19, waiting for transfers between devices: 43.2 us -> 51.6 us  [send(): return lax.ppermute(value, 'tensor', pairs)]
    convert_element_type x5, other arithmetic: 5.64 us -> 1.86 us  [narrow(): return (value * SUM_SCALE).astype(F16)]
    pallas_call x3, Pallas kernels: 18.9 us -> 15.6 us  [shares(): pl.pallas_call(shares_kernel, grid_spec=pltpu.PrefetchScalarGridSpec(num_...]
    pallas_call x2, Pallas kernels: 3.36 us -> 1.57 us  [fetch(): pl.pallas_call(functools.partial(fetch_kernel, held), grid_spec=pltpu.Pre...]
    add x1, other arithmetic: 1.86 us -> 0.26 us  [local(): base = rest[0] + up_o]
    unnamed x17 -> x21, local copies, waits for them, and re-layouts: 1.65 us -> 3.16 us
    pallas_call x1 -> x2, Pallas kernels: 2.91 us -> 1.52 us  [fill(): pl.pallas_call(functools.partial(fill_kernel, packed), grid_spec=pltpu.Pr...]
  transfers between devices with their start and end apart: 26 -> 27, of which waited for: 12 -> 13; matrix products, arithmetic and copies ran while one was open for 6% -> 3% of each run, Pallas kernels for 33% -> 32%
where the time goes in v7:
time: 138 us; the launch traced here: 137 us
  waiting for transfers between devices  54 us (39%)
  Pallas kernels  46.7 us (34%)
  starting transfers between devices  28.9 us (21%)
  local copies, waits for them, and re-layouts  3.6 us (3%)
  other arithmetic  3.15 us (2%)
    ppermute x19, waiting for transfers between devices, send(): return lax.ppermute(value, 'tensor', pairs)  51.6 us
    ppermute x19, starting transfers between devices, send(): return lax.ppermute(value, 'tensor', pairs)  27 us
    pallas_call x4, Pallas kernels, add_products(): pl.pallas_call(functools.partial(add_kernel, len(pieces)), grid_spec=pltp...  16.9 us
    pallas_call x3, Pallas kernels, shares(): pl.pallas_call(shares_kernel, grid_spec=pltpu.PrefetchScalarGridSpec(num_...  15.6 us
    pallas_call x2, Pallas kernels, unpack(): pl.pallas_call(unpack_kernel, grid_spec=pltpu.PrefetchScalarGridSpec(num_...  4.94 us
    unnamed x21, local copies, waits for them, and re-layouts  3.16 us
  transfers between devices with their start and end apart: 27, of which 13 were waited for; matrix products, arithmetic and copies ran while one was open for 3% of the time, Pallas kernels for 32%

profile of v7, /device:TPU:0, one launch (start us, length us, event | category | flops | bytes accessed | tf_op | source)
XLA Modules:
  0.0 137.4 jit_solution(1011221794065888355)
XLA Ops:
  5.1 3.1 %collective-permute-start.1 = (bf16[384,1024]{1,0:T(8,128)(2,1)S(1)}, bf16[384,1024]{1,0:T(8,128)(2,1)S(1)}, u32[]{:S(2)}, u32[]{:S(2)}) collective-permute-start(bf16[384,1024]{1,0:T(8,128)(2,1)S(1)} %fill_rows.2.refs_2_.x.refs_0_), channel_id=1, source_target_pairs={{0,4},{4,8},{8,12},{12,14},{14,10},{10,6},{6,2},{2,0},{1,5},{5,9},... | collective-permute-start | bytes 2359304 | tf_op jit(solution)/shard_map/gather_up_1/ppermute | solution.py:36
  12.7 3.1 %shares.4 = f32[1,384,1024]{2,1,0:T(8,128)S(1)} custom-call(s32[8]{0:T(128)S(1)} %stack.39.where, bf16[384,1024]{1,0:T(8,128)(2,1)S(1)} %fill_rows.3.x_ref.v, bf16[1024,8192]{1,0:T(8,128)(2,1)} %w_ref.5), custom_call_target="tpu_custom_call" | custom-call | tf_op jit(solution)/shard_map/shares/pallas_call | solution.py:294
  16.0 4.1 %shares.3 = f32[2,384,1024]{2,1,0:T(8,128)S(1)} custom-call(s32[8]{0:T(128)S(1)} %stack.39.where, bf16[384,1024]{1,0:T(8,128)(2,1)S(1)} %fill_rows.3.x_ref.v, bf16[1024,8192]{1,0:T(8,128)(2,1)} %w_ref.5), custom_call_target="tpu_custom_call" | custom-call | tf_op jit(solution)/shard_map/shares/pallas_call | solution.py:294
  20.3 2.1 %collective-permute-start.7 = (f16[192,1024]{1,0:T(8,128)(2,1)S(1)}, f16[192,1024]{1,0:T(8,128)(2,1)S(1)}, u32[]{:S(2)}, u32[]{:S(2)}) collective-permute-start(f16[192,1024]{1,0:T(8,128)(2,1)S(1)} %get-tuple-element.111), channel_id=1, source_target_pairs={{0,4},{4,8},{8,12},{12,14},{14,10},{10,6},{6,2},{2,0},{1,5},{5,9},... | collective-permute-start | bytes 1179656 | tf_op jit(solution)/shard_map/scatter_up_1/ppermute | solution.py:36
  22.4 2.3 %down_rows.1 = f32[384,128]{1,0:T(8,128)S(1)} custom-call(s32[4]{0:T(128)S(1)} %copy-done.7, s32[1]{0:T(128)} %bitcast.place, bf16[384,1024]{1,0:T(8,128)(2,1)S(1)} %fill_rows.2.refs_2_.x.refs_0_, bf16[384,1024]{1,0:T(8,128)(2,1)S(1)} %fill_rows.3.x_ref.v, bf16[256,1024]{1,0:T(8,128)(2,1)S(1)} %get-tuple-element.53.own_q, ...), custom_call_target="tpu_custom_call" | custom-call | tf_op jit(solution)/shard_map/down_rows/pallas_call | solution.py:234
  30.7 8.3 %shares.5 = f32[5,384,1024]{2,1,0:T(8,128)S(1)} custom-call(s32[8]{0:T(128)S(1)} %stack.39.where, bf16[384,1024]{1,0:T(8,128)(2,1)S(1)} %fill_rows.3.x_ref.v, bf16[1024,8192]{1,0:T(8,128)(2,1)} %w_ref.5), custom_call_target="tpu_custom_call" | custom-call | tf_op jit(solution)/shard_map/shares/pallas_call | solution.py:294
  39.0 5.4 %add_products.4.refs_4_ = f32[384,1024]{1,0:T(8,128)S(1)} custom-call(s32[8]{0:T(128)S(1)} %stack.39.where, bf16[384,1024]{1,0:T(8,128)(2,1)S(1)} %fill_rows.2.refs_2_.x.refs_0_, bf16[384,1024]{1,0:T(8,128)(2,1)S(1)} %collective-permute-done.5.refs_1_, bf16[384,1024]{1,0:T(8,128)(2,1)S(1)} %collective-permute-done.1.refs_2_, bf16[8192,1024]{1,0:T(8,128)(2,1)} %refs_1_.5, ...), custom_call_target="tpu_custom_call" | custom-call | tf_op jit(solution)/shard_map/add_products/pallas_call | solution.py:330
  48.8 5.0 %collective-permute-done.6.refs_1_ = bf16[384,1024]{1,0:T(8,128)(2,1)S(1)} collective-permute-done((bf16[384,1024]{1,0:T(8,128)(2,1)S(1)}, bf16[384,1024]{1,0:T(8,128)(2,1)S(1)}, u32[]{:S(2)}, u32[]{:S(2)}) %collective-permute-start.6) | collective-permute-done | bytes 786464 | tf_op jit(solution)/shard_map/gather_up_2/ppermute | solution.py:36
  55.5 4.3 %add_products.5.refs_4_.refs_2_ = f32[384,1024]{1,0:T(8,128)S(1)} custom-call(s32[8]{0:T(128)S(1)} %stack.39.where, bf16[384,1024]{1,0:T(8,128)(2,1)S(1)} %collective-permute-done.10.refs_0_, bf16[384,1024]{1,0:T(8,128)(2,1)S(1)} %collective-permute-done.6.refs_1_, bf16[8192,1024]{1,0:T(8,128)(2,1)} %refs_1_.5, bf16[8192,1024]{1,0:T(8,128)(2,1)} %refs_1_.5, ...), custom_call_target="tpu_custom_call" | custom-call | tf_op jit(solution)/shard_map/add_products/pallas_call | solution.py:330
  60.3 10.4 %collective-permute-done.12 = f16[384,1024]{1,0:T(8,128)(2,1)S(1)} collective-permute-done((f16[384,1024]{1,0:T(8,128)(2,1)S(1)}, f16[384,1024]{1,0:T(8,128)(2,1)S(1)}, u32[]{:S(2)}, u32[]{:S(2)}) %collective-permute-start.12) | collective-permute-done | bytes 786464 | tf_op jit(solution)/shard_map/scatter_up_2/ppermute | solution.py:36
  70.7 2.1 %collective-permute-done.14 = f16[384,128]{1,0:T(8,128)(2,1)S(1)} collective-permute-done((f16[384,128]{1,0:T(8,128)(2,1)S(1)}, f16[384,128]{1,0:T(8,128)(2,1)S(1)}, u32[]{:S(2)}, u32[]{:S(2)}) %collective-permute-start.14) | collective-permute-done | bytes 98336 | tf_op jit(solution)/shard_map/down_sums_2/ppermute | solution.py:36
  75.8 2.7 %collective-permute-start.19 = (f16[384,128]{1,0:T(8,128)(2,1)S(1)}, f16[384,128]{1,0:T(8,128)(2,1)S(1)}, u32[]{:S(2)}, u32[]{:S(2)}) collective-permute-start(f16[384,128]{1,0:T(8,128)(2,1)S(1)} %multiply_convert_fusion.1), channel_id=1, source_target_pairs={{0,8},{2,10},{4,12},{6,14},{8,0},{10,2},{12,4},{14,6},{1,9},{3,11}... | collective-permute-start | bytes 294920 | tf_op jit(solution)/shard_map/down_sums_4/ppermute | solution.py:36
  78.4 9.1 %collective-permute-done.11.refs_1_ = bf16[384,1024]{1,0:T(8,128)(2,1)S(1)} collective-permute-done((bf16[384,1024]{1,0:T(8,128)(2,1)S(1)}, bf16[384,1024]{1,0:T(8,128)(2,1)S(1)}, u32[]{:S(2)}, u32[]{:S(2)}) %collective-permute-start.11) | collective-permute-done | bytes 786464 | tf_op jit(solution)/shard_map/gather_up_3/ppermute | solution.py:36
  87.6 2.1 %collective-permute-done.15.refs_0_ = bf16[384,1024]{1,0:T(8,128)(2,1)S(1)} collective-permute-done((bf16[384,1024]{1,0:T(8,128)(2,1)S(1)}, bf16[384,1024]{1,0:T(8,128)(2,1)S(1)}, u32[]{:S(2)}, u32[]{:S(2)}) %collective-permute-start.15) | collective-permute-done | bytes 786464 | tf_op jit(solution)/shard_map/gather_down_3/ppermute | solution.py:36
  92.7 4.3 %add_products.6.refs_2_ = f32[384,1024]{1,0:T(8,128)S(1)} custom-call(s32[8]{0:T(128)S(1)} %stack.39.where, bf16[384,1024]{1,0:T(8,128)(2,1)S(1)} %collective-permute-done.15.refs_0_, bf16[384,1024]{1,0:T(8,128)(2,1)S(1)} %collective-permute-done.11.refs_1_, bf16[8192,1024]{1,0:T(8,128)(2,1)} %refs_1_.5, bf16[8192,1024]{1,0:T(8,128)(2,1)} %refs_1_.5, ...), custom_call_target="tpu_custom_call" | custom-call | tf_op jit(solution)/shard_map/add_products/pallas_call | solution.py:330
  97.0 7.4 %collective-permute-done.17 = f16[384,1024]{1,0:T(8,128)(2,1)S(1)} collective-permute-done((f16[384,1024]{1,0:T(8,128)(2,1)S(1)}, f16[384,1024]{1,0:T(8,128)(2,1)S(1)}, u32[]{:S(2)}, u32[]{:S(2)}) %collective-permute-start.17) | collective-permute-done | bytes 786464 | tf_op jit(solution)/shard_map/scatter_up_3/ppermute | solution.py:36
  104.4 4.3 %collective-permute-done.19 = f16[384,128]{1,0:T(8,128)(2,1)S(1)} collective-permute-done((f16[384,128]{1,0:T(8,128)(2,1)S(1)}, f16[384,128]{1,0:T(8,128)(2,1)S(1)}, u32[]{:S(2)}, u32[]{:S(2)}) %collective-permute-start.19) | collective-permute-done | bytes 98336 | tf_op jit(solution)/shard_map/down_sums_4/ppermute | solution.py:36
  110.0 2.6 %collective-permute-start.24 = (f16[384,1024]{1,0:T(8,128)(2,1)S(1)}, f16[384,1024]{1,0:T(8,128)(2,1)S(1)}, u32[]{:S(2)}, u32[]{:S(2)}) collective-permute-start(f16[384,1024]{1,0:T(8,128)(2,1)S(1)} %get-tuple-element.103), channel_id=1, source_target_pairs={{0,4},{4,8},{8,12},{12,14},{14,10},{10,6},{6,2},{2,0},{1,5},{5,9},... | collective-permute-start | bytes 2359304 | tf_op jit(solution)/shard_map/scatter_up_4/ppermute | solution.py:36
  114.6 2.4 %collective-permute-start.25 = (f16[384,1024]{1,0:T(8,128)(2,1)S(1)}, f16[384,1024]{1,0:T(8,128)(2,1)S(1)}, u32[]{:S(2)}, u32[]{:S(2)}) collective-permute-start(f16[384,1024]{1,0:T(8,128)(2,1)S(1)} %get-tuple-element.102), channel_id=1, source_target_pairs={{4,0},{8,4},{12,8},{14,12},{10,14},{6,10},{2,6},{0,2},{5,1},{9,5},... | collective-permute-start | bytes 2359304 | tf_op jit(solution)/shard_map/scatter_down_4/ppermute | solution.py:36
  118.7 3.0 %add_products.7.x_ref = bf16[384,1024]{1,0:T(8,128)(2,1)S(1)} custom-call(s32[8]{0:T(128)S(1)} %stack.39.where, bf16[384,1024]{1,0:T(8,128)(2,1)S(1)} %constant_dynamic-update-slice_fusion.refs_0_, bf16[8192,1024]{1,0:T(8,128)(2,1)} %refs_1_.5, f32[384,1024]{1,0:T(8,128)S(1)} %add_products.6.refs_2_, f32[384,1024]{1,0:T(8,128)S(1)} %get-tuple-element.97.refs_3_), custom_call_target="tpu_custom_call" | custom-call | tf_op jit(solution)/shard_map/add_products/pallas_call | solution.py:330
  123.4 2.5 %unpack_rows.2 = bf16[512,1024]{1,0:T(8,128)(2,1)} custom-call(s32[4]{0:T(128)S(1)} %copy-done.7, s32[1]{0:T(128)} %bitcast.place, bf16[384,1024]{1,0:T(8,128)(2,1)S(1)} %add_products.7.x_ref, bf16[128,1024]{1,0:T(8,128)(2,1)S(1)} %collective-permute-done.23.spare_ref), custom_call_target="tpu_custom_call" | custom-call | tf_op jit(solution)/shard_map/unpack_rows/pallas_call | solution.py:156
  125.9 4.7 %collective-permute-done.24 = f16[384,1024]{1,0:T(8,128)(2,1)S(1)} collective-permute-done((f16[384,1024]{1,0:T(8,128)(2,1)S(1)}, f16[384,1024]{1,0:T(8,128)(2,1)S(1)}, u32[]{:S(2)}, u32[]{:S(2)}) %collective-permute-start.24) | collective-permute-done | bytes 786464 | tf_op jit(solution)/shard_map/scatter_up_4/ppermute | solution.py:36
  130.6 2.6 %collective-permute-done.25 = f16[384,1024]{1,0:T(8,128)(2,1)S(1)} collective-permute-done((f16[384,1024]{1,0:T(8,128)(2,1)S(1)}, f16[384,1024]{1,0:T(8,128)(2,1)S(1)}, u32[]{:S(2)}, u32[]{:S(2)}) %collective-permute-start.25) | collective-permute-done | bytes 786464 | tf_op jit(solution)/shard_map/scatter_down_4/ppermute | solution.py:36
  134.9 2.5 %unpack_rows.3 = bf16[512,1024]{1,0:T(8,128)(2,1)} custom-call(s32[4]{0:T(128)S(1)} %copy-done.7, s32[1]{0:T(128)} %bitcast.place, bf16[384,1024]{1,0:T(8,128)(2,1)S(1)} %add_convert_fusion.x_ref, bf16[128,1024]{1,0:T(8,128)(2,1)S(1)} %collective-permute-done.26.spare_ref), custom_call_target="tpu_custom_call" | custom-call | tf_op jit(solution)/shard_map/unpack_rows/pallas_call | solution.py:156
  (90 shorter events, 35.8 us)
Async XLA Ops:
  1.2 10.8 %collective-permute-start.2 = (bf16[512,1024]{1,0:T(8,128)(2,1)}, bf16[512,1024]{1,0:T(8,128)(2,1)S(1)}, u32[]{:S(2)}, u32[]{:S(2)}) collective-permute-start(bf16[512,1024]{1,0:T(8,128)(2,1)} %x_ref.3), channel_id=1, source_target_pairs={{0,1},{1,0},{2,3},{3,2},{4,5},{5,4},{6,7},{7,6},{8,9},{9,8},{10,11... | collective-permute-start | bytes 3145736 | tf_op jit(solution)/shard_map/ppermute | solution.py:40
  5.1 21.8 %collective-permute-start.1 = (bf16[384,1024]{1,0:T(8,128)(2,1)S(1)}, bf16[384,1024]{1,0:T(8,128)(2,1)S(1)}, u32[]{:S(2)}, u32[]{:S(2)}) collective-permute-start(bf16[384,1024]{1,0:T(8,128)(2,1)S(1)} %fill_rows.2.refs_2_.x.refs_0_), channel_id=1, source_target_pairs={{0,4},{4,8},{8,12},{12,14},{14,10},{10,6},{6,2},{2,0},{1,5},{5,9},... | collective-permute-start | bytes 2359304 | tf_op jit(solution)/shard_map/gather_up_1/ppermute | solution.py:36
  8.2 20.4 %collective-permute-start.5 = (bf16[384,1024]{1,0:T(8,128)(2,1)S(1)}, bf16[384,1024]{1,0:T(8,128)(2,1)S(1)}, u32[]{:S(2)}, u32[]{:S(2)}) collective-permute-start(bf16[384,1024]{1,0:T(8,128)(2,1)S(1)} %fill_rows.2.refs_2_.x.refs_0_), channel_id=1, source_target_pairs={{4,0},{8,4},{12,8},{14,12},{10,14},{6,10},{2,6},{0,2},{5,1},{9,5},... | collective-permute-start | bytes 2359304 | tf_op jit(solution)/shard_map/gather_down_1/ppermute | solution.py:36
  11.4 11.0 %collective-permute-start.3 = (bf16[256,1024]{1,0:T(8,128)(2,1)S(1)}, bf16[256,1024]{1,0:T(8,128)(2,1)S(1)}, u32[]{:S(2)}, u32[]{:S(2)}) collective-permute-start(bf16[256,1024]{1,0:T(8,128)(2,1)S(1)} %get-tuple-element.53.own_q), channel_id=1, source_target_pairs={{0,1},{1,0},{2,3},{3,2},{4,5},{5,4},{6,7},{7,6},{8,9},{9,8},{10,11... | collective-permute-start | bytes 1572872 | tf_op jit(solution)/shard_map/ppermute | solution.py:40
  11.5 10.9 %collective-permute-start.4 = (bf16[256,1024]{1,0:T(8,128)(2,1)S(1)}, bf16[256,1024]{1,0:T(8,128)(2,1)S(1)}, u32[]{:S(2)}, u32[]{:S(2)}) collective-permute-start(bf16[256,1024]{1,0:T(8,128)(2,1)S(1)} %get-tuple-element.54.own_o), channel_id=1, source_target_pairs={{0,1},{1,0},{2,3},{3,2},{4,5},{5,4},{6,7},{7,6},{8,9},{9,8},{10,11... | collective-permute-start | bytes 1572872 | tf_op jit(solution)/shard_map/ppermute | solution.py:40
  20.3 24.1 %collective-permute-start.7 = (f16[192,1024]{1,0:T(8,128)(2,1)S(1)}, f16[192,1024]{1,0:T(8,128)(2,1)S(1)}, u32[]{:S(2)}, u32[]{:S(2)}) collective-permute-start(f16[192,1024]{1,0:T(8,128)(2,1)S(1)} %get-tuple-element.111), channel_id=1, source_target_pairs={{0,4},{4,8},{8,12},{12,14},{14,10},{10,6},{6,2},{2,0},{1,5},{5,9},... | collective-permute-start | bytes 1179656 | tf_op jit(solution)/shard_map/scatter_up_1/ppermute | solution.py:36
  22.4 22.0 %collective-permute-start.8 = (f16[192,1024]{1,0:T(8,128)(2,1)S(1)}, f16[192,1024]{1,0:T(8,128)(2,1)S(1)}, u32[]{:S(2)}, u32[]{:S(2)}) collective-permute-start(f16[192,1024]{1,0:T(8,128)(2,1)S(1)} %get-tuple-element.110), channel_id=1, source_target_pairs={{4,0},{8,4},{12,8},{14,12},{10,14},{6,10},{2,6},{0,2},{5,1},{9,5},... | collective-permute-start | bytes 1179656 | tf_op jit(solution)/shard_map/scatter_down_1/ppermute | solution.py:36
  24.8 19.6 %collective-permute-start.9 = (f16[384,128]{1,0:T(8,128)(2,1)S(1)}, f16[384,128]{1,0:T(8,128)(2,1)S(1)}, u32[]{:S(2)}, u32[]{:S(2)}) collective-permute-start(f16[384,128]{1,0:T(8,128)(2,1)S(1)} %multiply_convert_fusion.3), channel_id=1, source_target_pairs={{0,2},{2,0},{4,6},{6,4},{8,10},{10,8},{12,14},{14,12},{1,3},{3,1},... | collective-permute-start | bytes 294920 | tf_op jit(solution)/shard_map/down_sums_1/ppermute | solution.py:36
  28.6 25.2 %collective-permute-start.6 = (bf16[384,1024]{1,0:T(8,128)(2,1)S(1)}, bf16[384,1024]{1,0:T(8,128)(2,1)S(1)}, u32[]{:S(2)}, u32[]{:S(2)}) collective-permute-start(bf16[384,1024]{1,0:T(8,128)(2,1)S(1)} %collective-permute-done.1.refs_2_), channel_id=1, source_target_pairs={{0,4},{4,8},{8,12},{12,14},{14,10},{10,6},{6,2},{2,0},{1,5},{5,9},... | collective-permute-start | bytes 2359304 | tf_op jit(solution)/shard_map/gather_up_2/ppermute | solution.py:36
  30.2 23.7 %collective-permute-start.10 = (bf16[384,1024]{1,0:T(8,128)(2,1)S(1)}, bf16[384,1024]{1,0:T(8,128)(2,1)S(1)}, u32[]{:S(2)}, u32[]{:S(2)}) collective-permute-start(bf16[384,1024]{1,0:T(8,128)(2,1)S(1)} %collective-permute-done.5.refs_1_), channel_id=1, source_target_pairs={{4,0},{8,4},{12,8},{14,12},{10,14},{6,10},{2,6},{0,2},{5,1},{9,5},... | collective-permute-start | bytes 2359304 | tf_op jit(solution)/shard_map/gather_down_2/ppermute | solution.py:36
  44.9 25.9 %collective-permute-start.12 = (f16[384,1024]{1,0:T(8,128)(2,1)S(1)}, f16[384,1024]{1,0:T(8,128)(2,1)S(1)}, u32[]{:S(2)}, u32[]{:S(2)}) collective-permute-start(f16[384,1024]{1,0:T(8,128)(2,1)S(1)} %fusion.12), channel_id=1, source_target_pairs={{0,4},{4,8},{8,12},{12,14},{14,10},{10,6},{6,2},{2,0},{1,5},{5,9},... | collective-permute-start | bytes 2359304 | tf_op jit(solution)/shard_map/scatter_up_2/ppermute | solution.py:36
  46.6 26.2 %collective-permute-start.13 = (f16[384,1024]{1,0:T(8,128)(2,1)S(1)}, f16[384,1024]{1,0:T(8,128)(2,1)S(1)}, u32[]{:S(2)}, u32[]{:S(2)}) collective-permute-start(f16[384,1024]{1,0:T(8,128)(2,1)S(1)} %fusion.13), channel_id=1, source_target_pairs={{4,0},{8,4},{12,8},{14,12},{10,14},{6,10},{2,6},{0,2},{5,1},{9,5},... | collective-permute-start | bytes 2359304 | tf_op jit(solution)/shard_map/scatter_down_2/ppermute | solution.py:36
  47.2 25.7 %collective-permute-start.14 = (f16[384,128]{1,0:T(8,128)(2,1)S(1)}, f16[384,128]{1,0:T(8,128)(2,1)S(1)}, u32[]{:S(2)}, u32[]{:S(2)}) collective-permute-start(f16[384,128]{1,0:T(8,128)(2,1)S(1)} %multiply_convert_fusion.2), channel_id=1, source_target_pairs={{0,4},{2,6},{4,0},{6,2},{8,12},{10,14},{12,8},{14,10},{1,5},{3,7},... | collective-permute-start | bytes 294920 | tf_op jit(solution)/shard_map/down_sums_2/ppermute | solution.py:36
  53.9 33.7 %collective-permute-start.11 = (bf16[384,1024]{1,0:T(8,128)(2,1)S(1)}, bf16[384,1024]{1,0:T(8,128)(2,1)S(1)}, u32[]{:S(2)}, u32[]{:S(2)}) collective-permute-start(bf16[384,1024]{1,0:T(8,128)(2,1)S(1)} %collective-permute-done.6.refs_1_), channel_id=1, source_target_pairs={{0,4},{4,8},{8,12},{12,14},{14,10},{10,6},{6,2},{2,0},{1,5},{5,9},... | collective-permute-start | bytes 2359304 | tf_op jit(solution)/shard_map/gather_up_3/ppermute | solution.py:36
  59.8 30.0 %collective-permute-start.15 = (bf16[384,1024]{1,0:T(8,128)(2,1)S(1)}, bf16[384,1024]{1,0:T(8,128)(2,1)S(1)}, u32[]{:S(2)}, u32[]{:S(2)}) collective-permute-start(bf16[384,1024]{1,0:T(8,128)(2,1)S(1)} %collective-permute-done.10.refs_0_), channel_id=1, source_target_pairs={{4,0},{8,4},{12,8},{14,12},{10,14},{6,10},{2,6},{0,2},{5,1},{9,5},... | collective-permute-start | bytes 2359304 | tf_op jit(solution)/shard_map/gather_down_3/ppermute | solution.py:36
  73.6 30.8 %collective-permute-start.17 = (f16[384,1024]{1,0:T(8,128)(2,1)S(1)}, f16[384,1024]{1,0:T(8,128)(2,1)S(1)}, u32[]{:S(2)}, u32[]{:S(2)}) collective-permute-start(f16[384,1024]{1,0:T(8,128)(2,1)S(1)} %get-tuple-element.105), channel_id=1, source_target_pairs={{0,4},{4,8},{8,12},{12,14},{14,10},{10,6},{6,2},{2,0},{1,5},{5,9},... | collective-permute-start | bytes 2359304 | tf_op jit(solution)/shard_map/scatter_up_3/ppermute | solution.py:36
  73.7 35.0 %collective-permute-start.18 = (f16[384,1024]{1,0:T(8,128)(2,1)S(1)}, f16[384,1024]{1,0:T(8,128)(2,1)S(1)}, u32[]{:S(2)}, u32[]{:S(2)}) collective-permute-start(f16[384,1024]{1,0:T(8,128)(2,1)S(1)} %get-tuple-element.104), channel_id=1, source_target_pairs={{4,0},{8,4},{12,8},{14,12},{10,14},{6,10},{2,6},{0,2},{5,1},{9,5},... | collective-permute-start | bytes 2359304 | tf_op jit(solution)/shard_map/scatter_down_3/ppermute | solution.py:36
  75.8 32.9 %collective-permute-start.19 = (f16[384,128]{1,0:T(8,128)(2,1)S(1)}, f16[384,128]{1,0:T(8,128)(2,1)S(1)}, u32[]{:S(2)}, u32[]{:S(2)}) collective-permute-start(f16[384,128]{1,0:T(8,128)(2,1)S(1)} %multiply_convert_fusion.1), channel_id=1, source_target_pairs={{0,8},{2,10},{4,12},{6,14},{8,0},{10,2},{12,4},{14,6},{1,9},{3,11}... | collective-permute-start | bytes 294920 | tf_op jit(solution)/shard_map/down_sums_4/ppermute | solution.py:36
  89.8 24.8 %collective-permute-start.16 = (bf16[192,1024]{1,0:T(8,128)(2,1)S(1)}, bf16[192,1024]{1,0:T(8,128)(2,1)S(1)}, u32[]{:S(2)}, u32[]{:S(2)}) collective-permute-start(bf16[192,1024]{1,0:T(8,128)(2,1)S(1)} %slice.89), channel_id=1, source_target_pairs={{0,4},{4,8},{8,12},{12,14},{14,10},{10,6},{6,2},{2,0},{1,5},{5,9},... | collective-permute-start | bytes 1179656 | tf_op jit(solution)/shard_map/gather_up_4/ppermute | solution.py:36
  90.7 26.4 %collective-permute-start.20 = (bf16[192,1024]{1,0:T(8,128)(2,1)S(1)}, bf16[192,1024]{1,0:T(8,128)(2,1)S(1)}, u32[]{:S(2)}, u32[]{:S(2)}) collective-permute-start(bf16[192,1024]{1,0:T(8,128)(2,1)S(1)} %slice.90), channel_id=1, source_target_pairs={{4,0},{8,4},{12,8},{14,12},{10,14},{6,10},{2,6},{0,2},{5,1},{9,5},... | collective-permute-start | bytes 1179656 | tf_op jit(solution)/shard_map/gather_down_4/ppermute | solution.py:36
  109.4 7.8 %collective-permute-start.22 = (bf16[256,1024]{1,0:T(8,128)(2,1)S(1)}, bf16[256,1024]{1,0:T(8,128)(2,1)S(1)}, u32[]{:S(2)}, u32[]{:S(2)}) collective-permute-start(bf16[256,1024]{1,0:T(8,128)(2,1)S(1)} %get-tuple-element.96.own_o), channel_id=1, source_target_pairs={{0,1},{1,0},{2,3},{3,2},{4,5},{5,4},{6,7},{7,6},{8,9},{9,8},{10,11... | collective-permute-start | bytes 1572872 | tf_op jit(solution)/shard_map/ppermute | solution.py:40
  109.5 7.7 %collective-permute-start.21 = (bf16[256,1024]{1,0:T(8,128)(2,1)S(1)}, bf16[256,1024]{1,0:T(8,128)(2,1)S(1)}, u32[]{:S(2)}, u32[]{:S(2)}) collective-permute-start(bf16[256,1024]{1,0:T(8,128)(2,1)S(1)} %get-tuple-element.95.own_q), channel_id=1, source_target_pairs={{0,1},{1,0},{2,3},{3,2},{4,5},{5,4},{6,7},{7,6},{8,9},{9,8},{10,11... | collective-permute-start | bytes 1572872 | tf_op jit(solution)/shard_map/ppermute | solution.py:40
  110.0 20.6 %collective-permute-start.24 = (f16[384,1024]{1,0:T(8,128)(2,1)S(1)}, f16[384,1024]{1,0:T(8,128)(2,1)S(1)}, u32[]{:S(2)}, u32[]{:S(2)}) collective-permute-start(f16[384,1024]{1,0:T(8,128)(2,1)S(1)} %get-tuple-element.103), channel_id=1, source_target_pairs={{0,4},{4,8},{8,12},{12,14},{14,10},{10,6},{6,2},{2,0},{1,5},{5,9},... | collective-permute-start | bytes 2359304 | tf_op jit(solution)/shard_map/scatter_up_4/ppermute | solution.py:36
  114.6 18.6 %collective-permute-start.25 = (f16[384,1024]{1,0:T(8,128)(2,1)S(1)}, f16[384,1024]{1,0:T(8,128)(2,1)S(1)}, u32[]{:S(2)}, u32[]{:S(2)}) collective-permute-start(f16[384,1024]{1,0:T(8,128)(2,1)S(1)} %get-tuple-element.102), channel_id=1, source_target_pairs={{4,0},{8,4},{12,8},{14,12},{10,14},{6,10},{2,6},{0,2},{5,1},{9,5},... | collective-permute-start | bytes 2359304 | tf_op jit(solution)/shard_map/scatter_down_4/ppermute | solution.py:36
  (13 other events, 61.7 us)

commit v8 on v7

--- a/solution.py
+++ b/solution.py
@@ -135,36 +135,47 @@
     )(counts, place, x, theirs)
 
 
-def unpack_kernel(counts, place, x_ref, spare_ref, out):
+def seats_kernel(packed, counts, place, out):
     rows = out.shape[0]
-    packed, spare = x_ref.shape[0], spare_ref.shape[0]
-    first = packed - spare
+    first = 2 * packed - rows
     c_a, c_b, d_a, d_b = lengths(counts, place)
-    n_theirs = d_a + d_b
     row = iota((rows, 1), 0)
     late = row >= REQUEST_LENGTH
     offset = jnp.where(late, row - REQUEST_LENGTH, row)
     position = offset + jnp.where(late, c_a, 0)
-    target = jnp.where(position < packed, position, position + n_theirs - first)
+    target = jnp.where(position < packed, position, position + d_a + d_b - first)
     target = jnp.where(offset < jnp.where(late, c_b, c_a), target, -1)
-    hot = (iota((rows, rows), 1) == target).astype(F32).astype(BF16)
-    out[...] = (dot(hot[:, :packed], x_ref[...]) + dot(hot[:, packed:], spare_ref[...])).astype(BF16)
-
-
-def unpack(counts, place, rows, parts):
-    shape = (rows, parts[0].shape[1])
+    out[...] = (iota((rows, rows), 1) == target).astype(F32).astype(BF16)
+
+
+def seats(counts, place, rows, packed):
+    return pl.pallas_call(
+        functools.partial(seats_kernel, packed),
+        grid_spec=pltpu.PrefetchScalarGridSpec(
+            num_scalar_prefetch=2, grid=(1,), in_specs=[], out_specs=whole((rows, rows))
+        ),
+        out_shape=jax.ShapeDtypeStruct((rows, rows), BF16),
+        compiler_params=params(),
+        name="seats",
+    )(counts, place)
+
+
+def unpack_kernel(hot_ref, x_ref, spare_ref, out):
+    packed = x_ref.shape[0]
+    out[...] = (dot(hot_ref[:, :packed], x_ref[...]) + dot(hot_ref[:, packed:], spare_ref[...])).astype(BF16)
+
+
+def unpack(hot, x, spare):
+    shape = (hot.shape[0], x.shape[1])
     return pl.pallas_call(
         unpack_kernel,
-        grid_spec=pltpu.PrefetchScalarGridSpec(
-            num_scalar_prefetch=2,
-            grid=(1,),
-            in_specs=[whole(p.shape) for p in parts],
-            out_specs=whole(shape),
-        ),
+        grid=(1,),
+        in_specs=[whole(hot.shape), whole(x.shape), whole(spare.shape)],
+        out_specs=whole(shape),
         out_shape=jax.ShapeDtypeStruct(shape, BF16),
         compiler_params=params(),
         name="unpack_rows",
-    )(counts, place, *parts)
+    )(hot, x, spare)
 
 
 def request_of(counts, place, slot, packed):
@@ -449,15 +460,16 @@
         last = jnp.concatenate([got_up, got_down])
         up_q, up_o = up(counts, place, tie(parts, last), mine, theirs)
         q = add_products(where, [last], [size - 1], query_weight, [q, up_q], BF16)
+        hot = seats(counts, tie(place, q), rows, packed)
         q_m = other_replica(q[packed - spare :])
-        queries = unpack(counts, place, rows, (q, q_m))
+        queries = unpack(hot, q, q_m)
         base = rest[0] + up_o
         up_sum, down_sum = lax.optimization_barrier((tie(up_sum, queries, base), down_sum))
         first = packed - spare
         o_last = (base[first:] + widen(up_sum[first:]) + widen(down_sum[first:])).astype(BF16)
         o_m = other_replica(o_last)
         o = (base + widen(up_sum) + widen(down_sum)).astype(BF16)
-        attended = unpack(counts, place, rows, (o, o_m))
+        attended = unpack(hot, o, o_m)
         return queries, attended
 
     return local

time: 138 us -> 137 us (level)
    pallas_call x2 -> x3, Pallas kernels: 4.94 us -> 4.55 us  [the longest x2 3.87 us: unpack(): pl.pallas_call(unpack_kernel, grid=(1,), in_specs=[whole(hot.shape), whol...]
where the time goes in v8:
time: 137 us
  waiting for transfers between devices  53.8 us (39%)
  Pallas kernels  46.3 us (34%)
  starting transfers between devices  28.9 us (21%)
  local copies, waits for them, and re-layouts  3.6 us (3%)
  other arithmetic  3.15 us (2%)
    ppermute x19, waiting for transfers between devices, send(): return lax.ppermute(value, 'tensor', pairs)  52.2 us
    ppermute x19, starting transfers between devices, send(): return lax.ppermute(value, 'tensor', pairs)  27 us
    pallas_call x4, Pallas kernels, add_products(): pl.pallas_call(functools.partial(add_kernel, len(pieces)), grid_spec=pltp...  16.9 us
    pallas_call x3, Pallas kernels, shares(): pl.pallas_call(shares_kernel, grid_spec=pltpu.PrefetchScalarGridSpec(num_...  15.6 us
    pallas_call x2, Pallas kernels, unpack(): pl.pallas_call(unpack_kernel, grid=(1,), in_specs=[whole(hot.shape), whol...  3.87 us
    unnamed x21, local copies, waits for them, and re-layouts  3.16 us
  transfers between devices with their start and end apart: 27, of which 13 were waited for; matrix products, arithmetic and copies ran while one was open for 3% of the time, Pallas kernels for 32%

profile of v8, /device:TPU:0, one launch (start us, length us, event | category | flops | bytes accessed | tf_op | source)
XLA Modules:
  0.0 136.8 jit_solution(14759656640932433244)
XLA Ops:
  5.1 3.1 %collective-permute-start.1 = (bf16[384,1024]{1,0:T(8,128)(2,1)S(1)}, bf16[384,1024]{1,0:T(8,128)(2,1)S(1)}, u32[]{:S(2)}, u32[]{:S(2)}) collective-permute-start(bf16[384,1024]{1,0:T(8,128)(2,1)S(1)} %fill_rows.2.refs_2_.x.refs_0_), channel_id=1, source_target_pairs={{0,4},{4,8},{8,12},{12,14},{14,10},{10,6},{6,2},{2,0},{1,5},{5,9},... | collective-permute-start | bytes 2359304 | tf_op jit(solution)/shard_map/gather_up_1/ppermute | solution.py:36
  12.7 3.1 %shares.4 = f32[1,384,1024]{2,1,0:T(8,128)S(1)} custom-call(s32[8]{0:T(128)S(1)} %stack.39.where, bf16[384,1024]{1,0:T(8,128)(2,1)S(1)} %fill_rows.3.x_ref.v, bf16[1024,8192]{1,0:T(8,128)(2,1)} %w_ref.5), custom_call_target="tpu_custom_call" | custom-call | tf_op jit(solution)/shard_map/shares/pallas_call | solution.py:305
  16.0 4.1 %shares.3 = f32[2,384,1024]{2,1,0:T(8,128)S(1)} custom-call(s32[8]{0:T(128)S(1)} %stack.39.where, bf16[384,1024]{1,0:T(8,128)(2,1)S(1)} %fill_rows.3.x_ref.v, bf16[1024,8192]{1,0:T(8,128)(2,1)} %w_ref.5), custom_call_target="tpu_custom_call" | custom-call | tf_op jit(solution)/shard_map/shares/pallas_call | solution.py:305
  20.3 2.1 %collective-permute-start.7 = (f16[192,1024]{1,0:T(8,128)(2,1)S(1)}, f16[192,1024]{1,0:T(8,128)(2,1)S(1)}, u32[]{:S(2)}, u32[]{:S(2)}) collective-permute-start(f16[192,1024]{1,0:T(8,128)(2,1)S(1)} %get-tuple-element.113), channel_id=1, source_target_pairs={{0,4},{4,8},{8,12},{12,14},{14,10},{10,6},{6,2},{2,0},{1,5},{5,9},... | collective-permute-start | bytes 1179656 | tf_op jit(solution)/shard_map/scatter_up_1/ppermute | solution.py:36
  22.4 2.3 %down_rows.1 = f32[384,128]{1,0:T(8,128)S(1)} custom-call(s32[4]{0:T(128)S(1)} %copy-done.7, s32[1]{0:T(128)} %bitcast.place, bf16[384,1024]{1,0:T(8,128)(2,1)S(1)} %fill_rows.2.refs_2_.x.refs_0_, bf16[384,1024]{1,0:T(8,128)(2,1)S(1)} %fill_rows.3.x_ref.v, bf16[256,1024]{1,0:T(8,128)(2,1)S(1)} %get-tuple-element.54.own_q, ...), custom_call_target="tpu_custom_call" | custom-call | tf_op jit(solution)/shard_map/down_rows/pallas_call | solution.py:245
  30.7 8.3 %shares.5 = f32[5,384,1024]{2,1,0:T(8,128)S(1)} custom-call(s32[8]{0:T(128)S(1)} %stack.39.where, bf16[384,1024]{1,0:T(8,128)(2,1)S(1)} %fill_rows.3.x_ref.v, bf16[1024,8192]{1,0:T(8,128)(2,1)} %w_ref.5), custom_call_target="tpu_custom_call" | custom-call | tf_op jit(solution)/shard_map/shares/pallas_call | solution.py:305
  39.0 5.4 %add_products.4.refs_4_ = f32[384,1024]{1,0:T(8,128)S(1)} custom-call(s32[8]{0:T(128)S(1)} %stack.39.where, bf16[384,1024]{1,0:T(8,128)(2,1)S(1)} %fill_rows.2.refs_2_.x.refs_0_, bf16[384,1024]{1,0:T(8,128)(2,1)S(1)} %collective-permute-done.5.refs_1_, bf16[384,1024]{1,0:T(8,128)(2,1)S(1)} %collective-permute-done.1.refs_2_, bf16[8192,1024]{1,0:T(8,128)(2,1)} %refs_1_.5, ...), custom_call_target="tpu_custom_call" | custom-call | tf_op jit(solution)/shard_map/add_products/pallas_call | solution.py:341
  48.8 5.0 %collective-permute-done.6.refs_1_ = bf16[384,1024]{1,0:T(8,128)(2,1)S(1)} collective-permute-done((bf16[384,1024]{1,0:T(8,128)(2,1)S(1)}, bf16[384,1024]{1,0:T(8,128)(2,1)S(1)}, u32[]{:S(2)}, u32[]{:S(2)}) %collective-permute-start.6) | collective-permute-done | bytes 786464 | tf_op jit(solution)/shard_map/gather_up_2/ppermute | solution.py:36
  55.5 4.3 %add_products.5.refs_4_.refs_2_ = f32[384,1024]{1,0:T(8,128)S(1)} custom-call(s32[8]{0:T(128)S(1)} %stack.39.where, bf16[384,1024]{1,0:T(8,128)(2,1)S(1)} %collective-permute-done.10.refs_0_, bf16[384,1024]{1,0:T(8,128)(2,1)S(1)} %collective-permute-done.6.refs_1_, bf16[8192,1024]{1,0:T(8,128)(2,1)} %refs_1_.5, bf16[8192,1024]{1,0:T(8,128)(2,1)} %refs_1_.5, ...), custom_call_target="tpu_custom_call" | custom-call | tf_op jit(solution)/shard_map/add_products/pallas_call | solution.py:341
  60.3 10.4 %collective-permute-done.12 = f16[384,1024]{1,0:T(8,128)(2,1)S(1)} collective-permute-done((f16[384,1024]{1,0:T(8,128)(2,1)S(1)}, f16[384,1024]{1,0:T(8,128)(2,1)S(1)}, u32[]{:S(2)}, u32[]{:S(2)}) %collective-permute-start.12) | collective-permute-done | bytes 786464 | tf_op jit(solution)/shard_map/scatter_up_2/ppermute | solution.py:36
  70.7 2.1 %collective-permute-done.14 = f16[384,128]{1,0:T(8,128)(2,1)S(1)} collective-permute-done((f16[384,128]{1,0:T(8,128)(2,1)S(1)}, f16[384,128]{1,0:T(8,128)(2,1)S(1)}, u32[]{:S(2)}, u32[]{:S(2)}) %collective-permute-start.14) | collective-permute-done | bytes 98336 | tf_op jit(solution)/shard_map/down_sums_2/ppermute | solution.py:36
  75.8 2.7 %collective-permute-start.19 = (f16[384,128]{1,0:T(8,128)(2,1)S(1)}, f16[384,128]{1,0:T(8,128)(2,1)S(1)}, u32[]{:S(2)}, u32[]{:S(2)}) collective-permute-start(f16[384,128]{1,0:T(8,128)(2,1)S(1)} %multiply_convert_fusion.1), channel_id=1, source_target_pairs={{0,8},{2,10},{4,12},{6,14},{8,0},{10,2},{12,4},{14,6},{1,9},{3,11}... | collective-permute-start | bytes 294920 | tf_op jit(solution)/shard_map/down_sums_4/ppermute | solution.py:36
  78.4 9.1 %collective-permute-done.11.refs_1_ = bf16[384,1024]{1,0:T(8,128)(2,1)S(1)} collective-permute-done((bf16[384,1024]{1,0:T(8,128)(2,1)S(1)}, bf16[384,1024]{1,0:T(8,128)(2,1)S(1)}, u32[]{:S(2)}, u32[]{:S(2)}) %collective-permute-start.11) | collective-permute-done | bytes 786464 | tf_op jit(solution)/shard_map/gather_up_3/ppermute | solution.py:36
  87.6 2.1 %collective-permute-done.15.refs_0_ = bf16[384,1024]{1,0:T(8,128)(2,1)S(1)} collective-permute-done((bf16[384,1024]{1,0:T(8,128)(2,1)S(1)}, bf16[384,1024]{1,0:T(8,128)(2,1)S(1)}, u32[]{:S(2)}, u32[]{:S(2)}) %collective-permute-start.15) | collective-permute-done | bytes 786464 | tf_op jit(solution)/shard_map/gather_down_3/ppermute | solution.py:36
  90.7 2.0 %collective-permute-start.20 = (bf16[192,1024]{1,0:T(8,128)(2,1)S(1)}, bf16[192,1024]{1,0:T(8,128)(2,1)S(1)}, u32[]{:S(2)}, u32[]{:S(2)}) collective-permute-start(bf16[192,1024]{1,0:T(8,128)(2,1)S(1)} %slice.90), channel_id=1, source_target_pairs={{4,0},{8,4},{12,8},{14,12},{10,14},{6,10},{2,6},{0,2},{5,1},{9,5},... | collective-permute-start | bytes 1179656 | tf_op jit(solution)/shard_map/gather_down_4/ppermute | solution.py:36
  92.7 4.3 %add_products.6.refs_2_ = f32[384,1024]{1,0:T(8,128)S(1)} custom-call(s32[8]{0:T(128)S(1)} %stack.39.where, bf16[384,1024]{1,0:T(8,128)(2,1)S(1)} %collective-permute-done.15.refs_0_, bf16[384,1024]{1,0:T(8,128)(2,1)S(1)} %collective-permute-done.11.refs_1_, bf16[8192,1024]{1,0:T(8,128)(2,1)} %refs_1_.5, bf16[8192,1024]{1,0:T(8,128)(2,1)} %refs_1_.5, ...), custom_call_target="tpu_custom_call" | custom-call | tf_op jit(solution)/shard_map/add_products/pallas_call | solution.py:341
  97.0 7.4 %collective-permute-done.17 = f16[384,1024]{1,0:T(8,128)(2,1)S(1)} collective-permute-done((f16[384,1024]{1,0:T(8,128)(2,1)S(1)}, f16[384,1024]{1,0:T(8,128)(2,1)S(1)}, u32[]{:S(2)}, u32[]{:S(2)}) %collective-permute-start.17) | collective-permute-done | bytes 786464 | tf_op jit(solution)/shard_map/scatter_up_3/ppermute | solution.py:36
  104.4 4.3 %collective-permute-done.19 = f16[384,128]{1,0:T(8,128)(2,1)S(1)} collective-permute-done((f16[384,128]{1,0:T(8,128)(2,1)S(1)}, f16[384,128]{1,0:T(8,128)(2,1)S(1)}, u32[]{:S(2)}, u32[]{:S(2)}) %collective-permute-start.19) | collective-permute-done | bytes 98336 | tf_op jit(solution)/shard_map/down_sums_4/ppermute | solution.py:36
  110.0 2.6 %collective-permute-start.24 = (f16[384,1024]{1,0:T(8,128)(2,1)S(1)}, f16[384,1024]{1,0:T(8,128)(2,1)S(1)}, u32[]{:S(2)}, u32[]{:S(2)}) collective-permute-start(f16[384,1024]{1,0:T(8,128)(2,1)S(1)} %get-tuple-element.105), channel_id=1, source_target_pairs={{0,4},{4,8},{8,12},{12,14},{14,10},{10,6},{6,2},{2,0},{1,5},{5,9},... | collective-permute-start | bytes 2359304 | tf_op jit(solution)/shard_map/scatter_up_4/ppermute | solution.py:36
  112.6 2.0 %collective-permute-done.16 = bf16[192,1024]{1,0:T(8,128)(2,1)S(1)} collective-permute-done((bf16[192,1024]{1,0:T(8,128)(2,1)S(1)}, bf16[192,1024]{1,0:T(8,128)(2,1)S(1)}, u32[]{:S(2)}, u32[]{:S(2)}) %collective-permute-start.16) | collective-permute-done | bytes 393248 | tf_op jit(solution)/shard_map/gather_up_4/ppermute | solution.py:36
  114.6 2.4 %collective-permute-start.25 = (f16[384,1024]{1,0:T(8,128)(2,1)S(1)}, f16[384,1024]{1,0:T(8,128)(2,1)S(1)}, u32[]{:S(2)}, u32[]{:S(2)}) collective-permute-start(f16[384,1024]{1,0:T(8,128)(2,1)S(1)} %get-tuple-element.104), channel_id=1, source_target_pairs={{4,0},{8,4},{12,8},{14,12},{10,14},{6,10},{2,6},{0,2},{5,1},{9,5},... | collective-permute-start | bytes 2359304 | tf_op jit(solution)/shard_map/scatter_down_4/ppermute | solution.py:36
  118.7 3.0 %add_products.7.x_ref = bf16[384,1024]{1,0:T(8,128)(2,1)S(1)} custom-call(s32[8]{0:T(128)S(1)} %stack.39.where, bf16[384,1024]{1,0:T(8,128)(2,1)S(1)} %constant_dynamic-update-slice_fusion.refs_0_, bf16[8192,1024]{1,0:T(8,128)(2,1)} %refs_1_.5, f32[384,1024]{1,0:T(8,128)S(1)} %add_products.6.refs_2_, f32[384,1024]{1,0:T(8,128)S(1)} %get-tuple-element.98.refs_3_), custom_call_target="tpu_custom_call" | custom-call | tf_op jit(solution)/shard_map/add_products/pallas_call | solution.py:341
  125.3 5.3 %collective-permute-done.24 = f16[384,1024]{1,0:T(8,128)(2,1)S(1)} collective-permute-done((f16[384,1024]{1,0:T(8,128)(2,1)S(1)}, f16[384,1024]{1,0:T(8,128)(2,1)S(1)}, u32[]{:S(2)}, u32[]{:S(2)}) %collective-permute-start.24) | collective-permute-done | bytes 786464 | tf_op jit(solution)/shard_map/scatter_up_4/ppermute | solution.py:36
  130.6 2.6 %collective-permute-done.25 = f16[384,1024]{1,0:T(8,128)(2,1)S(1)} collective-permute-done((f16[384,1024]{1,0:T(8,128)(2,1)S(1)}, f16[384,1024]{1,0:T(8,128)(2,1)S(1)}, u32[]{:S(2)}, u32[]{:S(2)}) %collective-permute-start.25) | collective-permute-done | bytes 786464 | tf_op jit(solution)/shard_map/scatter_down_4/ppermute | solution.py:36
  (91 shorter events, 35.6 us)
Async XLA Ops:
  1.2 10.8 %collective-permute-start.2 = (bf16[512,1024]{1,0:T(8,128)(2,1)}, bf16[512,1024]{1,0:T(8,128)(2,1)S(1)}, u32[]{:S(2)}, u32[]{:S(2)}) collective-permute-start(bf16[512,1024]{1,0:T(8,128)(2,1)} %x_ref.3), channel_id=1, source_target_pairs={{0,1},{1,0},{2,3},{3,2},{4,5},{5,4},{6,7},{7,6},{8,9},{9,8},{10,11... | collective-permute-start | bytes 3145736 | tf_op jit(solution)/shard_map/ppermute | solution.py:40
  5.1 21.8 %collective-permute-start.1 = (bf16[384,1024]{1,0:T(8,128)(2,1)S(1)}, bf16[384,1024]{1,0:T(8,128)(2,1)S(1)}, u32[]{:S(2)}, u32[]{:S(2)}) collective-permute-start(bf16[384,1024]{1,0:T(8,128)(2,1)S(1)} %fill_rows.2.refs_2_.x.refs_0_), channel_id=1, source_target_pairs={{0,4},{4,8},{8,12},{12,14},{14,10},{10,6},{6,2},{2,0},{1,5},{5,9},... | collective-permute-start | bytes 2359304 | tf_op jit(solution)/shard_map/gather_up_1/ppermute | solution.py:36
  8.2 20.4 %collective-permute-start.5 = (bf16[384,1024]{1,0:T(8,128)(2,1)S(1)}, bf16[384,1024]{1,0:T(8,128)(2,1)S(1)}, u32[]{:S(2)}, u32[]{:S(2)}) collective-permute-start(bf16[384,1024]{1,0:T(8,128)(2,1)S(1)} %fill_rows.2.refs_2_.x.refs_0_), channel_id=1, source_target_pairs={{4,0},{8,4},{12,8},{14,12},{10,14},{6,10},{2,6},{0,2},{5,1},{9,5},... | collective-permute-start | bytes 2359304 | tf_op jit(solution)/shard_map/gather_down_1/ppermute | solution.py:36
  11.4 11.0 %collective-permute-start.3 = (bf16[256,1024]{1,0:T(8,128)(2,1)S(1)}, bf16[256,1024]{1,0:T(8,128)(2,1)S(1)}, u32[]{:S(2)}, u32[]{:S(2)}) collective-permute-start(bf16[256,1024]{1,0:T(8,128)(2,1)S(1)} %get-tuple-element.54.own_q), channel_id=1, source_target_pairs={{0,1},{1,0},{2,3},{3,2},{4,5},{5,4},{6,7},{7,6},{8,9},{9,8},{10,11... | collective-permute-start | bytes 1572872 | tf_op jit(solution)/shard_map/ppermute | solution.py:40
  11.5 10.9 %collective-permute-start.4 = (bf16[256,1024]{1,0:T(8,128)(2,1)S(1)}, bf16[256,1024]{1,0:T(8,128)(2,1)S(1)}, u32[]{:S(2)}, u32[]{:S(2)}) collective-permute-start(bf16[256,1024]{1,0:T(8,128)(2,1)S(1)} %get-tuple-element.55.own_o), channel_id=1, source_target_pairs={{0,1},{1,0},{2,3},{3,2},{4,5},{5,4},{6,7},{7,6},{8,9},{9,8},{10,11... | collective-permute-start | bytes 1572872 | tf_op jit(solution)/shard_map/ppermute | solution.py:40
  20.3 24.1 %collective-permute-start.7 = (f16[192,1024]{1,0:T(8,128)(2,1)S(1)}, f16[192,1024]{1,0:T(8,128)(2,1)S(1)}, u32[]{:S(2)}, u32[]{:S(2)}) collective-permute-start(f16[192,1024]{1,0:T(8,128)(2,1)S(1)} %get-tuple-element.113), channel_id=1, source_target_pairs={{0,4},{4,8},{8,12},{12,14},{14,10},{10,6},{6,2},{2,0},{1,5},{5,9},... | collective-permute-start | bytes 1179656 | tf_op jit(solution)/shard_map/scatter_up_1/ppermute | solution.py:36
  22.4 22.0 %collective-permute-start.8 = (f16[192,1024]{1,0:T(8,128)(2,1)S(1)}, f16[192,1024]{1,0:T(8,128)(2,1)S(1)}, u32[]{:S(2)}, u32[]{:S(2)}) collective-permute-start(f16[192,1024]{1,0:T(8,128)(2,1)S(1)} %get-tuple-element.112), channel_id=1, source_target_pairs={{4,0},{8,4},{12,8},{14,12},{10,14},{6,10},{2,6},{0,2},{5,1},{9,5},... | collective-permute-start | bytes 1179656 | tf_op jit(solution)/shard_map/scatter_down_1/ppermute | solution.py:36
  24.8 19.6 %collective-permute-start.9 = (f16[384,128]{1,0:T(8,128)(2,1)S(1)}, f16[384,128]{1,0:T(8,128)(2,1)S(1)}, u32[]{:S(2)}, u32[]{:S(2)}) collective-permute-start(f16[384,128]{1,0:T(8,128)(2,1)S(1)} %multiply_convert_fusion.3), channel_id=1, source_target_pairs={{0,2},{2,0},{4,6},{6,4},{8,10},{10,8},{12,14},{14,12},{1,3},{3,1},... | collective-permute-start | bytes 294920 | tf_op jit(solution)/shard_map/down_sums_1/ppermute | solution.py:36
  28.6 25.2 %collective-permute-start.6 = (bf16[384,1024]{1,0:T(8,128)(2,1)S(1)}, bf16[384,1024]{1,0:T(8,128)(2,1)S(1)}, u32[]{:S(2)}, u32[]{:S(2)}) collective-permute-start(bf16[384,1024]{1,0:T(8,128)(2,1)S(1)} %collective-permute-done.1.refs_2_), channel_id=1, source_target_pairs={{0,4},{4,8},{8,12},{12,14},{14,10},{10,6},{6,2},{2,0},{1,5},{5,9},... | collective-permute-start | bytes 2359304 | tf_op jit(solution)/shard_map/gather_up_2/ppermute | solution.py:36
  30.2 23.7 %collective-permute-start.10 = (bf16[384,1024]{1,0:T(8,128)(2,1)S(1)}, bf16[384,1024]{1,0:T(8,128)(2,1)S(1)}, u32[]{:S(2)}, u32[]{:S(2)}) collective-permute-start(bf16[384,1024]{1,0:T(8,128)(2,1)S(1)} %collective-permute-done.5.refs_1_), channel_id=1, source_target_pairs={{4,0},{8,4},{12,8},{14,12},{10,14},{6,10},{2,6},{0,2},{5,1},{9,5},... | collective-permute-start | bytes 2359304 | tf_op jit(solution)/shard_map/gather_down_2/ppermute | solution.py:36
  44.9 25.9 %collective-permute-start.12 = (f16[384,1024]{1,0:T(8,128)(2,1)S(1)}, f16[384,1024]{1,0:T(8,128)(2,1)S(1)}, u32[]{:S(2)}, u32[]{:S(2)}) collective-permute-start(f16[384,1024]{1,0:T(8,128)(2,1)S(1)} %fusion.12), channel_id=1, source_target_pairs={{0,4},{4,8},{8,12},{12,14},{14,10},{10,6},{6,2},{2,0},{1,5},{5,9},... | collective-permute-start | bytes 2359304 | tf_op jit(solution)/shard_map/scatter_up_2/ppermute | solution.py:36
  46.6 26.2 %collective-permute-start.13 = (f16[384,1024]{1,0:T(8,128)(2,1)S(1)}, f16[384,1024]{1,0:T(8,128)(2,1)S(1)}, u32[]{:S(2)}, u32[]{:S(2)}) collective-permute-start(f16[384,1024]{1,0:T(8,128)(2,1)S(1)} %fusion.13), channel_id=1, source_target_pairs={{4,0},{8,4},{12,8},{14,12},{10,14},{6,10},{2,6},{0,2},{5,1},{9,5},... | collective-permute-start | bytes 2359304 | tf_op jit(solution)/shard_map/scatter_down_2/ppermute | solution.py:36
  47.2 25.7 %collective-permute-start.14 = (f16[384,128]{1,0:T(8,128)(2,1)S(1)}, f16[384,128]{1,0:T(8,128)(2,1)S(1)}, u32[]{:S(2)}, u32[]{:S(2)}) collective-permute-start(f16[384,128]{1,0:T(8,128)(2,1)S(1)} %multiply_convert_fusion.2), channel_id=1, source_target_pairs={{0,4},{2,6},{4,0},{6,2},{8,12},{10,14},{12,8},{14,10},{1,5},{3,7},... | collective-permute-start | bytes 294920 | tf_op jit(solution)/shard_map/down_sums_2/ppermute | solution.py:36
  53.9 33.7 %collective-permute-start.11 = (bf16[384,1024]{1,0:T(8,128)(2,1)S(1)}, bf16[384,1024]{1,0:T(8,128)(2,1)S(1)}, u32[]{:S(2)}, u32[]{:S(2)}) collective-permute-start(bf16[384,1024]{1,0:T(8,128)(2,1)S(1)} %collective-permute-done.6.refs_1_), channel_id=1, source_target_pairs={{0,4},{4,8},{8,12},{12,14},{14,10},{10,6},{6,2},{2,0},{1,5},{5,9},... | collective-permute-start | bytes 2359304 | tf_op jit(solution)/shard_map/gather_up_3/ppermute | solution.py:36
  59.8 30.0 %collective-permute-start.15 = (bf16[384,1024]{1,0:T(8,128)(2,1)S(1)}, bf16[384,1024]{1,0:T(8,128)(2,1)S(1)}, u32[]{:S(2)}, u32[]{:S(2)}) collective-permute-start(bf16[384,1024]{1,0:T(8,128)(2,1)S(1)} %collective-permute-done.10.refs_0_), channel_id=1, source_target_pairs={{4,0},{8,4},{12,8},{14,12},{10,14},{6,10},{2,6},{0,2},{5,1},{9,5},... | collective-permute-start | bytes 2359304 | tf_op jit(solution)/shard_map/gather_down_3/ppermute | solution.py:36
  73.6 30.8 %collective-permute-start.17 = (f16[384,1024]{1,0:T(8,128)(2,1)S(1)}, f16[384,1024]{1,0:T(8,128)(2,1)S(1)}, u32[]{:S(2)}, u32[]{:S(2)}) collective-permute-start(f16[384,1024]{1,0:T(8,128)(2,1)S(1)} %get-tuple-element.107), channel_id=1, source_target_pairs={{0,4},{4,8},{8,12},{12,14},{14,10},{10,6},{6,2},{2,0},{1,5},{5,9},... | collective-permute-start | bytes 2359304 | tf_op jit(solution)/shard_map/scatter_up_3/ppermute | solution.py:36
  73.7 35.0 %collective-permute-start.18 = (f16[384,1024]{1,0:T(8,128)(2,1)S(1)}, f16[384,1024]{1,0:T(8,128)(2,1)S(1)}, u32[]{:S(2)}, u32[]{:S(2)}) collective-permute-start(f16[384,1024]{1,0:T(8,128)(2,1)S(1)} %get-tuple-element.106), channel_id=1, source_target_pairs={{4,0},{8,4},{12,8},{14,12},{10,14},{6,10},{2,6},{0,2},{5,1},{9,5},... | collective-permute-start | bytes 2359304 | tf_op jit(solution)/shard_map/scatter_down_3/ppermute | solution.py:36
  75.8 32.9 %collective-permute-start.19 = (f16[384,128]{1,0:T(8,128)(2,1)S(1)}, f16[384,128]{1,0:T(8,128)(2,1)S(1)}, u32[]{:S(2)}, u32[]{:S(2)}) collective-permute-start(f16[384,128]{1,0:T(8,128)(2,1)S(1)} %multiply_convert_fusion.1), channel_id=1, source_target_pairs={{0,8},{2,10},{4,12},{6,14},{8,0},{10,2},{12,4},{14,6},{1,9},{3,11}... | collective-permute-start | bytes 294920 | tf_op jit(solution)/shard_map/down_sums_4/ppermute | solution.py:36
  89.8 24.8 %collective-permute-start.16 = (bf16[192,1024]{1,0:T(8,128)(2,1)S(1)}, bf16[192,1024]{1,0:T(8,128)(2,1)S(1)}, u32[]{:S(2)}, u32[]{:S(2)}) collective-permute-start(bf16[192,1024]{1,0:T(8,128)(2,1)S(1)} %slice.89), channel_id=1, source_target_pairs={{0,4},{4,8},{8,12},{12,14},{14,10},{10,6},{6,2},{2,0},{1,5},{5,9},... | collective-permute-start | bytes 1179656 | tf_op jit(solution)/shard_map/gather_up_4/ppermute | solution.py:36
  90.7 26.4 %collective-permute-start.20 = (bf16[192,1024]{1,0:T(8,128)(2,1)S(1)}, bf16[192,1024]{1,0:T(8,128)(2,1)S(1)}, u32[]{:S(2)}, u32[]{:S(2)}) collective-permute-start(bf16[192,1024]{1,0:T(8,128)(2,1)S(1)} %slice.90), channel_id=1, source_target_pairs={{4,0},{8,4},{12,8},{14,12},{10,14},{6,10},{2,6},{0,2},{5,1},{9,5},... | collective-permute-start | bytes 1179656 | tf_op jit(solution)/shard_map/gather_down_4/ppermute | solution.py:36
  109.4 7.8 %collective-permute-start.22 = (bf16[256,1024]{1,0:T(8,128)(2,1)S(1)}, bf16[256,1024]{1,0:T(8,128)(2,1)S(1)}, u32[]{:S(2)}, u32[]{:S(2)}) collective-permute-start(bf16[256,1024]{1,0:T(8,128)(2,1)S(1)} %get-tuple-element.97.own_o), channel_id=1, source_target_pairs={{0,1},{1,0},{2,3},{3,2},{4,5},{5,4},{6,7},{7,6},{8,9},{9,8},{10,11... | collective-permute-start | bytes 1572872 | tf_op jit(solution)/shard_map/ppermute | solution.py:40
  109.5 7.7 %collective-permute-start.21 = (bf16[256,1024]{1,0:T(8,128)(2,1)S(1)}, bf16[256,1024]{1,0:T(8,128)(2,1)S(1)}, u32[]{:S(2)}, u32[]{:S(2)}) collective-permute-start(bf16[256,1024]{1,0:T(8,128)(2,1)S(1)} %get-tuple-element.96.own_q), channel_id=1, source_target_pairs={{0,1},{1,0},{2,3},{3,2},{4,5},{5,4},{6,7},{7,6},{8,9},{9,8},{10,11... | collective-permute-start | bytes 1572872 | tf_op jit(solution)/shard_map/ppermute | solution.py:40
  110.0 20.6 %collective-permute-start.24 = (f16[384,1024]{1,0:T(8,128)(2,1)S(1)}, f16[384,1024]{1,0:T(8,128)(2,1)S(1)}, u32[]{:S(2)}, u32[]{:S(2)}) collective-permute-start(f16[384,1024]{1,0:T(8,128)(2,1)S(1)} %get-tuple-element.105), channel_id=1, source_target_pairs={{0,4},{4,8},{8,12},{12,14},{14,10},{10,6},{6,2},{2,0},{1,5},{5,9},... | collective-permute-start | bytes 2359304 | tf_op jit(solution)/shard_map/scatter_up_4/ppermute | solution.py:36
  114.6 18.6 %collective-permute-start.25 = (f16[384,1024]{1,0:T(8,128)(2,1)S(1)}, f16[384,1024]{1,0:T(8,128)(2,1)S(1)}, u32[]{:S(2)}, u32[]{:S(2)}) collective-permute-start(f16[384,1024]{1,0:T(8,128)(2,1)S(1)} %get-tuple-element.104), channel_id=1, source_target_pairs={{4,0},{8,4},{12,8},{14,12},{10,14},{6,10},{2,6},{0,2},{5,1},{9,5},... | collective-permute-start | bytes 2359304 | tf_op jit(solution)/shard_map/scatter_down_4/ppermute | solution.py:36
  (13 other events, 61.7 us)

commit v9 on v8

--- a/solution.py
+++ b/solution.py
@@ -176,6 +176,50 @@
         compiler_params=params(),
         name="unpack_rows",
     )(hot, x, spare)
+
+
+def unpack_first(hot, x):
+    rows, (packed, width) = hot.shape[0], x.shape
+
+    def kernel(hot_ref, x_ref, out):
+        out[...] = dot(hot_ref[:, :packed], x_ref[...]).astype(BF16)
+
+    return pl.pallas_call(
+        kernel,
+        grid=(1,),
+        in_specs=[pl.BlockSpec((packed, rows), lambda j: (0, 0)), whole(x.shape)],
+        out_specs=pl.BlockSpec((packed, width), lambda j: (0, 0)),
+        out_shape=jax.ShapeDtypeStruct((rows, width), BF16),
+        compiler_params=params(),
+        name="unpack_first",
+    )(hot, x)
+
+
+def unpack_last(hot, x, spare, into):
+    rows, (packed, width) = hot.shape[0], x.shape
+    count = rows - packed
+    last = pl.BlockSpec((count, width), lambda j: (packed // count, 0))
+
+    def kernel(hot_ref, x_ref, spare_ref, into_ref, out):
+        out[...] = (
+            dot(hot_ref[:, :packed], x_ref[...]) + dot(hot_ref[:, packed:], spare_ref[...])
+        ).astype(BF16)
+
+    return pl.pallas_call(
+        kernel,
+        grid=(1,),
+        in_specs=[
+            pl.BlockSpec((count, rows), lambda j: (packed // count, 0)),
+            whole(x.shape),
+            whole(spare.shape),
+            pl.BlockSpec(memory_space=pl.ANY),
+        ],
+        out_specs=last,
+        out_shape=jax.ShapeDtypeStruct((rows, width), BF16),
+        input_output_aliases={3: 0},
+        compiler_params=params(),
+        name="unpack_last",
+    )(hot, x, spare, into)
 
 
 def request_of(counts, place, slot, packed):
@@ -469,7 +513,8 @@
         o_last = (base[first:] + widen(up_sum[first:]) + widen(down_sum[first:])).astype(BF16)
         o_m = other_replica(o_last)
         o = (base + widen(up_sum) + widen(down_sum)).astype(BF16)
-        attended = unpack(hot, o, o_m)
+        attended = unpack_first(hot, o)
+        attended = unpack_last(hot, o, tie(o_m, attended), attended)
         return queries, attended
 
     return local

time: 137 us -> 137 us (level)
    pallas_call x0 -> x2, Pallas kernels: none -> 2.51 us  [the longest x1 1.45 us: unpack_first(): pl.pallas_call(kernel, grid=(1,), in_specs=[pl.BlockSpec((packed, rows),...]
    pallas_call x2 -> x1, Pallas kernels: 3.87 us -> 1.93 us  [unpack(): pl.pallas_call(unpack_kernel, grid=(1,), in_specs=[whole(hot.shape), whol...]
  transfers between devices with their start and end apart: 27 -> 27, of which waited for: 13 -> 12; matrix products, arithmetic and copies ran while one was open for 3% -> 3% of each run, Pallas kernels for 32% -> 34%
where the time goes in v9:
time: 137 us; the launch traced here: 136 us
  waiting for transfers between devices  52.8 us (39%)
  Pallas kernels  46.9 us (34%)
  starting transfers between devices  28.9 us (21%)
  local copies, waits for them, and re-layouts  3.6 us (3%)
  other arithmetic  3.15 us (2%)
    ppermute x19, waiting for transfers between devices, send(): return lax.ppermute(value, 'tensor', pairs)  52.2 us
    ppermute x19, starting transfers between devices, send(): return lax.ppermute(value, 'tensor', pairs)  27 us
    pallas_call x4, Pallas kernels, add_products(): pl.pallas_call(functools.partial(add_kernel, len(pieces)), grid_spec=pltp...  16.9 us
    pallas_call x3, Pallas kernels, shares(): pl.pallas_call(shares_kernel, grid_spec=pltpu.PrefetchScalarGridSpec(num_...  15.6 us
    unnamed x21, local copies, waits for them, and re-layouts  3.16 us
  transfers between devices with their start and end apart: 27, of which 12 were waited for; matrix products, arithmetic and copies ran while one was open for 3% of the time, Pallas kernels for 34%

profile of v9, /device:TPU:0, one launch (start us, length us, event | category | flops | bytes accessed | tf_op | source)
XLA Modules:
  0.0 136.4 jit_solution(11158094243012164434)
XLA Ops:
  5.1 3.1 %collective-permute-start.1 = (bf16[384,1024]{1,0:T(8,128)(2,1)S(1)}, bf16[384,1024]{1,0:T(8,128)(2,1)S(1)}, u32[]{:S(2)}, u32[]{:S(2)}) collective-permute-start(bf16[384,1024]{1,0:T(8,128)(2,1)S(1)} %fill_rows.2.refs_2_.x.refs_0_), channel_id=1, source_target_pairs={{0,4},{4,8},{8,12},{12,14},{14,10},{10,6},{6,2},{2,0},{1,5},{5,9},... | collective-permute-start | bytes 2359304 | tf_op jit(solution)/shard_map/gather_up_1/ppermute | solution.py:36
  12.7 3.1 %shares.4 = f32[1,384,1024]{2,1,0:T(8,128)S(1)} custom-call(s32[8]{0:T(128)S(1)} %stack.39.where, bf16[384,1024]{1,0:T(8,128)(2,1)S(1)} %fill_rows.3.x_ref.v, bf16[1024,8192]{1,0:T(8,128)(2,1)} %w_ref.5), custom_call_target="tpu_custom_call" | custom-call | tf_op jit(solution)/shard_map/shares/pallas_call | solution.py:349
  16.0 4.1 %shares.3 = f32[2,384,1024]{2,1,0:T(8,128)S(1)} custom-call(s32[8]{0:T(128)S(1)} %stack.39.where, bf16[384,1024]{1,0:T(8,128)(2,1)S(1)} %fill_rows.3.x_ref.v, bf16[1024,8192]{1,0:T(8,128)(2,1)} %w_ref.5), custom_call_target="tpu_custom_call" | custom-call | tf_op jit(solution)/shard_map/shares/pallas_call | solution.py:349
  20.3 2.1 %collective-permute-start.7 = (f16[192,1024]{1,0:T(8,128)(2,1)S(1)}, f16[192,1024]{1,0:T(8,128)(2,1)S(1)}, u32[]{:S(2)}, u32[]{:S(2)}) collective-permute-start(f16[192,1024]{1,0:T(8,128)(2,1)S(1)} %get-tuple-element.115), channel_id=1, source_target_pairs={{0,4},{4,8},{8,12},{12,14},{14,10},{10,6},{6,2},{2,0},{1,5},{5,9},... | collective-permute-start | bytes 1179656 | tf_op jit(solution)/shard_map/scatter_up_1/ppermute | solution.py:36
  22.4 2.3 %down_rows.1 = f32[384,128]{1,0:T(8,128)S(1)} custom-call(s32[4]{0:T(128)S(1)} %copy-done.7, s32[1]{0:T(128)} %bitcast.place, bf16[384,1024]{1,0:T(8,128)(2,1)S(1)} %fill_rows.2.refs_2_.x.refs_0_, bf16[384,1024]{1,0:T(8,128)(2,1)S(1)} %fill_rows.3.x_ref.v, bf16[256,1024]{1,0:T(8,128)(2,1)S(1)} %get-tuple-element.55.own_q, ...), custom_call_target="tpu_custom_call" | custom-call | tf_op jit(solution)/shard_map/down_rows/pallas_call | solution.py:289
  30.7 8.3 %shares.5 = f32[5,384,1024]{2,1,0:T(8,128)S(1)} custom-call(s32[8]{0:T(128)S(1)} %stack.39.where, bf16[384,1024]{1,0:T(8,128)(2,1)S(1)} %fill_rows.3.x_ref.v, bf16[1024,8192]{1,0:T(8,128)(2,1)} %w_ref.5), custom_call_target="tpu_custom_call" | custom-call | tf_op jit(solution)/shard_map/shares/pallas_call | solution.py:349
  39.0 5.4 %add_products.4.refs_4_ = f32[384,1024]{1,0:T(8,128)S(1)} custom-call(s32[8]{0:T(128)S(1)} %stack.39.where, bf16[384,1024]{1,0:T(8,128)(2,1)S(1)} %fill_rows.2.refs_2_.x.refs_0_, bf16[384,1024]{1,0:T(8,128)(2,1)S(1)} %collective-permute-done.5.refs_1_, bf16[384,1024]{1,0:T(8,128)(2,1)S(1)} %collective-permute-done.1.refs_2_, bf16[8192,1024]{1,0:T(8,128)(2,1)} %refs_1_.5, ...), custom_call_target="tpu_custom_call" | custom-call | tf_op jit(solution)/shard_map/add_products/pallas_call | solution.py:385
  48.8 5.0 %collective-permute-done.6.refs_1_ = bf16[384,1024]{1,0:T(8,128)(2,1)S(1)} collective-permute-done((bf16[384,1024]{1,0:T(8,128)(2,1)S(1)}, bf16[384,1024]{1,0:T(8,128)(2,1)S(1)}, u32[]{:S(2)}, u32[]{:S(2)}) %collective-permute-start.6) | collective-permute-done | bytes 786464 | tf_op jit(solution)/shard_map/gather_up_2/ppermute | solution.py:36
  55.5 4.3 %add_products.5.refs_4_.refs_2_ = f32[384,1024]{1,0:T(8,128)S(1)} custom-call(s32[8]{0:T(128)S(1)} %stack.39.where, bf16[384,1024]{1,0:T(8,128)(2,1)S(1)} %collective-permute-done.10.refs_0_, bf16[384,1024]{1,0:T(8,128)(2,1)S(1)} %collective-permute-done.6.refs_1_, bf16[8192,1024]{1,0:T(8,128)(2,1)} %refs_1_.5, bf16[8192,1024]{1,0:T(8,128)(2,1)} %refs_1_.5, ...), custom_call_target="tpu_custom_call" | custom-call | tf_op jit(solution)/shard_map/add_products/pallas_call | solution.py:385
  60.3 10.4 %collective-permute-done.12 = f16[384,1024]{1,0:T(8,128)(2,1)S(1)} collective-permute-done((f16[384,1024]{1,0:T(8,128)(2,1)S(1)}, f16[384,1024]{1,0:T(8,128)(2,1)S(1)}, u32[]{:S(2)}, u32[]{:S(2)}) %collective-permute-start.12) | collective-permute-done | bytes 786464 | tf_op jit(solution)/shard_map/scatter_up_2/ppermute | solution.py:36
  70.7 2.1 %collective-permute-done.14 = f16[384,128]{1,0:T(8,128)(2,1)S(1)} collective-permute-done((f16[384,128]{1,0:T(8,128)(2,1)S(1)}, f16[384,128]{1,0:T(8,128)(2,1)S(1)}, u32[]{:S(2)}, u32[]{:S(2)}) %collective-permute-start.14) | collective-permute-done | bytes 98336 | tf_op jit(solution)/shard_map/down_sums_2/ppermute | solution.py:36
  75.8 2.7 %collective-permute-start.19 = (f16[384,128]{1,0:T(8,128)(2,1)S(1)}, f16[384,128]{1,0:T(8,128)(2,1)S(1)}, u32[]{:S(2)}, u32[]{:S(2)}) collective-permute-start(f16[384,128]{1,0:T(8,128)(2,1)S(1)} %multiply_convert_fusion.1), channel_id=1, source_target_pairs={{0,8},{2,10},{4,12},{6,14},{8,0},{10,2},{12,4},{14,6},{1,9},{3,11}... | collective-permute-start | bytes 294920 | tf_op jit(solution)/shard_map/down_sums_4/ppermute | solution.py:36
  78.4 9.1 %collective-permute-done.11.refs_1_ = bf16[384,1024]{1,0:T(8,128)(2,1)S(1)} collective-permute-done((bf16[384,1024]{1,0:T(8,128)(2,1)S(1)}, bf16[384,1024]{1,0:T(8,128)(2,1)S(1)}, u32[]{:S(2)}, u32[]{:S(2)}) %collective-permute-start.11) | collective-permute-done | bytes 786464 | tf_op jit(solution)/shard_map/gather_up_3/ppermute | solution.py:36
  87.6 2.1 %collective-permute-done.15.refs_0_ = bf16[384,1024]{1,0:T(8,128)(2,1)S(1)} collective-permute-done((bf16[384,1024]{1,0:T(8,128)(2,1)S(1)}, bf16[384,1024]{1,0:T(8,128)(2,1)S(1)}, u32[]{:S(2)}, u32[]{:S(2)}) %collective-permute-start.15) | collective-permute-done | bytes 786464 | tf_op jit(solution)/shard_map/gather_down_3/ppermute | solution.py:36
  90.7 2.0 %collective-permute-start.20 = (bf16[192,1024]{1,0:T(8,128)(2,1)S(1)}, bf16[192,1024]{1,0:T(8,128)(2,1)S(1)}, u32[]{:S(2)}, u32[]{:S(2)}) collective-permute-start(bf16[192,1024]{1,0:T(8,128)(2,1)S(1)} %slice.90), channel_id=1, source_target_pairs={{4,0},{8,4},{12,8},{14,12},{10,14},{6,10},{2,6},{0,2},{5,1},{9,5},... | collective-permute-start | bytes 1179656 | tf_op jit(solution)/shard_map/gather_down_4/ppermute | solution.py:36
  92.7 4.3 %add_products.6.refs_2_ = f32[384,1024]{1,0:T(8,128)S(1)} custom-call(s32[8]{0:T(128)S(1)} %stack.39.where, bf16[384,1024]{1,0:T(8,128)(2,1)S(1)} %collective-permute-done.15.refs_0_, bf16[384,1024]{1,0:T(8,128)(2,1)S(1)} %collective-permute-done.11.refs_1_, bf16[8192,1024]{1,0:T(8,128)(2,1)} %refs_1_.5, bf16[8192,1024]{1,0:T(8,128)(2,1)} %refs_1_.5, ...), custom_call_target="tpu_custom_call" | custom-call | tf_op jit(solution)/shard_map/add_products/pallas_call | solution.py:385
  97.0 7.4 %collective-permute-done.17 = f16[384,1024]{1,0:T(8,128)(2,1)S(1)} collective-permute-done((f16[384,1024]{1,0:T(8,128)(2,1)S(1)}, f16[384,1024]{1,0:T(8,128)(2,1)S(1)}, u32[]{:S(2)}, u32[]{:S(2)}) %collective-permute-start.17) | collective-permute-done | bytes 786464 | tf_op jit(solution)/shard_map/scatter_up_3/ppermute | solution.py:36
  104.4 4.3 %collective-permute-done.19 = f16[384,128]{1,0:T(8,128)(2,1)S(1)} collective-permute-done((f16[384,128]{1,0:T(8,128)(2,1)S(1)}, f16[384,128]{1,0:T(8,128)(2,1)S(1)}, u32[]{:S(2)}, u32[]{:S(2)}) %collective-permute-start.19) | collective-permute-done | bytes 98336 | tf_op jit(solution)/shard_map/down_sums_4/ppermute | solution.py:36
  110.0 2.6 %collective-permute-start.24 = (f16[384,1024]{1,0:T(8,128)(2,1)S(1)}, f16[384,1024]{1,0:T(8,128)(2,1)S(1)}, u32[]{:S(2)}, u32[]{:S(2)}) collective-permute-start(f16[384,1024]{1,0:T(8,128)(2,1)S(1)} %get-tuple-element.107), channel_id=1, source_target_pairs={{0,4},{4,8},{8,12},{12,14},{14,10},{10,6},{6,2},{2,0},{1,5},{5,9},... | collective-permute-start | bytes 2359304 | tf_op jit(solution)/shard_map/scatter_up_4/ppermute | solution.py:36
  112.6 2.0 %collective-permute-done.16 = bf16[192,1024]{1,0:T(8,128)(2,1)S(1)} collective-permute-done((bf16[192,1024]{1,0:T(8,128)(2,1)S(1)}, bf16[192,1024]{1,0:T(8,128)(2,1)S(1)}, u32[]{:S(2)}, u32[]{:S(2)}) %collective-permute-start.16) | collective-permute-done | bytes 393248 | tf_op jit(solution)/shard_map/gather_up_4/ppermute | solution.py:36
  114.6 2.4 %collective-permute-start.25 = (f16[384,1024]{1,0:T(8,128)(2,1)S(1)}, f16[384,1024]{1,0:T(8,128)(2,1)S(1)}, u32[]{:S(2)}, u32[]{:S(2)}) collective-permute-start(f16[384,1024]{1,0:T(8,128)(2,1)S(1)} %get-tuple-element.106), channel_id=1, source_target_pairs={{4,0},{8,4},{12,8},{14,12},{10,14},{6,10},{2,6},{0,2},{5,1},{9,5},... | collective-permute-start | bytes 2359304 | tf_op jit(solution)/shard_map/scatter_down_4/ppermute | solution.py:36
  118.7 3.0 %add_products.7.x_ref = bf16[384,1024]{1,0:T(8,128)(2,1)S(1)} custom-call(s32[8]{0:T(128)S(1)} %stack.39.where, bf16[384,1024]{1,0:T(8,128)(2,1)S(1)} %constant_dynamic-update-slice_fusion.refs_0_, bf16[8192,1024]{1,0:T(8,128)(2,1)} %refs_1_.5, f32[384,1024]{1,0:T(8,128)S(1)} %add_products.6.refs_2_, f32[384,1024]{1,0:T(8,128)S(1)} %get-tuple-element.99.refs_3_), custom_call_target="tpu_custom_call" | custom-call | tf_op jit(solution)/shard_map/add_products/pallas_call | solution.py:385
  125.3 5.3 %collective-permute-done.24 = f16[384,1024]{1,0:T(8,128)(2,1)S(1)} collective-permute-done((f16[384,1024]{1,0:T(8,128)(2,1)S(1)}, f16[384,1024]{1,0:T(8,128)(2,1)S(1)}, u32[]{:S(2)}, u32[]{:S(2)}) %collective-permute-start.24) | collective-permute-done | bytes 786464 | tf_op jit(solution)/shard_map/scatter_up_4/ppermute | solution.py:36
  130.6 2.6 %collective-permute-done.25 = f16[384,1024]{1,0:T(8,128)(2,1)S(1)} collective-permute-done((f16[384,1024]{1,0:T(8,128)(2,1)S(1)}, f16[384,1024]{1,0:T(8,128)(2,1)S(1)}, u32[]{:S(2)}, u32[]{:S(2)}) %collective-permute-start.25) | collective-permute-done | bytes 786464 | tf_op jit(solution)/shard_map/scatter_down_4/ppermute | solution.py:36
  (92 shorter events, 35.1 us)
Async XLA Ops:
  1.2 10.8 %collective-permute-start.2 = (bf16[512,1024]{1,0:T(8,128)(2,1)}, bf16[512,1024]{1,0:T(8,128)(2,1)S(1)}, u32[]{:S(2)}, u32[]{:S(2)}) collective-permute-start(bf16[512,1024]{1,0:T(8,128)(2,1)} %x_ref.3), channel_id=1, source_target_pairs={{0,1},{1,0},{2,3},{3,2},{4,5},{5,4},{6,7},{7,6},{8,9},{9,8},{10,11... | collective-permute-start | bytes 3145736 | tf_op jit(solution)/shard_map/ppermute | solution.py:40
  5.1 21.8 %collective-permute-start.1 = (bf16[384,1024]{1,0:T(8,128)(2,1)S(1)}, bf16[384,1024]{1,0:T(8,128)(2,1)S(1)}, u32[]{:S(2)}, u32[]{:S(2)}) collective-permute-start(bf16[384,1024]{1,0:T(8,128)(2,1)S(1)} %fill_rows.2.refs_2_.x.refs_0_), channel_id=1, source_target_pairs={{0,4},{4,8},{8,12},{12,14},{14,10},{10,6},{6,2},{2,0},{1,5},{5,9},... | collective-permute-start | bytes 2359304 | tf_op jit(solution)/shard_map/gather_up_1/ppermute | solution.py:36
  8.2 20.4 %collective-permute-start.5 = (bf16[384,1024]{1,0:T(8,128)(2,1)S(1)}, bf16[384,1024]{1,0:T(8,128)(2,1)S(1)}, u32[]{:S(2)}, u32[]{:S(2)}) collective-permute-start(bf16[384,1024]{1,0:T(8,128)(2,1)S(1)} %fill_rows.2.refs_2_.x.refs_0_), channel_id=1, source_target_pairs={{4,0},{8,4},{12,8},{14,12},{10,14},{6,10},{2,6},{0,2},{5,1},{9,5},... | collective-permute-start | bytes 2359304 | tf_op jit(solution)/shard_map/gather_down_1/ppermute | solution.py:36
  11.4 11.0 %collective-permute-start.3 = (bf16[256,1024]{1,0:T(8,128)(2,1)S(1)}, bf16[256,1024]{1,0:T(8,128)(2,1)S(1)}, u32[]{:S(2)}, u32[]{:S(2)}) collective-permute-start(bf16[256,1024]{1,0:T(8,128)(2,1)S(1)} %get-tuple-element.55.own_q), channel_id=1, source_target_pairs={{0,1},{1,0},{2,3},{3,2},{4,5},{5,4},{6,7},{7,6},{8,9},{9,8},{10,11... | collective-permute-start | bytes 1572872 | tf_op jit(solution)/shard_map/ppermute | solution.py:40
  11.5 10.9 %collective-permute-start.4 = (bf16[256,1024]{1,0:T(8,128)(2,1)S(1)}, bf16[256,1024]{1,0:T(8,128)(2,1)S(1)}, u32[]{:S(2)}, u32[]{:S(2)}) collective-permute-start(bf16[256,1024]{1,0:T(8,128)(2,1)S(1)} %get-tuple-element.56.own_o), channel_id=1, source_target_pairs={{0,1},{1,0},{2,3},{3,2},{4,5},{5,4},{6,7},{7,6},{8,9},{9,8},{10,11... | collective-permute-start | bytes 1572872 | tf_op jit(solution)/shard_map/ppermute | solution.py:40
  20.3 24.1 %collective-permute-start.7 = (f16[192,1024]{1,0:T(8,128)(2,1)S(1)}, f16[192,1024]{1,0:T(8,128)(2,1)S(1)}, u32[]{:S(2)}, u32[]{:S(2)}) collective-permute-start(f16[192,1024]{1,0:T(8,128)(2,1)S(1)} %get-tuple-element.115), channel_id=1, source_target_pairs={{0,4},{4,8},{8,12},{12,14},{14,10},{10,6},{6,2},{2,0},{1,5},{5,9},... | collective-permute-start | bytes 1179656 | tf_op jit(solution)/shard_map/scatter_up_1/ppermute | solution.py:36
  22.4 22.0 %collective-permute-start.8 = (f16[192,1024]{1,0:T(8,128)(2,1)S(1)}, f16[192,1024]{1,0:T(8,128)(2,1)S(1)}, u32[]{:S(2)}, u32[]{:S(2)}) collective-permute-start(f16[192,1024]{1,0:T(8,128)(2,1)S(1)} %get-tuple-element.114), channel_id=1, source_target_pairs={{4,0},{8,4},{12,8},{14,12},{10,14},{6,10},{2,6},{0,2},{5,1},{9,5},... | collective-permute-start | bytes 1179656 | tf_op jit(solution)/shard_map/scatter_down_1/ppermute | solution.py:36
  24.8 19.6 %collective-permute-start.9 = (f16[384,128]{1,0:T(8,128)(2,1)S(1)}, f16[384,128]{1,0:T(8,128)(2,1)S(1)}, u32[]{:S(2)}, u32[]{:S(2)}) collective-permute-start(f16[384,128]{1,0:T(8,128)(2,1)S(1)} %multiply_convert_fusion.3), channel_id=1, source_target_pairs={{0,2},{2,0},{4,6},{6,4},{8,10},{10,8},{12,14},{14,12},{1,3},{3,1},... | collective-permute-start | bytes 294920 | tf_op jit(solution)/shard_map/down_sums_1/ppermute | solution.py:36
  28.6 25.2 %collective-permute-start.6 = (bf16[384,1024]{1,0:T(8,128)(2,1)S(1)}, bf16[384,1024]{1,0:T(8,128)(2,1)S(1)}, u32[]{:S(2)}, u32[]{:S(2)}) collective-permute-start(bf16[384,1024]{1,0:T(8,128)(2,1)S(1)} %collective-permute-done.1.refs_2_), channel_id=1, source_target_pairs={{0,4},{4,8},{8,12},{12,14},{14,10},{10,6},{6,2},{2,0},{1,5},{5,9},... | collective-permute-start | bytes 2359304 | tf_op jit(solution)/shard_map/gather_up_2/ppermute | solution.py:36
  30.2 23.7 %collective-permute-start.10 = (bf16[384,1024]{1,0:T(8,128)(2,1)S(1)}, bf16[384,1024]{1,0:T(8,128)(2,1)S(1)}, u32[]{:S(2)}, u32[]{:S(2)}) collective-permute-start(bf16[384,1024]{1,0:T(8,128)(2,1)S(1)} %collective-permute-done.5.refs_1_), channel_id=1, source_target_pairs={{4,0},{8,4},{12,8},{14,12},{10,14},{6,10},{2,6},{0,2},{5,1},{9,5},... | collective-permute-start | bytes 2359304 | tf_op jit(solution)/shard_map/gather_down_2/ppermute | solution.py:36
  44.9 25.9 %collective-permute-start.12 = (f16[384,1024]{1,0:T(8,128)(2,1)S(1)}, f16[384,1024]{1,0:T(8,128)(2,1)S(1)}, u32[]{:S(2)}, u32[]{:S(2)}) collective-permute-start(f16[384,1024]{1,0:T(8,128)(2,1)S(1)} %fusion.12), channel_id=1, source_target_pairs={{0,4},{4,8},{8,12},{12,14},{14,10},{10,6},{6,2},{2,0},{1,5},{5,9},... | collective-permute-start | bytes 2359304 | tf_op jit(solution)/shard_map/scatter_up_2/ppermute | solution.py:36
  46.6 26.2 %collective-permute-start.13 = (f16[384,1024]{1,0:T(8,128)(2,1)S(1)}, f16[384,1024]{1,0:T(8,128)(2,1)S(1)}, u32[]{:S(2)}, u32[]{:S(2)}) collective-permute-start(f16[384,1024]{1,0:T(8,128)(2,1)S(1)} %fusion.13), channel_id=1, source_target_pairs={{4,0},{8,4},{12,8},{14,12},{10,14},{6,10},{2,6},{0,2},{5,1},{9,5},... | collective-permute-start | bytes 2359304 | tf_op jit(solution)/shard_map/scatter_down_2/ppermute | solution.py:36
  47.2 25.7 %collective-permute-start.14 = (f16[384,128]{1,0:T(8,128)(2,1)S(1)}, f16[384,128]{1,0:T(8,128)(2,1)S(1)}, u32[]{:S(2)}, u32[]{:S(2)}) collective-permute-start(f16[384,128]{1,0:T(8,128)(2,1)S(1)} %multiply_convert_fusion.2), channel_id=1, source_target_pairs={{0,4},{2,6},{4,0},{6,2},{8,12},{10,14},{12,8},{14,10},{1,5},{3,7},... | collective-permute-start | bytes 294920 | tf_op jit(solution)/shard_map/down_sums_2/ppermute | solution.py:36
  53.9 33.7 %collective-permute-start.11 = (bf16[384,1024]{1,0:T(8,128)(2,1)S(1)}, bf16[384,1024]{1,0:T(8,128)(2,1)S(1)}, u32[]{:S(2)}, u32[]{:S(2)}) collective-permute-start(bf16[384,1024]{1,0:T(8,128)(2,1)S(1)} %collective-permute-done.6.refs_1_), channel_id=1, source_target_pairs={{0,4},{4,8},{8,12},{12,14},{14,10},{10,6},{6,2},{2,0},{1,5},{5,9},... | collective-permute-start | bytes 2359304 | tf_op jit(solution)/shard_map/gather_up_3/ppermute | solution.py:36
  59.8 30.0 %collective-permute-start.15 = (bf16[384,1024]{1,0:T(8,128)(2,1)S(1)}, bf16[384,1024]{1,0:T(8,128)(2,1)S(1)}, u32[]{:S(2)}, u32[]{:S(2)}) collective-permute-start(bf16[384,1024]{1,0:T(8,128)(2,1)S(1)} %collective-permute-done.10.refs_0_), channel_id=1, source_target_pairs={{4,0},{8,4},{12,8},{14,12},{10,14},{6,10},{2,6},{0,2},{5,1},{9,5},... | collective-permute-start | bytes 2359304 | tf_op jit(solution)/shard_map/gather_down_3/ppermute | solution.py:36
  73.6 30.8 %collective-permute-start.17 = (f16[384,1024]{1,0:T(8,128)(2,1)S(1)}, f16[384,1024]{1,0:T(8,128)(2,1)S(1)}, u32[]{:S(2)}, u32[]{:S(2)}) collective-permute-start(f16[384,1024]{1,0:T(8,128)(2,1)S(1)} %get-tuple-element.109), channel_id=1, source_target_pairs={{0,4},{4,8},{8,12},{12,14},{14,10},{10,6},{6,2},{2,0},{1,5},{5,9},... | collective-permute-start | bytes 2359304 | tf_op jit(solution)/shard_map/scatter_up_3/ppermute | solution.py:36
  73.7 35.0 %collective-permute-start.18 = (f16[384,1024]{1,0:T(8,128)(2,1)S(1)}, f16[384,1024]{1,0:T(8,128)(2,1)S(1)}, u32[]{:S(2)}, u32[]{:S(2)}) collective-permute-start(f16[384,1024]{1,0:T(8,128)(2,1)S(1)} %get-tuple-element.108), channel_id=1, source_target_pairs={{4,0},{8,4},{12,8},{14,12},{10,14},{6,10},{2,6},{0,2},{5,1},{9,5},... | collective-permute-start | bytes 2359304 | tf_op jit(solution)/shard_map/scatter_down_3/ppermute | solution.py:36
  75.8 32.9 %collective-permute-start.19 = (f16[384,128]{1,0:T(8,128)(2,1)S(1)}, f16[384,128]{1,0:T(8,128)(2,1)S(1)}, u32[]{:S(2)}, u32[]{:S(2)}) collective-permute-start(f16[384,128]{1,0:T(8,128)(2,1)S(1)} %multiply_convert_fusion.1), channel_id=1, source_target_pairs={{0,8},{2,10},{4,12},{6,14},{8,0},{10,2},{12,4},{14,6},{1,9},{3,11}... | collective-permute-start | bytes 294920 | tf_op jit(solution)/shard_map/down_sums_4/ppermute | solution.py:36
  89.8 24.8 %collective-permute-start.16 = (bf16[192,1024]{1,0:T(8,128)(2,1)S(1)}, bf16[192,1024]{1,0:T(8,128)(2,1)S(1)}, u32[]{:S(2)}, u32[]{:S(2)}) collective-permute-start(bf16[192,1024]{1,0:T(8,128)(2,1)S(1)} %slice.89), channel_id=1, source_target_pairs={{0,4},{4,8},{8,12},{12,14},{14,10},{10,6},{6,2},{2,0},{1,5},{5,9},... | collective-permute-start | bytes 1179656 | tf_op jit(solution)/shard_map/gather_up_4/ppermute | solution.py:36
  90.7 26.4 %collective-permute-start.20 = (bf16[192,1024]{1,0:T(8,128)(2,1)S(1)}, bf16[192,1024]{1,0:T(8,128)(2,1)S(1)}, u32[]{:S(2)}, u32[]{:S(2)}) collective-permute-start(bf16[192,1024]{1,0:T(8,128)(2,1)S(1)} %slice.90), channel_id=1, source_target_pairs={{4,0},{8,4},{12,8},{14,12},{10,14},{6,10},{2,6},{0,2},{5,1},{9,5},... | collective-permute-start | bytes 1179656 | tf_op jit(solution)/shard_map/gather_down_4/ppermute | solution.py:36
  109.4 7.8 %collective-permute-start.22 = (bf16[256,1024]{1,0:T(8,128)(2,1)S(1)}, bf16[256,1024]{1,0:T(8,128)(2,1)S(1)}, u32[]{:S(2)}, u32[]{:S(2)}) collective-permute-start(bf16[256,1024]{1,0:T(8,128)(2,1)S(1)} %get-tuple-element.98.own_o), channel_id=1, source_target_pairs={{0,1},{1,0},{2,3},{3,2},{4,5},{5,4},{6,7},{7,6},{8,9},{9,8},{10,11... | collective-permute-start | bytes 1572872 | tf_op jit(solution)/shard_map/ppermute | solution.py:40
  109.5 7.7 %collective-permute-start.21 = (bf16[256,1024]{1,0:T(8,128)(2,1)S(1)}, bf16[256,1024]{1,0:T(8,128)(2,1)S(1)}, u32[]{:S(2)}, u32[]{:S(2)}) collective-permute-start(bf16[256,1024]{1,0:T(8,128)(2,1)S(1)} %get-tuple-element.97.own_q), channel_id=1, source_target_pairs={{0,1},{1,0},{2,3},{3,2},{4,5},{5,4},{6,7},{7,6},{8,9},{9,8},{10,11... | collective-permute-start | bytes 1572872 | tf_op jit(solution)/shard_map/ppermute | solution.py:40
  110.0 20.6 %collective-permute-start.24 = (f16[384,1024]{1,0:T(8,128)(2,1)S(1)}, f16[384,1024]{1,0:T(8,128)(2,1)S(1)}, u32[]{:S(2)}, u32[]{:S(2)}) collective-permute-start(f16[384,1024]{1,0:T(8,128)(2,1)S(1)} %get-tuple-element.107), channel_id=1, source_target_pairs={{0,4},{4,8},{8,12},{12,14},{14,10},{10,6},{6,2},{2,0},{1,5},{5,9},... | collective-permute-start | bytes 2359304 | tf_op jit(solution)/shard_map/scatter_up_4/ppermute | solution.py:36
  114.6 18.6 %collective-permute-start.25 = (f16[384,1024]{1,0:T(8,128)(2,1)S(1)}, f16[384,1024]{1,0:T(8,128)(2,1)S(1)}, u32[]{:S(2)}, u32[]{:S(2)}) collective-permute-start(f16[384,1024]{1,0:T(8,128)(2,1)S(1)} %get-tuple-element.106), channel_id=1, source_target_pairs={{4,0},{8,4},{12,8},{14,12},{10,14},{6,10},{2,6},{0,2},{5,1},{9,5},... | collective-permute-start | bytes 2359304 | tf_op jit(solution)/shard_map/scatter_down_4/ppermute | solution.py:36
  (13 other events, 62.1 us)
